TPU v7x, 128 devices: a whole 4x4x4 slice. The times are simulated.
128 devices in a mesh: sample: 8 (over y, x_hi), tok: 16 (over z, x_lo, core).
Axes of the slice: x: 4 (x_hi: 2, x_lo: 2; x = x_hi * 2 + x_lo), y: 4, z: 4, core: 2. Of those that a mesh axis runs over, the one named last changes fastest.
Arguments:
- single: bfloat16 [32, 1024, 768], P('sample', 'tok'), may hold values from -6 to 6
- pair: bfloat16 [1024, 1024, 128], P('tok', 'sample'), may hold values from -400 to 400
- w_query: bfloat16 [768, 768], replicated, may hold values from -0.21875 to 0.21875
- w_key: bfloat16 [768, 768], replicated, may hold values from -0.21875 to 0.21875
- w_value: bfloat16 [768, 768], replicated, may hold values from -0.21875 to 0.21875
- w_out: bfloat16 [768, 768], replicated, may hold values from -0.21875 to 0.21875
- w_pair: bfloat16 [128, 16], replicated, may hold values from -0.5 to 0.5
- cotangent: bfloat16 [32, 1024, 768], P('sample', 'tok'), may hold values from -64 to 64
Outputs:
- grad_single: bfloat16 [32, 1024, 768], P('sample', 'tok')
- grad_pair: bfloat16 [1024, 1024, 128], P('tok', 'sample')
All inputs are finite; a program needn't handle non-finite values.
Results may differ from a plain program's by a relative error of at most 0.02.
Values may be sent and summed in bfloat16 or wider, within the bound.
No kernel may reach another device: no remote copies, remote signals or barrier semaphores. Data moves between devices by JAX's collectives and lax.ppermute only.
A program may use at most 128 MiB of HBM per device.

v0:
```python
import math

import jax
import jax.numpy as jnp
from jax import lax
from jax.sharding import PartitionSpec as P


def times_weight(matrix, weight):
    return jnp.dot(matrix, weight, preferred_element_type=jnp.float32)


def times_transpose(matrix, weight):
    return lax.dot_general(
        matrix, weight, (((1,), (1,)), ((), ())), preferred_element_type=jnp.float32
    )


def attend(
    query_rows,
    keys_whole,
    values_whole,
    grad_rows,
    pair_bias,
    head_count,
    score_scale,
    w_key,
    w_value,
):
    row_count, width = query_rows.shape
    key_count = keys_whole.shape[0]
    head_size = width // head_count
    query_heads = query_rows.reshape(row_count, head_count, head_size)
    key_heads = keys_whole.reshape(key_count, head_count, head_size)
    value_heads = values_whole.reshape(key_count, head_count, head_size)
    out_heads = grad_rows.reshape(row_count, head_count, head_size)
    scores = (
        jnp.einsum("ihd,jhd->hij", query_heads, key_heads, preferred_element_type=jnp.float32)
        * score_scale
        + pair_bias
    )
    shifted = scores - jnp.max(scores, axis=-1, keepdims=True)
    weights = jnp.exp(shifted)
    probs = weights / jnp.sum(weights, axis=-1, keepdims=True)
    probs_low = probs.astype(jnp.bfloat16)
    grad_probs = jnp.einsum(
        "ihd,jhd->hij", out_heads, value_heads, preferred_element_type=jnp.float32
    )
    row_dot = jnp.sum(probs * grad_probs, axis=-1, keepdims=True)
    grad_scores = probs * (grad_probs - row_dot)
    grad_low = grad_scores.astype(jnp.bfloat16)
    grad_query = (
        jnp.einsum("hij,jhd->ihd", grad_low, key_heads, preferred_element_type=jnp.float32)
        * score_scale
    )
    grad_query = grad_query.astype(jnp.bfloat16).reshape(row_count, width)
    key_block = (
        jnp.einsum("hij,ihd->jhd", grad_low, query_heads, preferred_element_type=jnp.float32)
        * score_scale
    )
    value_block = jnp.einsum(
        "hij,ihd->jhd", probs_low, out_heads, preferred_element_type=jnp.float32
    )
    key_block = key_block.astype(jnp.bfloat16).reshape(key_count, width)
    value_block = value_block.astype(jnp.bfloat16).reshape(key_count, width)
    mapped = times_transpose(key_block, w_key) + times_transpose(value_block, w_value)
    return (grad_scores, grad_query, mapped)


def local(single, pair, w_query, w_key, w_value, w_out, w_pair, cotangent):
    sample_count, row_count, width = single.shape
    local_keys = pair.shape[1]
    channels = pair.shape[2]
    head_count = w_pair.shape[1]
    score_scale = 1.0 / math.sqrt(width // head_count)
    flat_rows = single.reshape(sample_count * row_count, width)
    queries = (
        times_weight(flat_rows, w_query)
        .astype(jnp.bfloat16)
        .reshape(sample_count, row_count, width)
    )
    shard_rows = lax.all_gather(single, "tok", axis=1, tiled=True)
    piece_flat = shard_rows.reshape(-1, width)
    keys_piece = times_weight(piece_flat, w_key).astype(jnp.bfloat16).reshape(shard_rows.shape)
    values_piece = times_weight(piece_flat, w_value).astype(jnp.bfloat16).reshape(shard_rows.shape)
    stacked = jnp.stack([keys_piece, values_piece])
    keys_whole = stacked[0]
    values_whole = stacked[1]
    bias_piece = times_weight(pair.reshape(row_count * local_keys, channels), w_pair)
    bias_piece = bias_piece.reshape(row_count, local_keys, head_count).transpose(2, 0, 1)
    pair_bias = lax.all_gather(bias_piece, "sample", axis=2, tiled=True)
    key_count = pair_bias.shape[2]
    out_grads = times_transpose(cotangent.reshape(sample_count * row_count, width), w_out)
    out_grads = out_grads.astype(jnp.bfloat16).reshape(sample_count, row_count, width)
    bias_grad = jnp.zeros((head_count, row_count, key_count), jnp.float32)
    query_grads = []
    mapped_parts = []
    for sample in range(sample_count):
        grad_scores, grad_query, mapped = attend(
            queries[sample],
            keys_whole[sample],
            values_whole[sample],
            out_grads[sample],
            pair_bias,
            head_count,
            score_scale,
            w_key,
            w_value,
        )
        bias_grad = bias_grad + grad_scores
        query_grads.append(grad_query)
        mapped_parts.append(mapped)
    key_value_grad = lax.psum_scatter(
        jnp.stack(mapped_parts).astype(jnp.bfloat16), "tok", scatter_dimension=1, tiled=True
    ).astype(jnp.float32)
    grad_queries = jnp.stack(query_grads).reshape(sample_count * row_count, width)
    grad_sum = times_transpose(grad_queries, w_query) + key_value_grad.reshape(
        sample_count * row_count, width
    )
    grad_single = grad_sum.astype(jnp.bfloat16).reshape(sample_count, row_count, width)
    bias_share = lax.psum_scatter(
        bias_grad.astype(jnp.bfloat16), "sample", scatter_dimension=2, tiled=True
    )
    grad_pair = times_transpose(
        bias_share.transpose(1, 2, 0).reshape(row_count * local_keys, head_count), w_pair
    )
    grad_pair = grad_pair.astype(jnp.bfloat16).reshape(row_count, local_keys, channels)
    return (grad_single, grad_pair)


def solution(mesh):
    in_specs = (
        P("sample", "tok", None),
        P("tok", "sample", None),
        P(),
        P(),
        P(),
        P(),
        P(),
        P("sample", "tok", None),
    )
    out_specs = (P("sample", "tok", None), P("tok", "sample", None))
    return jax.shard_map(local, mesh=mesh, in_specs=in_specs, out_specs=out_specs, check_vma=False)
```

profile of v0, /device:TPU:0, one launch (start us, length us, event | category | flops | bytes accessed | tf_op | source)
XLA Modules:
  0.0 384.2 jit_solution(14951340285547512021)
XLA Ops:
  11.2 1.9 convolution_convert_fusion.3
  18.3 36.3 %all-gather.3.cloned.1.call-done = bf16[4,1024,768]{2,1,0:T(8,128)(2,1)} async-done(((bf16[4,64,768]{2,1,0:T(8,128)(2,1)}), bf16[4,1024,768]{2,1,0:T(8,128)(2,1)}) %all-gather.3.cloned.1.call-update) | async-done | bytes 6291472 | tf_op jit(solution)/shard_map/all_gather | solution.py:82
  54.6 7.6 %convolution_convert_fusion.2 = bf16[4096,768]{0,1:T(8,128)(2,1)S(1)} fusion(bf16[4096,768]{1,0:T(8,128)(2,1)} %bitcast.197, bf16[768,768]{1,0:T(8,128)(2,1)} %param.11), kind=kOutput, calls=%fused_computation.6 | convolution fusion | flops 4834983936 | bytes 13762560 | tf_op jit(solution)/shard_map/dot_general | solution.py:10
  62.2 2.6 fusion.42
  64.8 1.9 copy-done.37
  67.0 5.5 %convolution_convert_fusion.1 = bf16[4096,768]{0,1:T(8,128)(2,1)S(1)} fusion(bf16[4096,768]{1,0:T(8,128)(2,1)S(1)} %bitcast.198, bf16[768,768]{1,0:T(8,128)(2,1)S(1)} %copy-done.39), kind=kOutput, calls=%fused_computation.5 | convolution fusion | flops 4834983936 | bytes 13762560 | tf_op jit(solution)/shard_map/dot_general | solution.py:10
  72.5 3.0 fusion.41
  75.5 55.7 %all-gather.5.cloned.1.call-done = f32[16,64,1024]{2,1,0:T(8,128)} async-done(((f32[16,64,128]{2,1,0:T(8,128)}), f32[16,64,1024]{2,1,0:T(8,128)}) %all-gather.5.cloned.1.call-update) | async-done | bytes 4194320 | tf_op jit(solution)/shard_map/all_gather | solution.py:91
  131.2 3.5 multiply_add_fusion.2
  134.7 2.7 fusion.46
  141.1 3.2 fusion.47
  145.2 2.7 fusion.45
  149.2 3.1 fusion.48
  152.4 6.8 %fusion.15 = bf16[16,48,1024]{2,1,0:T(8,128)(2,1)} fusion(bf16[64,16,48]{0,2,1:T(8,128)(2,1)S(1)} %bitcast.195, f32[16,64]{1,0:T(8,128)S(1)} %get-tuple-element.27, f32[16,64,1024]{2,1,0:T(8,128)} %copy-done.9), kind=kOutput, calls=%fused_computation.46 | convolution fusion | flops 104597504 | bytes 5869568 | tf_op jit(solution)/shard_map/hij,ihd->jhd/dot_general | solution.py:61
  159.2 5.0 %multiply_reduce_fusion.2 = (f32[16,64]{1,0:T(8,128)S(1)}, f32[16,64,1024]{2,1,0:T(8,128)}) fusion(f32[16,64,1024]{2,1,0:T(8,128)} %get-tuple-element.28, f32[16,64]{1,0:T(8,128)S(1)} %get-tuple-element.27, bf16[64,16,48]{0,2,1:T(8,128)(2,1)S(1)} %bitcast.196, bf16[1024,16,48]{0,2,1:T(8,128)(2,1)S(1)} %bitcast.174), kind=kOutput, calls=%fused_computation.18 | convolution fusion | flops 103808000 | bytes 10067968 | tf_op jit(solution)/shard_map/ihd,jhd->hij/dot_general | solution.py:46
  164.2 6.8 %fusion.18 = bf16[16,48,1024]{2,1,0:T(8,128)(2,1)} fusion(bf16[64,16,48]{0,2,1:T(8,128)(2,1)S(1)} %bitcast.193, f32[16,64]{1,0:T(8,128)S(1)} %get-tuple-element.31, f32[16,64,1024]{2,1,0:T(8,128)} %copy-done.8), kind=kOutput, calls=%fused_computation.47 | convolution fusion | flops 104597504 | bytes 5869568 | tf_op jit(solution)/shard_map/hij,ihd->jhd/dot_general | solution.py:61
  171.0 5.0 %multiply_reduce_fusion.1 = (f32[16,64]{1,0:T(8,128)S(1)}, f32[16,64,1024]{2,1,0:T(8,128)}) fusion(f32[16,64,1024]{2,1,0:T(8,128)} %get-tuple-element.32, f32[16,64]{1,0:T(8,128)S(1)} %get-tuple-element.31, bf16[64,16,48]{0,2,1:T(8,128)(2,1)S(1)} %bitcast.194, bf16[1024,16,48]{0,2,1:T(8,128)(2,1)S(1)} %bitcast.173), kind=kOutput, calls=%fused_computation.14 | convolution fusion | flops 103808000 | bytes 10067968 | tf_op jit(solution)/shard_map/ihd,jhd->hij/dot_general | solution.py:46
  176.0 6.9 %fusion.12 = bf16[16,48,1024]{2,1,0:T(8,128)(2,1)} fusion(bf16[64,16,48]{0,2,1:T(8,128)(2,1)S(1)} %bitcast.191, f32[16,64]{1,0:T(8,128)S(1)} %get-tuple-element.23, f32[16,64,1024]{2,1,0:T(8,128)} %copy-done.7), kind=kOutput, calls=%fused_computation.45 | convolution fusion | flops 104597504 | bytes 5869568 | tf_op jit(solution)/shard_map/hij,ihd->jhd/dot_general | solution.py:61
  182.9 5.8 %multiply_reduce_fusion.3 = (f32[16,64]{1,0:T(8,128)S(1)}, f32[16,64,1024]{2,1,0:T(8,128)}) fusion(f32[16,64,1024]{2,1,0:T(8,128)} %get-tuple-element.24, f32[16,64]{1,0:T(8,128)S(1)} %get-tuple-element.23, bf16[64,16,48]{0,2,1:T(8,128)(2,1)S(1)} %bitcast.192, bf16[1024,16,48]{0,2,1:T(8,128)(2,1)} %bitcast.172), kind=kOutput, calls=%fused_computation.22 | convolution fusion | flops 103808000 | bytes 10067968 | tf_op jit(solution)/shard_map/ihd,jhd->hij/dot_general | solution.py:46
  188.8 3.0 multiply_reduce_fusion
  195.4 7.8 %add_convert_fusion = (bf16[16,64,1024]{2,1,0:T(8,128)(2,1)}, bf16[16,64,1024]{2,1,0:T(8,128)(2,1)S(1)}, bf16[16,64,1024]{2,1,0:T(8,128)(2,1)S(1)}, bf16[16,64,1...) fusion(f32[16,64,1024]{2,1,0:T(8,128)} %get-tuple-element.26, f32[16,64]{1,0:T(8,128)S(1)} %get-tuple-element.25, ...), kind=kLoop, calls=%fused_computation.8 | loop fusion | flops 20971520 | bytes 44072960 | tf_op jit(solution)/shard_map/convert_element_type | solution.py:122
  203.2 1.7 multiply_convert_fusion
  205.0 1.9 multiply_convert_fusion.1
  206.8 1.7 multiply_convert_fusion.2
  208.6 1.7 multiply_convert_fusion.3
  210.3 6.2 %copy.69 = bf16[16,64,1024]{1,0,2:T(8,128)(2,1)} copy(bf16[16,64,1024]{2,1,0:T(8,128)(2,1)} %get-tuple-element.2) | data formatting | bytes 4194304
  216.5 6.5 %reshape.125 = bf16[1024,1024]{1,0:T(8,128)(2,1)} reshape(bf16[1024,16,64]{2,1,0:T(8,128)(2,1)} %bitcast.152) | data formatting | bytes 4194304
  223.6 6.7 %fusion.21 = bf16[16,48,1024]{2,1,0:T(8,128)(2,1)} fusion(bf16[64,16,48]{0,2,1:T(8,128)(2,1)S(1)} %bitcast.190, f32[16,64]{1,0:T(8,128)S(1)} %get-tuple-element.35, f32[16,64,1024]{2,1,0:T(8,128)} %copy-done.6), kind=kOutput, calls=%fused_computation.48 | convolution fusion | flops 104597504 | bytes 5869568 | tf_op jit(solution)/shard_map/hij,ihd->jhd/dot_general | solution.py:61
  230.3 3.4 fusion.49
  233.7 1.5 fusion.50
  235.2 1.5 fusion.51
  236.7 1.5 fusion.52
  238.5 1.5 fusion.28
  240.0 1.5 fusion.29
  241.5 1.5 fusion.30
  243.0 1.7 fusion.31
  244.7 3.4 pad_maximum_fusion
  248.1 2.8 fusion.36
  251.6 2.8 fusion.35
  255.2 2.8 fusion.34
  258.8 2.1 fusion.33
  261.7 2.0 pad_maximum_fusion.1
  263.7 32.5 %reduce-scatter.7.cloned.1.call-done = bf16[128,1024]{1,0:T(8,128)(2,1)} async-done(((bf16[1024,1024]{1,0:T(8,128)(2,1)}), bf16[128,1024]{1,0:T(8,128)(2,1)}) %reduce-scatter.7.cloned.1.call-update) | async-done | bytes 262160
  296.2 2.1 reshape.126
  298.3 1.5 copy.70
  299.8 2.1 convolution_convert_fusion
  301.9 73.2 %reduce-scatter.5.cloned.1.call-done = bf16[4,64,768]{2,1,0:T(8,128)(2,1)} async-done(((bf16[4,1024,768]{2,1,0:T(8,128)(2,1)}), bf16[4,64,768]{2,1,0:T(8,128)(2,1)}) %reduce-scatter.5.cloned.1.call-update) | async-done | bytes 393232 | tf_op jit(solution)/shard_map/reduce_scatter | solution.py:113
  375.1 2.4 fusion.32
  (117 shorter events, 22.9 us)
Async XLA Ops:
  7.2 1.6 copy-start
  7.2 47.4 %all-gather.3.cloned.1.call-start = ((), (), s32[]{:S(2)}) async-start(), calls=%async_computation.2 | async-start | bytes 6684672 | tf_op jit(solution)/shard_map/all_gather | solution.py:82
  7.9 123.3 %all-gather.5.cloned.1.call-start = ((), (), s32[]{:S(2)}) async-start(), calls=%async_computation.3 | async-start | bytes 4718592 | tf_op jit(solution)/shard_map/all_gather | solution.py:91
  10.1 6.3 %copy-start.17 = (bf16[768,768]{1,0:T(8,128)(2,1)S(1)}, bf16[768,768]{1,0:T(8,128)(2,1)}, u32[]{:S(2)}) copy-start(bf16[768,768]{1,0:T(8,128)(2,1)} %param.10) | copy-start | bytes 3538948
  10.1 6.3 %copy-start.30 = (bf16[4,64,768]{2,1,0:T(8,128)(2,1)S(1)}, bf16[4,64,768]{2,1,0:T(8,128)(2,1)}, u32[]{:S(2)}) copy-start(bf16[4,64,768]{2,1,0:T(8,128)(2,1)} %param.8) | copy-start | bytes 1179652
  11.2 285.0 %reduce-scatter.7.cloned.1.call-start = ((), (), s32[]{:S(2)}) async-start(), calls=%async_computation.5 | async-start | bytes 2359296
  17.3 131.1 %copy-start.19 = (bf16[64,768]{0,1:T(8,128)(2,1)}, bf16[64,768]{0,1:T(8,128)(2,1)S(1)}, u32[]{:S(2)}) copy-start(bf16[64,768]{0,1:T(8,128)(2,1)S(1)} %copy.77) | copy-start | bytes 294916
  17.5 121.4 %copy-start.21 = (bf16[64,768]{0,1:T(8,128)(2,1)}, bf16[64,768]{0,1:T(8,128)(2,1)S(1)}, u32[]{:S(2)}) copy-start(bf16[64,768]{0,1:T(8,128)(2,1)S(1)} %copy.75) | copy-start | bytes 294916
  62.2 4.5 %copy-start.37 = (bf16[4,1024,768]{2,1,0:T(8,128)(2,1)S(1)}, bf16[4,1024,768]{2,1,0:T(8,128)(2,1)}, u32[]{:S(2)}) copy-start(bf16[4,1024,768]{2,1,0:T(8,128)(2,1)} %all-gather.3.cloned.1.call-done) | copy-start | bytes 18874372
  62.2 4.8 %copy-start.39 = (bf16[768,768]{1,0:T(8,128)(2,1)S(1)}, bf16[768,768]{1,0:T(8,128)(2,1)}, u32[]{:S(2)}) copy-start(bf16[768,768]{1,0:T(8,128)(2,1)} %param.12) | copy-start | bytes 3538948
  67.0 77.4 %copy-start.14 = (bf16[1024,768]{0,1:T(8,128)(2,1)}, bf16[1024,768]{0,1:T(8,128)(2,1)S(1)}, u32[]{:S(2)}) copy-start(bf16[1024,768]{0,1:T(8,128)(2,1)S(1)} %get-tuple-element.11) | copy-start | bytes 4718596
  134.7 4.1 %copy-start.9 = (f32[16,64,1024]{2,1,0:T(8,128)}, f32[16,64,1024]{2,1,0:T(8,128)S(1)}, u32[]{:S(2)}) copy-start(f32[16,64,1024]{2,1,0:T(8,128)S(1)} %multiply_add_fusion.2) | copy-start | bytes 12582916
  134.7 5.1 %copy-start.2 = (f32[16,64,1024]{2,1,0:T(8,128)S(1)}, f32[16,64,1024]{2,1,0:T(8,128)}, u32[]{:S(2)}) copy-start(f32[16,64,1024]{2,1,0:T(8,128)} %all-gather.5.cloned.1.call-done) | copy-start | bytes 12582916
  134.7 5.6 %copy-start.15 = (bf16[1024,768]{0,1:T(8,128)(2,1)S(1)}, bf16[1024,768]{0,1:T(8,128)(2,1)}, u32[]{:S(2)}) copy-start(bf16[1024,768]{0,1:T(8,128)(2,1)} %get-tuple-element.13) | copy-start | bytes 4718596
  141.1 3.3 copy-start.8
  145.1 3.2 copy-start.7
  145.1 3.2 copy-start.16
  149.1 3.2 copy-start.6
  149.1 3.2 copy-start.35
  152.4 6.8 %copy-start.26 = (bf16[1024,768]{0,1:T(8,128)(2,1)S(1)}, bf16[1024,768]{0,1:T(8,128)(2,1)}, u32[]{:S(2)}) copy-start(bf16[1024,768]{0,1:T(8,128)(2,1)} %get-tuple-element.10) | copy-start | bytes 4718596
  159.2 5.0 %copy-start.34 = (bf16[64,768]{0,1:T(8,128)(2,1)S(1)}, bf16[64,768]{0,1:T(8,128)(2,1)}, u32[]{:S(2)}) copy-start(bf16[64,768]{0,1:T(8,128)(2,1)} %copy.76) | copy-start | bytes 294916
  164.2 6.8 %copy-start.25 = (bf16[1024,768]{0,1:T(8,128)(2,1)S(1)}, bf16[1024,768]{0,1:T(8,128)(2,1)}, u32[]{:S(2)}) copy-start(bf16[1024,768]{0,1:T(8,128)(2,1)} %get-tuple-element.9) | copy-start | bytes 4718596
  171.0 5.0 %copy-start.33 = (bf16[64,768]{0,1:T(8,128)(2,1)S(1)}, bf16[64,768]{0,1:T(8,128)(2,1)}, u32[]{:S(2)}) copy-start(bf16[64,768]{0,1:T(8,128)(2,1)} %copy.72) | copy-start | bytes 294916
  182.9 5.8 %copy-start.13 = (f32[16,64,1024]{2,1,0:T(8,128)S(1)}, f32[16,64,1024]{2,1,0:T(8,128)}, u32[]{:S(2)}) copy-start(f32[16,64,1024]{2,1,0:T(8,128)} %get-tuple-element.36) | copy-start | bytes 12582916
  182.9 5.8 %copy-start.24 = (bf16[1024,768]{0,1:T(8,128)(2,1)S(1)}, bf16[1024,768]{0,1:T(8,128)(2,1)}, u32[]{:S(2)}) copy-start(bf16[1024,768]{0,1:T(8,128)(2,1)} %get-tuple-element.8) | copy-start | bytes 4718596
  182.9 5.8 %copy-start.31 = (bf16[64,768]{0,1:T(8,128)(2,1)S(1)}, bf16[64,768]{0,1:T(8,128)(2,1)}, u32[]{:S(2)}) copy-start(bf16[64,768]{0,1:T(8,128)(2,1)} %copy.78) | copy-start | bytes 294916
  182.9 8.9 %copy-start.18 = (f32[16,64,1024]{2,1,0:T(8,128)S(1)}, f32[16,64,1024]{2,1,0:T(8,128)}, u32[]{:S(2)}) copy-start(f32[16,64,1024]{2,1,0:T(8,128)} %get-tuple-element.30) | copy-start | bytes 12582916
  188.7 4.3 %copy-start.10 = (f32[16,64,1024]{2,1,0:T(8,128)S(1)}, f32[16,64,1024]{2,1,0:T(8,128)}, u32[]{:S(2)}) copy-start(f32[16,64,1024]{2,1,0:T(8,128)} %get-tuple-element.28) | copy-start | bytes 12582916
  188.7 5.5 %copy-start.11 = (f32[16,64,1024]{2,1,0:T(8,128)S(1)}, f32[16,64,1024]{2,1,0:T(8,128)}, u32[]{:S(2)}) copy-start(f32[16,64,1024]{2,1,0:T(8,128)} %get-tuple-element.32) | copy-start | bytes 12582916
  188.7 6.7 %copy-start.12 = (f32[16,64,1024]{2,1,0:T(8,128)S(1)}, f32[16,64,1024]{2,1,0:T(8,128)}, u32[]{:S(2)}) copy-start(f32[16,64,1024]{2,1,0:T(8,128)} %get-tuple-element.24) | copy-start | bytes 12582916
  195.4 7.8 %copy-start.20 = (bf16[64,768]{0,1:T(8,128)(2,1)S(1)}, bf16[64,768]{0,1:T(8,128)(2,1)}, u32[]{:S(2)}) copy-start(bf16[64,768]{0,1:T(8,128)(2,1)} %copy-done.19) | copy-start | bytes 294916
  203.2 3.6 copy-start.4
  203.2 3.6 copy-start.5
  203.2 3.6 copy-start.3
  203.2 1.8 copy-start.22
  203.2 3.6 copy-start.23
  216.5 7.0 %copy-start.32 = (bf16[64,768]{0,1:T(8,128)(2,1)S(1)}, bf16[64,768]{0,1:T(8,128)(2,1)}, u32[]{:S(2)}) copy-start(bf16[64,768]{0,1:T(8,128)(2,1)} %copy.78) | copy-start | bytes 294916
  223.1 152.0 %reduce-scatter.5.cloned.1.call-start = ((), (), s32[]{:S(2)}) async-start(), calls=%async_computation.4 | async-start | bytes 6684672 | tf_op jit(solution)/shard_map/reduce_scatter | solution.py:113
  230.3 3.4 copy-start.29
  230.3 3.4 copy-start.38
  233.7 1.5 copy-start.28
  236.7 1.5 copy-start.40
  236.7 1.8 copy-start.43
  238.5 1.5 copy-start.41
  240.0 1.5 copy-start.42
  241.5 1.5 copy-start.44
  258.8 41.0 %copy-start.36 = (bf16[128,16]{0,1:T(8,128)(2,1)S(1)}, bf16[128,16]{0,1:T(8,128)(2,1)}, u32[]{:S(2)}) copy-start(bf16[128,16]{0,1:T(8,128)(2,1)} %param.14) | copy-start | bytes 12292
  261.7 115.8 %copy-start.1 = (bf16[64,128,128]{2,1,0:T(8,128)(2,1)S(1)}, bf16[64,128,128]{2,1,0:T(8,128)(2,1)}, u32[]{:S(2)}) copy-start(bf16[64,128,128]{2,1,0:T(8,128)(2,1)} %param.9) | copy-start | bytes 6291460
  (1 other events, 1.5 us)
Sparse Core Ops, SparseCore 0:
  9.7 44.8 all-gather.2
  56.8 74.4 all-gather.4
  223.2 72.8 reduce-scatter.6
  298.4 76.6 reduce-scatter.4
where the time goes:
time: 391 us; the launch traced here: 384 us
  waiting for transfers between devices  198 us (51%)
  matrix products  105 us (27%)
  local copies, waits for them, and re-layouts  41.4 us (11%)
  other arithmetic  24.8 us (6%)
  between operations  14.4 us (4%)
    reduce_scatter x1, waiting for transfers between devices, local(): lax.psum_scatter(jnp.stack(mapped_parts).astype(jnp.bfloat16), 'tok', sca...  73.2 us
    all_gather x1, waiting for transfers between devices, local(): pair_bias = lax.all_gather(bias_piece, 'sample', axis=2, tiled=True)  55.7 us
    all_gather x1, waiting for transfers between devices, local(): shard_rows = lax.all_gather(single, 'tok', axis=1, tiled=True)  36.3 us
    unnamed x5, waiting for transfers between devices  33.2 us
    dot_general x4, matrix products, attend(): jnp.einsum('hij,ihd->jhd', probs_low, out_heads, preferred_element_type=j...  27.2 us
    unnamed x94, local copies, waits for them, and re-layouts  27 us
    dot_general x11, matrix products, times_transpose(): lax.dot_general(matrix, weight, (((1,), (1,)), ((), ())), preferred_eleme...  20.3 us
    dot_general x4, matrix products, attend(): jnp.einsum('ihd,jhd->hij', out_heads, value_heads, preferred_element_type...  18.8 us
  transfers between devices with their start and end apart: 4, of which 4 were waited for; matrix products, arithmetic and copies ran while one was open for 19% of the time, Pallas kernels for 0%

commit v1 on v0

v1 whole, which is shorter than its diff:
```python
import math
import functools
import jax, jax.numpy as jnp
from jax import lax
from jax.experimental import pallas as pl
from jax.experimental.pallas import tpu as pltpu
from jax.sharding import PartitionSpec as P

F32 = jnp.float32
BF16 = jnp.bfloat16
LOG2E = 1.4426950408889634
NB = 4
HEADS = 16
WIDTH = 768
HD = 48
TOK = 1024


def prep_body(order_ref, r_ref, q_ref, o_ref, qt_ref, ot_ref, kt_ref, vt_ref, k_ref):
    def piece(slot, first, sample):
        lanes = slice(sample * 64, sample * 64 + 64)
        return jnp.concatenate([r_ref[first, slot, :, lanes], r_ref[first + 1, slot, :, lanes]], axis=1)

    def turned(block):
        return block.astype(F32).T.astype(BF16)

    for u in range(8):
        cols = slice(u * 128, u * 128 + 128)
        other = order_ref[u] * 2
        for b in range(NB):
            qt = piece(0, 2 * u, b)
            qt_ref[b, :, cols] = qt
            q_ref[b, cols, :] = turned(qt)
            ot = piece(3, 2 * u, b)
            ot_ref[b, :, cols] = ot
            o_ref[b, cols, :] = turned(ot)
            kt = piece(1, other, b)
            kt_ref[b, :, cols] = kt
            k_ref[b, cols, :] = turned(kt)
            vt_ref[b, :, cols] = piece(2, other, b)


def prep(order, received):
    nat = jax.ShapeDtypeStruct((NB, TOK, HD), BF16)
    tr = jax.ShapeDtypeStruct((NB, HD, TOK), BF16)
    vm = pl.BlockSpec(memory_space=pltpu.VMEM)
    return pl.pallas_call(
        prep_body,
        out_shape=[nat, nat, tr, tr, tr, tr, nat],
        in_specs=[pl.BlockSpec(memory_space=pltpu.SMEM), vm],
        out_specs=[vm] * 7,
        compiler_params=pltpu.CompilerParams(vmem_limit_bytes=32 * 2**20),
        name="prep",
    )(order, received)


TILE = 256


def attend_body(scale, steps, order_ref, bias_ref, q_ref, o_ref, qt_ref, ot_ref, kt_ref, vt_ref, k_ref,
                dbias_ref, g_ref, s_ref, dp_ref, p_ref, ds_ref, acc_ref, dqt_ref, dkt_ref, dvt_ref):
    step = pl.program_id(0)

    @pl.when(step == 0)
    def _():
        dkt_ref[...] = jnp.zeros_like(dkt_ref)
        dvt_ref[...] = jnp.zeros_like(dvt_ref)

    G = 16
    for b in range(NB):
        s_ref[b % 2] = jnp.dot(q_ref[b], kt_ref[b], preferred_element_type=F32)
        dp_ref[b % 2] = jnp.dot(o_ref[b], vt_ref[b], preferred_element_type=F32)
        for g in range(TILE // G):
            rows = slice(g * G, g * G + G)
            bias = jnp.concatenate([bias_ref[u, rows, :] for u in range(8)], axis=1)
            s = s_ref[b % 2, rows, :] * (scale * LOG2E) + bias
            m = jnp.max(s, axis=1, keepdims=True)
            e = jnp.exp2(s - m)
            inv = 1.0 / jnp.sum(e, axis=1, keepdims=True)
            p = e * inv
            dp = dp_ref[b % 2, rows, :]
            rd = jnp.sum(p * dp, axis=1, keepdims=True)
            ds = p * (dp - rd)
            p_ref[b % 2, rows, :] = p.astype(BF16)
            ds_ref[b % 2, rows, :] = ds.astype(BF16)
            if b == 0:
                acc_ref[rows, :] = ds
            elif b < NB - 1:
                acc_ref[rows, :] += ds
            else:
                tot = (acc_ref[rows, :] + ds).astype(BF16)
                for u in range(8):
                    dbias_ref[u, rows, :] = tot[:, u * 128:u * 128 + 128]
        pl_, dl = p_ref[b % 2], ds_ref[b % 2]
        dkt_ref[b] += jnp.dot(qt_ref[b], dl, preferred_element_type=F32)
        dvt_ref[b] += jnp.dot(ot_ref[b], pl_, preferred_element_type=F32)
        dq = jnp.dot(dl, k_ref[b], preferred_element_type=F32)
        dqt_ref[step, b] = (dq * scale).T.astype(BF16)

    @pl.when(step == steps - 1)
    def _():
        for b in range(NB):
            lanes = slice(b * 64, b * 64 + 64)
            for t in range(16):
                c = (t % 4) * 64
                g_ref[t, 0, :, lanes] = dqt_ref[t // 4, b, :, c:c + 64]
            for u in range(8):
                first = order_ref[u] * 2
                dk = (dkt_ref[b, :, u * 128:u * 128 + 128] * scale).astype(BF16)
                dv = dvt_ref[b, :, u * 128:u * 128 + 128].astype(BF16)
                g_ref[first, 1, :, lanes] = dk[:, :64]
                g_ref[first + 1, 1, :, lanes] = dk[:, 64:]
                g_ref[first, 2, :, lanes] = dv[:, :64]
                g_ref[first + 1, 2, :, lanes] = dv[:, 64:]


def attend(order, bias, q, o, qt, ot, kt, vt, k):
    steps = TOK // TILE
    scale = 1.0 / math.sqrt(HD)
    nat_t = pl.BlockSpec((NB, TILE, HD), lambda i: (0, i, 0))
    tr_t = pl.BlockSpec((NB, HD, TILE), lambda i: (0, 0, i))
    tr_w = pl.BlockSpec((NB, HD, TOK), lambda i: (0, 0, 0))
    nat_w = pl.BlockSpec((NB, TOK, HD), lambda i: (0, 0, 0))
    bias_t = pl.BlockSpec((8, TILE, 128), lambda i: (0, i, 0))
    return pl.pallas_call(
        functools.partial(attend_body, scale, steps),
        grid=(steps,),
        out_shape=[jax.ShapeDtypeStruct((8, TOK, 128), BF16), jax.ShapeDtypeStruct((16, 3, HD, 256), BF16)],
        in_specs=[pl.BlockSpec(memory_space=pltpu.SMEM), bias_t, nat_t, nat_t, tr_t, tr_t, tr_w, tr_w, nat_w],
        out_specs=[bias_t, pl.BlockSpec((16, 3, HD, 256), lambda i: (0, 0, 0, 0))],
        scratch_shapes=[
            pltpu.VMEM((2, TILE, TOK), F32), pltpu.VMEM((2, TILE, TOK), F32),
            pltpu.VMEM((2, TILE, TOK), BF16), pltpu.VMEM((2, TILE, TOK), BF16),
            pltpu.VMEM((TILE, TOK), F32), pltpu.VMEM((steps, NB, HD, TILE), BF16),
            pltpu.VMEM((NB, HD, TOK), F32), pltpu.VMEM((NB, HD, TOK), F32),
        ],
        compiler_params=pltpu.CompilerParams(vmem_limit_bytes=48 * 2**20),
        name="attend",
    )(order, bias, q, o, qt, ot, kt, vt, k)


def bias_body(pair_ref, w_ref, out_ref):
    for g in range(8):
        cols = jnp.concatenate([pair_ref[g * 8 + r] for r in range(8)], axis=1)
        t = lax.dot_general(w_ref[...], cols, (((1,), (1,)), ((), ())), preferred_element_type=F32)
        t = t * LOG2E
        for h in range(16):
            out_ref[h, g * 8:g * 8 + 8, :] = t[h * 8:h * 8 + 8, :]


def bias_part(pair, w_pair):
    eye = jnp.eye(8, dtype=BF16)
    w = (w_pair.T[:, None, None, :] * eye[None, :, :, None]).reshape(128, 1024)
    vm = pl.BlockSpec(memory_space=pltpu.VMEM)
    return pl.pallas_call(
        bias_body, out_shape=jax.ShapeDtypeStruct((16, 64, 128), F32),
        in_specs=[vm, vm], out_specs=vm,
        compiler_params=pltpu.CompilerParams(vmem_limit_bytes=32 * 2**20), name="bias_part",
    )(pair, w)


def gpair_body(x_ref, w_ref, out_ref):
    for g in range(4):
        x = x_ref[:, g * 16:g * 16 + 16, :].reshape(256, 128)
        t = lax.dot_general(x, w_ref[...], (((0,), (0,)), ((), ())), preferred_element_type=F32)
        for r in range(16):
            out_ref[g * 16 + r] = t[:, r * 128:r * 128 + 128].astype(BF16)


def gpair(x, w_pair):
    eye = jnp.eye(16, dtype=BF16)
    w = (w_pair.T[:, None, None, :] * eye[None, :, :, None]).reshape(256, 2048)
    vm = pl.BlockSpec(memory_space=pltpu.VMEM)
    return pl.pallas_call(
        gpair_body, out_shape=jax.ShapeDtypeStruct((64, 128, 128), BF16),
        in_specs=[vm, vm], out_specs=vm,
        compiler_params=pltpu.CompilerParams(vmem_limit_bytes=32 * 2**20), name="gpair",
    )(x, w)


def project_body(x_ref, c_ref, wq_ref, wk_ref, wv_ref, wo_ref, out_ref):
    x = x_ref[...].reshape(NB * 64, WIDTH)
    c = c_ref[...].reshape(NB * 64, WIDTH)
    for slot, w_ref in enumerate((wq_ref, wk_ref, wv_ref)):
        t = jnp.dot(x, w_ref[...], preferred_element_type=F32).T.astype(BF16)
        for h in range(HEADS):
            out_ref[h, slot] = t[h * HD:h * HD + HD, :]
    t = lax.dot_general(wo_ref[...], c, (((1,), (1,)), ((), ())), preferred_element_type=F32).astype(BF16)
    for h in range(HEADS):
        out_ref[h, 3] = t[h * HD:h * HD + HD, :]


def project(single, cotangent, w_query, w_key, w_value, w_out):
    vm = pl.BlockSpec(memory_space=pltpu.VMEM)
    return pl.pallas_call(
        project_body, out_shape=jax.ShapeDtypeStruct((HEADS, 4, HD, NB * 64), BF16),
        in_specs=[vm] * 6, out_specs=vm,
        compiler_params=pltpu.CompilerParams(vmem_limit_bytes=40 * 2**20), name="project",
    )(single, cotangent, w_query, w_key, w_value, w_out)


def final_body(g_ref, wq_ref, wk_ref, wv_ref, out_ref):
    total = None
    for slot, w_ref in enumerate((wq_ref, wk_ref, wv_ref)):
        part = jnp.dot(w_ref[...], g_ref[:, slot].reshape(WIDTH, NB * 64), preferred_element_type=F32)
        total = part if total is None else total + part
    out_ref[...] = total.T.astype(BF16).reshape(NB, 64, WIDTH)


def final(g, w_query, w_key, w_value):
    vm = pl.BlockSpec(memory_space=pltpu.VMEM)
    return pl.pallas_call(
        final_body, out_shape=jax.ShapeDtypeStruct((NB, 64, WIDTH), BF16),
        in_specs=[vm] * 4, out_specs=vm,
        compiler_params=pltpu.CompilerParams(vmem_limit_bytes=40 * 2**20), name="final",
    )(g, w_query, w_key, w_value)


def shift_y(x, d):
    return lax.ppermute(x, "sample", [(i, ((i // 2 + d) % 4) * 2 + i % 2) for i in range(8)])


def swap_x(x):
    return lax.ppermute(x, "sample", [(i, i ^ 1) for i in range(8)])


def gather_blocks(own):
    half = own.shape[0] // 2
    pair = [own, swap_x(own)]
    up = [shift_y(v, 1) for v in pair]
    down = [shift_y(v, -1) for v in pair]
    far = [jnp.concatenate([shift_y(u[:half], 1), shift_y(d[half:], -1)]) for u, d in zip(up, down)]
    return jnp.stack(pair + up + down + far)


def key_order():
    me = lax.axis_index("sample")
    y, x = me // 2, me % 2
    return jnp.stack([((y + d) % 4) * 2 + (x ^ e) for d in (0, 3, 1, 2) for e in (0, 1)]).astype(jnp.int32)


def plus(a, b):
    return (a.astype(F32) + b.astype(F32)).astype(BF16)


def scatter_blocks(blocks):
    half = blocks.shape[1] // 2
    sums = []
    for e in (1, 0):
        far, up, down = blocks[6 + e], blocks[4 + e], blocks[2 + e]
        from_down = shift_y(far[:half], 1)
        from_up = shift_y(far[half:], -1)
        up = jnp.concatenate([plus(up[:half], from_down), up[half:]])
        down = jnp.concatenate([down[:half], plus(down[half:], from_up)])
        total = blocks[e].astype(F32) + shift_y(up, 1).astype(F32) + shift_y(down, -1).astype(F32)
        sums.append(total)
    return (sums[1] + swap_x(sums[0].astype(BF16)).astype(F32)).astype(BF16)


def local(single, pair, w_query, w_key, w_value, w_out, w_pair, cotangent):
    order = key_order()
    bias = lax.all_to_all(bias_part(pair, w_pair), "tok", 0, 0).reshape(TOK, 128)
    bias = gather_blocks(bias)
    sent = project(single, cotangent, w_query, w_key, w_value, w_out)
    held = prep(order, lax.all_to_all(sent, "tok", 0, 0))
    dbias, grads = attend(order, bias, *held)
    grads = lax.all_to_all(grads, "tok", 0, 0)
    grad_single = final(grads, w_query, w_key, w_value)
    dbias = scatter_blocks(dbias).reshape(16, 64, 128)
    grad_pair = gpair(lax.all_to_all(dbias, "tok", 0, 0), w_pair)
    return (grad_single, grad_pair)


def solution(mesh):
    rows, keys = P("sample", "tok", None), P("tok", "sample", None)
    return jax.shard_map(
        local, mesh=mesh, in_specs=(rows, keys, P(), P(), P(), P(), P(), rows),
        out_specs=(rows, keys), check_vma=False,
    )
```

time: 391 us -> 185 us (0.47); the launches traced: 384 us -> 183 us
  waiting for transfers between devices: 198 us -> 65.7 us
  matrix products: 105 us -> 0 us
  starting transfers between devices: 0.57 us -> 43.7 us
  Pallas kernels: 0 us -> 31.8 us
  local copies, waits for them, and re-layouts: 41.4 us -> 21.4 us
  other arithmetic: 24.8 us -> 7.27 us
  between operations: 14.4 us -> 0.88 us
  blocking collectives: 0 us -> 12.6 us
    dot_general x35 -> x0, matrix products: 105 us -> none  [the longest x4 27.2 us: attend(): jnp.einsum('hij,ihd->jhd', probs_low, out_heads, preferred_element_type=j...]
    all_gather x2 -> x0, waiting for transfers between devices: 92 us -> none  [the longest x1 55.7 us: local(): pair_bias = lax.all_gather(bias_piece, 'sample', axis=2, tiled=True)]
    reduce_scatter x1 -> x0, waiting for transfers between devices: 73.2 us -> none  [local(): lax.psum_scatter(jnp.stack(mapped_parts).astype(jnp.bfloat16), 'tok', sca...]
    ppermute x0 -> x18, waiting for transfers between devices: none -> 44.4 us  [the longest x2 33.2 us: swap_x(): return lax.ppermute(x, 'sample', [(i, i ^ 1) for i in range(8)])]
    unnamed x5 -> x0, waiting for transfers between devices: 33.2 us -> none
    pallas_call x0 -> x6, Pallas kernels: none -> 31.8 us  [the longest x1 19.8 us: attend(): pl.pallas_call(functools.partial(attend_body, scale, steps), grid=(steps,...]
    ppermute x0 -> x18, starting transfers between devices: none -> 29 us  [the longest x16 25.3 us: shift_y(): lax.ppermute(x, 'sample', [(i, (i // 2 + d) % 4 * 2 + i % 2) for i in ran...]
    all_to_all x0 -> x3, waiting for transfers between devices: none -> 21.3 us  [the longest x1 15.5 us: local(): grads = lax.all_to_all(grads, 'tok', 0, 0)]
  transfers between devices with their start and end apart: 4 -> 21, of which waited for: 4 -> 11; matrix products, arithmetic and copies ran while one was open for 19% -> 9% of each run, Pallas kernels for 0% -> 4%
where the time goes in v1:
time: 185 us; the launch traced here: 183 us
  waiting for transfers between devices  65.7 us (36%)
  starting transfers between devices  43.7 us (24%)
  Pallas kernels  31.8 us (17%)
  local copies, waits for them, and re-layouts  21.4 us (12%)
  blocking collectives  12.6 us (7%)
  other arithmetic  7.27 us (4%)
    ppermute x2, waiting for transfers between devices, swap_x(): return lax.ppermute(x, 'sample', [(i, i ^ 1) for i in range(8)])  33.2 us
    ppermute x16, starting transfers between devices, shift_y(): lax.ppermute(x, 'sample', [(i, (i // 2 + d) % 4 * 2 + i % 2) for i in ran...  25.3 us
    pallas_call x1, Pallas kernels, attend(): pl.pallas_call(functools.partial(attend_body, scale, steps), grid=(steps,...  19.8 us
    unnamed x29, local copies, waits for them, and re-layouts  15.9 us
    all_to_all x1, waiting for transfers between devices, local(): grads = lax.all_to_all(grads, 'tok', 0, 0)  15.5 us
    all_to_all x1, blocking collectives, local(): grad_pair = gpair(lax.all_to_all(dbias, 'tok', 0, 0), w_pair)  12.6 us
    ppermute x16, waiting for transfers between devices, shift_y(): lax.ppermute(x, 'sample', [(i, (i // 2 + d) % 4 * 2 + i % 2) for i in ran...  11.2 us
    all_to_all x1, starting transfers between devices, local(): lax.all_to_all(bias_part(pair, w_pair), 'tok', 0, 0).reshape(TOK, 128)  6.48 us
  transfers between devices with their start and end apart: 21, of which 11 were waited for; matrix products, arithmetic and copies ran while one was open for 9% of the time, Pallas kernels for 4%

profile of v1, /device:TPU:0, one launch (start us, length us, event | category | flops | bytes accessed | tf_op | source)
XLA Modules:
  0.0 183.3 jit_solution(6951580230380536524)
XLA Ops:
  0.7 0.9 multiply_bitcast_fusion.w_ref
  1.6 1.6 copy-done.5
  3.2 1.5 bias_part.1
  4.7 6.5 %all-to-all-start = ((f32[16,64,128]{2,1,0:T(8,128)}), f32[16,64,128]{2,1,0:T(8,128)}, u32[]{:S(2)}, u32[]{:S(2)}) async-start(f32[16,64,128]{2,1,0:T(8,128)} %bias_part.1), calls=%async_computation | async-start | bytes 1048576 | tf_op jit(solution)/shard_map/all_to_all | solution.py:262
  11.2 1.3 copy-done.3
  12.5 1.3 copy-done.6
  13.8 2.5 %project.1 = bf16[16,4,48,256]{3,2,1,0:T(8,128)(2,1)} custom-call(bf16[4,64,768]{2,1,0:T(8,128)(2,1)S(1)} %copy-done.8, bf16[4,64,768]{2,1,0:T(8,128)(2,1)S(1)} %copy-done.9, bf16[768,768]{1,0:T(8,128)(2,1)S(1)} %copy-done, bf16[768,768]{1,0:T(8,128)(2,1)S(1)} %copy-done.1, bf16[768,768]{1,0:T(8,128)(2,1)S(1)} %copy-done.3, bf16[768,768]{1,0:T(8,128)(2,1)S(1)} %copy-done.6), custom_call_target="tpu_custom_call" | custom-call | tf_op jit(solution)/shard_map/project/pallas_call | solution.py:195
  16.3 5.8 %all-to-all-done = f32[16,64,128]{2,1,0:T(8,128)} async-done(((f32[16,64,128]{2,1,0:T(8,128)}), f32[16,64,128]{2,1,0:T(8,128)}, u32[]{:S(2)}, u32[]{:S(2)}) %all-to-all-start) | async-done | bytes 524320 | tf_op jit(solution)/shard_map/all_to_all | solution.py:262
  22.1 3.7 %all-to-all-start.1 = ((bf16[16,4,48,256]{3,2,1,0:T(8,128)(2,1)}), bf16[16,4,48,256]{3,2,1,0:T(8,128)(2,1)S(1)}, u32[]{:S(2)}, u32[]{:S(2)}) async-start(bf16[16,4,48,256]{3,2,1,0:T(8,128)(2,1)} %project.1), calls=%async_computation.1 | async-start | bytes 3145728 | tf_op jit(solution)/shard_map/all_to_all | solution.py:265
  25.8 2.8 %collective-permute-start = (f32[1024,128]{1,0:T(8,128)}, f32[1024,128]{1,0:T(8,128)}, u32[]{:S(2)}, u32[]{:S(2)}) collective-permute-start(f32[1024,128]{1,0:T(8,128)} %bitcast.11), channel_id=1, source_target_pairs={{0,16},{16,0},{32,48},{48,32},{64,80},{80,64},{96,112},{112,96},{1... | collective-permute-start | bytes 1572872 | tf_op jit(solution)/shard_map/ppermute | solution.py:224
  28.6 3.0 %collective-permute-start.3 = (f32[1024,128]{1,0:T(8,128)}, f32[1024,128]{1,0:T(8,128)S(1)}, u32[]{:S(2)}, u32[]{:S(2)}) collective-permute-start(f32[1024,128]{1,0:T(8,128)} %bitcast.11), channel_id=1, source_target_pairs={{0,96},{16,112},{32,0},{48,16},{64,32},{80,48},{96,64},{112,80},{1... | collective-permute-start | bytes 1572872 | tf_op jit(solution)/shard_map/ppermute | solution.py:220
  31.7 27.6 %collective-permute-done = f32[1024,128]{1,0:T(8,128)} collective-permute-done((f32[1024,128]{1,0:T(8,128)}, f32[1024,128]{1,0:T(8,128)}, u32[]{:S(2)}, u32[]{:S(2)}) %collective-permute-start) | collective-permute-done | bytes 524320 | tf_op jit(solution)/shard_map/ppermute | solution.py:224
  59.4 1.6 collective-permute-start.2
  60.9 1.7 collective-permute-start.4
  62.6 1.9 %bitcast_dynamic-update-slice_fusion.5 = f32[8,1024,128]{2,1,0:T(8,128)} fusion(f32[1,1024,128]{2,1,0:T(8,128)} %bitcast.72), kind=kLoop, calls=%fused_computation.17 | loop fusion | bytes 1048576
  64.5 1.9 %collective-permute-start.6 = (f32[512,128]{1,0:T(8,128)S(1)}, f32[512,128]{1,0:T(8,128)}, u32[]{:S(2)}, u32[]{:S(2)}) collective-permute-start(f32[512,128]{1,0:T(8,128)S(1)} %slice.127), channel_id=1, source_target_pairs={{0,96},{16,112},{32,0},{48,16},{64,32},{80,48},{96,64},{112,80},{1... | collective-permute-start | bytes 786440 | tf_op jit(solution)/shard_map/ppermute | solution.py:220
  66.4 1.7 slice.126
  68.3 1.9 %bitcast_dynamic-update-slice_fusion.4 = f32[8,1024,128]{2,1,0:T(8,128)} fusion(f32[8,1024,128]{2,1,0:T(8,128)} %bitcast_dynamic-update-slice_fusion.5, f32[1024,128]{1,0:T(8,128)} %collective-permute-done), kind=kLoop, calls=%fused_computation.16 | loop fusion | bytes 1048576
  70.1 1.9 %bitcast_dynamic-update-slice_fusion.3 = f32[8,1024,128]{2,1,0:T(8,128)} fusion(f32[8,1024,128]{2,1,0:T(8,128)} %bitcast_dynamic-update-slice_fusion.4, f32[1024,128]{1,0:T(8,128)} %collective-permute-done.1), kind=kLoop, calls=%fused_computation.15 | loop fusion | bytes 1048576
  72.0 2.8 %prep.1 = (bf16[4,1024,48]{2,1,0:T(8,128)(2,1)S(1)}, bf16[4,1024,48]{2,1,0:T(8,128)(2,1)S(1)}, bf16[4,48,1024]{2,1,0:T(8,128)(2,1)S(1)}, bf16[4,48,1024]{2,1,0:T...) custom-call(s32[8]{0:T(128)S(1)} %stack.59.order_ref, ...), custom_call_target="tpu_custom_call" | custom-call | tf_op jit(solution)/shard_map/prep/pallas_call | solution.py:47
  74.8 1.3 collective-permute-done.4
  76.1 1.0 slice.129
  77.1 2.9 %collective-permute-start.8 = (f32[512,128]{1,0:T(8,128)S(1)}, f32[512,128]{1,0:T(8,128)S(1)}, u32[]{:S(2)}, u32[]{:S(2)}) collective-permute-start(f32[512,128]{1,0:T(8,128)S(1)} %slice.129), channel_id=1, source_target_pairs={{0,96},{16,112},{32,0},{48,16},{64,32},{80,48},{96,64},{112,80},{1... | collective-permute-start | bytes 786440 | tf_op jit(solution)/shard_map/ppermute | solution.py:220
  80.0 1.0 slice.128
  81.2 1.9 %bitcast_dynamic-update-slice_fusion.2 = f32[8,1024,128]{2,1,0:T(8,128)} fusion(f32[8,1024,128]{2,1,0:T(8,128)} %bitcast_dynamic-update-slice_fusion.3, f32[1024,128]{1,0:T(8,128)} %collective-permute-done.2), kind=kLoop, calls=%fused_computation.14 | loop fusion | bytes 1048576
  84.0 1.9 %bitcast_dynamic-update-slice_fusion = f32[8,1024,128]{2,1,0:T(8,128)} fusion(f32[8,1024,128]{2,1,0:T(8,128)} %bitcast_dynamic-update-slice_fusion.1, f32[1024,128]{1,0:T(8,128)} %collective-permute-done.4), kind=kLoop, calls=%fused_computation.12 | loop fusion | bytes 1048576
  85.8 1.9 %fusion = f32[8,1024,128]{2,1,0:T(8,128)} fusion(f32[8,1024,128]{2,1,0:T(8,128)} %bitcast_dynamic-update-slice_fusion, f32[512,128]{1,0:T(8,128)} %collective-permute-done.6, f32[512,128]{1,0:T(8,128)} %collective-permute-done.5), kind=kLoop, calls=%fused_computation.2 | loop fusion | flops 131072 | bytes 1048576
  87.7 1.1 collective-permute-done.7
  89.6 19.8 %attend.1 = (bf16[8,1024,128]{2,1,0:T(8,128)(2,1)}, bf16[16,3,48,256]{3,2,1,0:T(8,128)(2,1)S(1)}) custom-call(s32[8]{0:T(128)S(1)} %stack.59.order_ref, f32[8,1024,128]{2,1,0:T(8,128)} %fusion.1.bias_ref, bf16[4,1024,48]{2,1,0:T(8,128)(2,1)S(1)} %get-tuple-element.11.q_ref, bf16[4,1024,48]{2,1,0:T(8,128)(2,1)S(1)} %get-tuple-element.12.o_ref, ...), custom_call_target="tpu_custom_call" | custom-call | tf_op jit(solution)/shard_map/attend/pallas_call | solution.py:125
  109.4 1.8 slice_bitcast_fusion.7
  111.3 3.2 %collective-permute-start.15 = (bf16[512,128]{1,0:T(8,128)(2,1)S(1)}, bf16[512,128]{1,0:T(8,128)(2,1)S(1)}, u32[]{:S(2)}, u32[]{:S(2)}) collective-permute-start(bf16[512,128]{1,0:T(8,128)(2,1)S(1)} %get-tuple-element.25), channel_id=1, source_target_pairs={{0,96},{16,112},{32,0},{48,16},{64,32},{80,48},{96,64},{112,80},{1... | collective-permute-start | bytes 393224 | tf_op jit(solution)/shard_map/ppermute | solution.py:220
  114.5 3.2 %collective-permute-start.11 = (bf16[512,128]{1,0:T(8,128)(2,1)S(1)}, bf16[512,128]{1,0:T(8,128)(2,1)S(1)}, u32[]{:S(2)}, u32[]{:S(2)}) collective-permute-start(bf16[512,128]{1,0:T(8,128)(2,1)S(1)} %get-tuple-element.29), channel_id=1, source_target_pairs={{0,96},{16,112},{32,0},{48,16},{64,32},{80,48},{96,64},{112,80},{1... | collective-permute-start | bytes 393224 | tf_op jit(solution)/shard_map/ppermute | solution.py:220
  117.7 2.9 %collective-permute-done.13 = bf16[512,128]{1,0:T(8,128)(2,1)S(1)} collective-permute-done((bf16[512,128]{1,0:T(8,128)(2,1)S(1)}, bf16[512,128]{1,0:T(8,128)(2,1)S(1)}, u32[]{:S(2)}, u32[]{:S(2)}) %collective-permute-start.13) | collective-permute-done | bytes 131104 | tf_op jit(solution)/shard_map/ppermute | solution.py:220
  120.9 1.2 fusion.10
  122.1 3.8 %collective-permute-start.16 = (bf16[1024,128]{1,0:T(8,128)(2,1)S(1)}, bf16[1024,128]{1,0:T(8,128)(2,1)S(1)}, u32[]{:S(2)}, u32[]{:S(2)}) collective-permute-start(bf16[1024,128]{1,0:T(8,128)(2,1)S(1)} %pad_maximum_fusion.3), channel_id=1, source_target_pairs={{0,96},{16,112},{32,0},{48,16},{64,32},{80,48},{96,64},{112,80},{1... | collective-permute-start | bytes 786440 | tf_op jit(solution)/shard_map/ppermute | solution.py:220
  126.0 3.3 %collective-permute-start.12 = (bf16[1024,128]{1,0:T(8,128)(2,1)S(1)}, bf16[1024,128]{1,0:T(8,128)(2,1)S(1)}, u32[]{:S(2)}, u32[]{:S(2)}) collective-permute-start(bf16[1024,128]{1,0:T(8,128)(2,1)S(1)} %pad_maximum_fusion.1), channel_id=1, source_target_pairs={{0,96},{16,112},{32,0},{48,16},{64,32},{80,48},{96,64},{112,80},{1... | collective-permute-start | bytes 786440 | tf_op jit(solution)/shard_map/ppermute | solution.py:220
  129.8 3.8 %collective-permute-done.14 = bf16[1024,128]{1,0:T(8,128)(2,1)S(1)} collective-permute-done((bf16[1024,128]{1,0:T(8,128)(2,1)S(1)}, bf16[1024,128]{1,0:T(8,128)(2,1)S(1)}, u32[]{:S(2)}, u32[]{:S(2)}) %collective-permute-start.14) | collective-permute-done | bytes 262176 | tf_op jit(solution)/shard_map/ppermute | solution.py:220
  133.6 1.1 fusion.3
  134.6 0.9 collective-permute-start.17
  135.5 1.5 collective-permute-done.10
  137.0 5.6 %collective-permute-done.17 = bf16[1024,128]{1,0:T(8,128)(2,1)S(1)} collective-permute-done((bf16[1024,128]{1,0:T(8,128)(2,1)S(1)}, bf16[1024,128]{1,0:T(8,128)(2,1)S(1)}, u32[]{:S(2)}, u32[]{:S(2)}) %collective-permute-start.17) | collective-permute-done | bytes 262176 | tf_op jit(solution)/shard_map/ppermute | solution.py:224
  142.6 1.1 fusion.6
  143.7 12.6 %all_to_all.20.x_ref = bf16[16,64,128]{2,1,0:T(8,128)(2,1)S(1)} all-to-all(bf16[16,64,128]{2,1,0:T(8,128)(2,1)S(1)} %bitcast.75), channel_id=1, replica_groups=mesh['sample'=8,'tok'=16] {'tok'}, dimensions={0} | all-to-all | bytes 524288 | tf_op jit(solution)/shard_map/all_to_all | solution.py:270
  156.2 4.5 %all-to-all-start.2 = ((bf16[16,3,48,256]{3,2,1,0:T(8,128)(2,1)}), bf16[16,3,48,256]{3,2,1,0:T(8,128)(2,1)}, u32[]{:S(2)}, u32[]{:S(2)}) async-start(bf16[16,3,48,256]{3,2,1,0:T(8,128)(2,1)} %copy-done.7), calls=%async_computation.2 | async-start | bytes 2359296 | tf_op jit(solution)/shard_map/all_to_all | solution.py:267
  161.2 2.1 %gpair.1 = bf16[64,128,128]{2,1,0:T(8,128)(2,1)} custom-call(bf16[16,64,128]{2,1,0:T(8,128)(2,1)S(1)} %all_to_all.20.x_ref, bf16[256,2048]{1,0:T(8,128)(2,1)S(1)} %bitcast.73), custom_call_target="tpu_custom_call" | custom-call | tf_op jit(solution)/shard_map/gpair/pallas_call | solution.py:174
  163.3 15.5 %all-to-all-done.2.g_ref = bf16[16,3,48,256]{3,2,1,0:T(8,128)(2,1)} async-done(((bf16[16,3,48,256]{3,2,1,0:T(8,128)(2,1)}), bf16[16,3,48,256]{3,2,1,0:T(8,128)(2,1)}, u32[]{:S(2)}, u32[]{:S(2)}) %all-to-all-start.2) | async-done | bytes 1179680 | tf_op jit(solution)/shard_map/all_to_all | solution.py:267
  178.9 1.3 copy-done.4
  180.1 3.2 %final.1 = bf16[4,64,768]{2,1,0:T(8,128)(2,1)} custom-call(bf16[16,3,48,256]{3,2,1,0:T(8,128)(2,1)} %all-to-all-done.2.g_ref, bf16[768,768]{1,0:T(8,128)(2,1)S(1)} %copy-done, bf16[768,768]{1,0:T(8,128)(2,1)S(1)} %copy-done.2, bf16[768,768]{1,0:T(8,128)(2,1)S(1)} %copy-done.4), custom_call_target="tpu_custom_call" | custom-call | tf_op jit(solution)/shard_map/final/pallas_call | solution.py:212
  (49 shorter events, 3.6 us)
Async XLA Ops:
  0.6 10.6 %copy-start = (bf16[768,768]{1,0:T(8,128)(2,1)S(1)}, bf16[768,768]{1,0:T(8,128)(2,1)}, u32[]{:S(2)}) copy-start(bf16[768,768]{1,0:T(8,128)(2,1)} %wq_ref.3) | copy-start | bytes 3538948
  0.6 10.6 %copy-start.1 = (bf16[768,768]{1,0:T(8,128)(2,1)S(1)}, bf16[768,768]{1,0:T(8,128)(2,1)}, u32[]{:S(2)}) copy-start(bf16[768,768]{1,0:T(8,128)(2,1)} %wk_ref.3) | copy-start | bytes 3538948
  1.6 1.6 copy-start.5
  3.2 8.0 %copy-start.8 = (bf16[4,64,768]{2,1,0:T(8,128)(2,1)S(1)}, bf16[4,64,768]{2,1,0:T(8,128)(2,1)}, u32[]{:S(2)}) copy-start(bf16[4,64,768]{2,1,0:T(8,128)(2,1)} %x_ref.1) | copy-start | bytes 1179652
  3.2 8.0 %copy-start.9 = (bf16[4,64,768]{2,1,0:T(8,128)(2,1)S(1)}, bf16[4,64,768]{2,1,0:T(8,128)(2,1)}, u32[]{:S(2)}) copy-start(bf16[4,64,768]{2,1,0:T(8,128)(2,1)} %c_ref.1) | copy-start | bytes 1179652
  4.7 17.4 %all-to-all-start = ((f32[16,64,128]{2,1,0:T(8,128)}), f32[16,64,128]{2,1,0:T(8,128)}, u32[]{:S(2)}, u32[]{:S(2)}) async-start(f32[16,64,128]{2,1,0:T(8,128)} %bias_part.1), calls=%async_computation | async-start | bytes 1048576 | tf_op jit(solution)/shard_map/all_to_all | solution.py:262
  11.2 1.3 copy-start.3
  12.5 1.3 copy-start.6
  22.1 49.9 %all-to-all-start.1 = ((bf16[16,4,48,256]{3,2,1,0:T(8,128)(2,1)}), bf16[16,4,48,256]{3,2,1,0:T(8,128)(2,1)S(1)}, u32[]{:S(2)}, u32[]{:S(2)}) async-start(bf16[16,4,48,256]{3,2,1,0:T(8,128)(2,1)} %project.1), calls=%async_computation.1 | async-start | bytes 3145728 | tf_op jit(solution)/shard_map/all_to_all | solution.py:265
  25.8 33.5 %collective-permute-start = (f32[1024,128]{1,0:T(8,128)}, f32[1024,128]{1,0:T(8,128)}, u32[]{:S(2)}, u32[]{:S(2)}) collective-permute-start(f32[1024,128]{1,0:T(8,128)} %bitcast.11), channel_id=1, source_target_pairs={{0,16},{16,0},{32,48},{48,32},{64,80},{80,64},{96,112},{112,96},{1... | collective-permute-start | bytes 1572872 | tf_op jit(solution)/shard_map/ppermute | solution.py:224
  28.6 35.8 %collective-permute-start.3 = (f32[1024,128]{1,0:T(8,128)}, f32[1024,128]{1,0:T(8,128)S(1)}, u32[]{:S(2)}, u32[]{:S(2)}) collective-permute-start(f32[1024,128]{1,0:T(8,128)} %bitcast.11), channel_id=1, source_target_pairs={{0,96},{16,112},{32,0},{48,16},{64,32},{80,48},{96,64},{112,80},{1... | collective-permute-start | bytes 1572872 | tf_op jit(solution)/shard_map/ppermute | solution.py:220
  31.6 34.7 %collective-permute-start.1 = (f32[1024,128]{1,0:T(8,128)}, f32[1024,128]{1,0:T(8,128)}, u32[]{:S(2)}, u32[]{:S(2)}) collective-permute-start(f32[1024,128]{1,0:T(8,128)} %bitcast.11), channel_id=1, source_target_pairs={{0,32},{16,48},{32,64},{48,80},{64,96},{80,112},{96,0},{112,16},{1... | collective-permute-start | bytes 1572872 | tf_op jit(solution)/shard_map/ppermute | solution.py:220
  59.4 20.6 %collective-permute-start.2 = (f32[1024,128]{1,0:T(8,128)}, f32[1024,128]{1,0:T(8,128)}, u32[]{:S(2)}, u32[]{:S(2)}) collective-permute-start(f32[1024,128]{1,0:T(8,128)} %collective-permute-done), channel_id=1, source_target_pairs={{0,32},{16,48},{32,64},{48,80},{64,96},{80,112},{96,0},{112,16},{1... | collective-permute-start | bytes 1572872 | tf_op jit(solution)/shard_map/ppermute | solution.py:220
  60.9 15.2 %collective-permute-start.4 = (f32[1024,128]{1,0:T(8,128)}, f32[1024,128]{1,0:T(8,128)}, u32[]{:S(2)}, u32[]{:S(2)}) collective-permute-start(f32[1024,128]{1,0:T(8,128)} %collective-permute-done), channel_id=1, source_target_pairs={{0,96},{16,112},{32,0},{48,16},{64,32},{80,48},{96,64},{112,80},{1... | collective-permute-start | bytes 1572872 | tf_op jit(solution)/shard_map/ppermute | solution.py:220
  64.5 21.3 %collective-permute-start.6 = (f32[512,128]{1,0:T(8,128)S(1)}, f32[512,128]{1,0:T(8,128)}, u32[]{:S(2)}, u32[]{:S(2)}) collective-permute-start(f32[512,128]{1,0:T(8,128)S(1)} %slice.127), channel_id=1, source_target_pairs={{0,96},{16,112},{32,0},{48,16},{64,32},{80,48},{96,64},{112,80},{1... | collective-permute-start | bytes 786440 | tf_op jit(solution)/shard_map/ppermute | solution.py:220
  68.0 17.8 %collective-permute-start.5 = (f32[512,128]{1,0:T(8,128)}, f32[512,128]{1,0:T(8,128)}, u32[]{:S(2)}, u32[]{:S(2)}) collective-permute-start(f32[512,128]{1,0:T(8,128)} %slice.126), channel_id=1, source_target_pairs={{0,32},{16,48},{32,64},{48,80},{64,96},{80,112},{96,0},{112,16},{1... | collective-permute-start | bytes 786440 | tf_op jit(solution)/shard_map/ppermute | solution.py:220
  77.1 10.6 %collective-permute-start.8 = (f32[512,128]{1,0:T(8,128)S(1)}, f32[512,128]{1,0:T(8,128)S(1)}, u32[]{:S(2)}, u32[]{:S(2)}) collective-permute-start(f32[512,128]{1,0:T(8,128)S(1)} %slice.129), channel_id=1, source_target_pairs={{0,96},{16,112},{32,0},{48,16},{64,32},{80,48},{96,64},{112,80},{1... | collective-permute-start | bytes 786440 | tf_op jit(solution)/shard_map/ppermute | solution.py:220
  81.0 7.8 %collective-permute-start.7 = (f32[512,128]{1,0:T(8,128)S(1)}, f32[512,128]{1,0:T(8,128)S(1)}, u32[]{:S(2)}, u32[]{:S(2)}) collective-permute-start(f32[512,128]{1,0:T(8,128)S(1)} %slice.128), channel_id=1, source_target_pairs={{0,32},{16,48},{32,64},{48,80},{64,96},{80,112},{96,0},{112,16},{1... | collective-permute-start | bytes 786440 | tf_op jit(solution)/shard_map/ppermute | solution.py:220
  109.4 46.8 %copy-start.7 = (bf16[16,3,48,256]{3,2,1,0:T(8,128)(2,1)}, bf16[16,3,48,256]{3,2,1,0:T(8,128)(2,1)S(1)}, u32[]{:S(2)}) copy-start(bf16[16,3,48,256]{3,2,1,0:T(8,128)(2,1)S(1)} %get-tuple-element.18) | copy-start | bytes 3538948
  111.2 6.5 %collective-permute-start.9 = (bf16[512,128]{1,0:T(8,128)(2,1)S(1)}, bf16[512,128]{1,0:T(8,128)(2,1)S(1)}, u32[]{:S(2)}, u32[]{:S(2)}) collective-permute-start(bf16[512,128]{1,0:T(8,128)(2,1)S(1)} %get-tuple-element.24), channel_id=1, source_target_pairs={{0,32},{16,48},{32,64},{48,80},{64,96},{80,112},{96,0},{112,16},{1... | collective-permute-start | bytes 393224 | tf_op jit(solution)/shard_map/ppermute | solution.py:220
  111.3 6.5 %collective-permute-start.15 = (bf16[512,128]{1,0:T(8,128)(2,1)S(1)}, bf16[512,128]{1,0:T(8,128)(2,1)S(1)}, u32[]{:S(2)}, u32[]{:S(2)}) collective-permute-start(bf16[512,128]{1,0:T(8,128)(2,1)S(1)} %get-tuple-element.25), channel_id=1, source_target_pairs={{0,96},{16,112},{32,0},{48,16},{64,32},{80,48},{96,64},{112,80},{1... | collective-permute-start | bytes 393224 | tf_op jit(solution)/shard_map/ppermute | solution.py:220
  114.5 6.2 %collective-permute-start.13 = (bf16[512,128]{1,0:T(8,128)(2,1)S(1)}, bf16[512,128]{1,0:T(8,128)(2,1)S(1)}, u32[]{:S(2)}, u32[]{:S(2)}) collective-permute-start(bf16[512,128]{1,0:T(8,128)(2,1)S(1)} %get-tuple-element.28), channel_id=1, source_target_pairs={{0,32},{16,48},{32,64},{48,80},{64,96},{80,112},{96,0},{112,16},{1... | collective-permute-start | bytes 393224 | tf_op jit(solution)/shard_map/ppermute | solution.py:220
  114.5 46.3 %copy-start.10 = (bf16[128,16]{0,1:T(8,128)(2,1)S(1)}, bf16[128,16]{0,1:T(8,128)(2,1)}, u32[]{:S(2)}) copy-start(bf16[128,16]{0,1:T(8,128)(2,1)} %param.14) | copy-start | bytes 12292
  114.5 6.4 %collective-permute-start.11 = (bf16[512,128]{1,0:T(8,128)(2,1)S(1)}, bf16[512,128]{1,0:T(8,128)(2,1)S(1)}, u32[]{:S(2)}, u32[]{:S(2)}) collective-permute-start(bf16[512,128]{1,0:T(8,128)(2,1)S(1)} %get-tuple-element.29), channel_id=1, source_target_pairs={{0,96},{16,112},{32,0},{48,16},{64,32},{80,48},{96,64},{112,80},{1... | collective-permute-start | bytes 393224 | tf_op jit(solution)/shard_map/ppermute | solution.py:220
  122.1 7.7 %collective-permute-start.16 = (bf16[1024,128]{1,0:T(8,128)(2,1)S(1)}, bf16[1024,128]{1,0:T(8,128)(2,1)S(1)}, u32[]{:S(2)}, u32[]{:S(2)}) collective-permute-start(bf16[1024,128]{1,0:T(8,128)(2,1)S(1)} %pad_maximum_fusion.3), channel_id=1, source_target_pairs={{0,96},{16,112},{32,0},{48,16},{64,32},{80,48},{96,64},{112,80},{1... | collective-permute-start | bytes 786440 | tf_op jit(solution)/shard_map/ppermute | solution.py:220
  125.9 7.7 %collective-permute-start.14 = (bf16[1024,128]{1,0:T(8,128)(2,1)S(1)}, bf16[1024,128]{1,0:T(8,128)(2,1)S(1)}, u32[]{:S(2)}, u32[]{:S(2)}) collective-permute-start(bf16[1024,128]{1,0:T(8,128)(2,1)S(1)} %pad_maximum_fusion.2), channel_id=1, source_target_pairs={{0,32},{16,48},{32,64},{48,80},{64,96},{80,112},{96,0},{112,16},{1... | collective-permute-start | bytes 786440 | tf_op jit(solution)/shard_map/ppermute | solution.py:220
  126.0 9.5 %collective-permute-start.12 = (bf16[1024,128]{1,0:T(8,128)(2,1)S(1)}, bf16[1024,128]{1,0:T(8,128)(2,1)S(1)}, u32[]{:S(2)}, u32[]{:S(2)}) collective-permute-start(bf16[1024,128]{1,0:T(8,128)(2,1)S(1)} %pad_maximum_fusion.1), channel_id=1, source_target_pairs={{0,96},{16,112},{32,0},{48,16},{64,32},{80,48},{96,64},{112,80},{1... | collective-permute-start | bytes 786440 | tf_op jit(solution)/shard_map/ppermute | solution.py:220
  129.3 7.7 %collective-permute-start.10 = (bf16[1024,128]{1,0:T(8,128)(2,1)S(1)}, bf16[1024,128]{1,0:T(8,128)(2,1)S(1)}, u32[]{:S(2)}, u32[]{:S(2)}) collective-permute-start(bf16[1024,128]{1,0:T(8,128)(2,1)S(1)} %pad_maximum_fusion), channel_id=1, source_target_pairs={{0,32},{16,48},{32,64},{48,80},{64,96},{80,112},{96,0},{112,16},{1... | collective-permute-start | bytes 786440 | tf_op jit(solution)/shard_map/ppermute | solution.py:220
  134.6 8.0 %collective-permute-start.17 = (bf16[1024,128]{1,0:T(8,128)(2,1)S(1)}, bf16[1024,128]{1,0:T(8,128)(2,1)S(1)}, u32[]{:S(2)}, u32[]{:S(2)}) collective-permute-start(bf16[1024,128]{1,0:T(8,128)(2,1)S(1)} %fusion.3), channel_id=1, source_target_pairs={{0,16},{16,0},{32,48},{48,32},{64,80},{80,64},{96,112},{112,96},{1... | collective-permute-start | bytes 786440 | tf_op jit(solution)/shard_map/ppermute | solution.py:224
  156.2 22.6 %copy-start.2 = (bf16[768,768]{1,0:T(8,128)(2,1)S(1)}, bf16[768,768]{1,0:T(8,128)(2,1)}, u32[]{:S(2)}) copy-start(bf16[768,768]{1,0:T(8,128)(2,1)} %wk_ref.3) | copy-start | bytes 3538948
  156.2 22.6 %all-to-all-start.2 = ((bf16[16,3,48,256]{3,2,1,0:T(8,128)(2,1)}), bf16[16,3,48,256]{3,2,1,0:T(8,128)(2,1)}, u32[]{:S(2)}, u32[]{:S(2)}) async-start(bf16[16,3,48,256]{3,2,1,0:T(8,128)(2,1)} %copy-done.7), calls=%async_computation.2 | async-start | bytes 2359296 | tf_op jit(solution)/shard_map/all_to_all | solution.py:267
  178.9 1.3 copy-start.4

commit v2 on v1

v2 whole, which is shorter than its diff:
```python
import math
import functools
import jax, jax.numpy as jnp
from jax import lax
from jax.experimental import pallas as pl
from jax.experimental.pallas import tpu as pltpu
from jax.sharding import PartitionSpec as P

F32 = jnp.float32
BF16 = jnp.bfloat16
LOG2E = 1.4426950408889634
NB = 4
HEADS = 16
WIDTH = 768
HD = 48
TOK = 1024


def prep_body(order_ref, r_ref, q_ref, o_ref, qt_ref, ot_ref, kt_ref, vt_ref, k_ref):
    def piece(slot, first, sample):
        lanes = slice(sample * 64, sample * 64 + 64)
        return jnp.concatenate([r_ref[first, slot, :, lanes], r_ref[first + 1, slot, :, lanes]], axis=1)

    def turned(block):
        return block.astype(F32).T.astype(BF16)

    for u in range(8):
        cols = slice(u * 128, u * 128 + 128)
        other = order_ref[u] * 2
        for b in range(NB):
            qt = piece(0, 2 * u, b)
            qt_ref[b, :, cols] = qt
            q_ref[b, cols, :] = turned(qt)
            ot = piece(3, 2 * u, b)
            ot_ref[b, :, cols] = ot
            o_ref[b, cols, :] = turned(ot)
            kt = piece(1, other, b)
            kt_ref[b, :, cols] = kt
            k_ref[b, cols, :] = turned(kt)
            vt_ref[b, :, cols] = piece(2, other, b)


def prep(order, received):
    nat = jax.ShapeDtypeStruct((NB, TOK, HD), BF16)
    tr = jax.ShapeDtypeStruct((NB, HD, TOK), BF16)
    vm = pl.BlockSpec(memory_space=pltpu.VMEM)
    return pl.pallas_call(
        prep_body,
        out_shape=[nat, nat, tr, tr, tr, tr, nat],
        in_specs=[pl.BlockSpec(memory_space=pltpu.SMEM), vm],
        out_specs=[vm] * 7,
        compiler_params=pltpu.CompilerParams(vmem_limit_bytes=32 * 2**20),
        name="prep",
    )(order, received)


TILE = 256
VMEM_ATT = 40
CHUNKS = 2


def attend_body(scale, steps, chunk, order_ref, *refs):
    first, last = chunk == 0, chunk == CHUNKS - 1
    bias_refs, refs = refs[:5], refs[5:]
    (q_ref, o_ref, qt_ref, ot_ref, kt_ref, vt_ref, k_ref), refs = refs[:7], refs[7:]
    if not first:
        (g_in, dk_in, dv_in), refs = refs[:3], refs[11:]
    dbias_refs, refs = refs[:8], refs[8:]
    g_ref, dkt_ref, dvt_ref, s_ref, dp_ref, p_ref, ds_ref, acc_ref, dqt_ref = refs
    step = pl.program_id(0)

    @pl.when(step == 0)
    def _():
        dkt_ref[...] = jnp.zeros_like(dkt_ref) if first else dk_in[...]
        dvt_ref[...] = jnp.zeros_like(dvt_ref) if first else dv_in[...]

    def products(b):
        s_ref[b % 2] = jnp.dot(q_ref[b], kt_ref[b], preferred_element_type=F32)
        dp_ref[b % 2] = jnp.dot(o_ref[b], vt_ref[b], preferred_element_type=F32)

    def softmax(b):
        group = 16
        for g in range(TILE // group):
            rows = slice(g * group, g * group + group)
            bias = [ref[e, rows, :] for ref in bias_refs[:3] for e in range(2)] + [ref[rows, :] for ref in bias_refs[3:]]
            bias = jnp.concatenate(bias, axis=1)
            s = s_ref[b % 2, rows, :] * (scale * LOG2E) + bias
            m = jnp.max(s, axis=1, keepdims=True)
            e = jnp.exp2(s - m)
            inv = 1.0 / jnp.sum(e, axis=1, keepdims=True)
            p = e * inv
            dp = dp_ref[b % 2, rows, :]
            rd = jnp.sum(p * dp, axis=1, keepdims=True)
            ds = p * (dp - rd)
            p_ref[b % 2, rows, :] = p.astype(BF16)
            ds_ref[b % 2, rows, :] = ds.astype(BF16)
            if b == 0:
                acc_ref[rows, :] = ds
            elif b < NB - 1:
                acc_ref[rows, :] += ds
            else:
                total = (acc_ref[rows, :] + ds).astype(BF16)
                for u in range(8):
                    dbias_refs[u][rows, :] = total[:, u * 128:u * 128 + 128]

    def gradients(b):
        p_low, ds_low = p_ref[b % 2], ds_ref[b % 2]
        dkt_ref[b] += jnp.dot(qt_ref[b], ds_low, preferred_element_type=F32)
        dvt_ref[b] += jnp.dot(ot_ref[b], p_low, preferred_element_type=F32)
        dq = jnp.dot(ds_low, k_ref[b], preferred_element_type=F32)
        dqt_ref[step, b] = (dq * scale).T.astype(BF16)

    products(0)
    for b in range(NB):
        if b + 1 < NB:
            products(b + 1)
        softmax(b)
        if b:
            gradients(b - 1)
    gradients(NB - 1)

    @pl.when(step == steps - 1)
    def _():
        each = TILE // 64
        if not first:
            for t in range(chunk * steps * each):
                g_ref[t, 0] = g_in[t]
        for b in range(NB):
            lanes = slice(b * 64, b * 64 + 64)
            for t in range(steps * each):
                c = (t % each) * 64
                block = dqt_ref[t // each, b, :, c:c + 64]
                if last:
                    g_ref[chunk * steps * each + t, 0, :, lanes] = block
                else:
                    g_ref[t, :, lanes] = block
            if last:
                for u in range(8):
                    one = order_ref[u] * 2
                    dk = (dkt_ref[b, :, u * 128:u * 128 + 128] * scale).astype(BF16)
                    dv = dvt_ref[b, :, u * 128:u * 128 + 128].astype(BF16)
                    g_ref[one, 1, :, lanes] = dk[:, :64]
                    g_ref[one + 1, 1, :, lanes] = dk[:, 64:]
                    g_ref[one, 2, :, lanes] = dv[:, :64]
                    g_ref[one + 1, 2, :, lanes] = dv[:, 64:]


def attend(chunk, order, bias, held, dbias, carried):
    rows = TOK // CHUNKS
    steps = rows // TILE
    at = chunk * steps
    last = chunk == CHUNKS - 1
    scale = 1.0 / math.sqrt(HD)
    nat_t = pl.BlockSpec((NB, TILE, HD), lambda i: (0, i + at, 0))
    tr_t = pl.BlockSpec((NB, HD, TILE), lambda i: (0, 0, i + at))
    tr_w = pl.BlockSpec((NB, HD, TOK), lambda i: (0, 0, 0))
    nat_w = pl.BlockSpec((NB, TOK, HD), lambda i: (0, 0, 0))
    bias_t = [pl.BlockSpec((2, TILE, 128), lambda i: (0, i, 0))] * 3 + [pl.BlockSpec((TILE, 128), lambda i: (i, 0))] * 2
    dbias_t = pl.BlockSpec((TILE, 128), lambda i: (i + at, 0))
    g_spec = pl.BlockSpec((16, 3, HD, 256), lambda i: (0, 0, 0, 0))
    dq_spec = pl.BlockSpec((16 // CHUNKS, HD, 256), lambda i: (0, 0, 0))
    sums = jax.ShapeDtypeStruct((NB, HD, TOK), F32)
    in_specs = [pl.BlockSpec(memory_space=pltpu.SMEM)] + bias_t + [nat_t, nat_t, tr_t, tr_t, tr_w, tr_w, nat_w]
    aliases = {}
    if chunk:
        in_specs += [dq_spec, tr_w, tr_w]
        aliases = {len(in_specs) + u: u for u in range(8)}
        in_specs += [pl.BlockSpec(memory_space=pl.ANY)] * 8
    out_shape, out_specs = [pltpu.HBM((TOK, 128), BF16)] * 8, [dbias_t] * 8
    scratch = [
        pltpu.VMEM((2, TILE, TOK), F32), pltpu.VMEM((2, TILE, TOK), F32),
        pltpu.VMEM((2, TILE, TOK), BF16), pltpu.VMEM((2, TILE, TOK), BF16),
        pltpu.VMEM((TILE, TOK), F32), pltpu.VMEM((steps, NB, HD, TILE), BF16),
    ]
    if last:
        out_shape, out_specs = out_shape + [jax.ShapeDtypeStruct((16, 3, HD, 256), BF16)], out_specs + [g_spec]
        scratch = [pltpu.VMEM((NB, HD, TOK), F32)] * 2 + scratch
    else:
        out_shape = out_shape + [jax.ShapeDtypeStruct((16 // CHUNKS, HD, 256), BF16), sums, sums]
        out_specs = out_specs + [dq_spec, tr_w, tr_w]
    outs = pl.pallas_call(
        functools.partial(attend_body, scale, steps, chunk),
        grid=(steps,),
        out_shape=out_shape, in_specs=in_specs, out_specs=out_specs, scratch_shapes=scratch,
        input_output_aliases=aliases,
        compiler_params=pltpu.CompilerParams(vmem_limit_bytes=VMEM_ATT * 2**20),
        cost_estimate=pl.CostEstimate(flops=10**6, bytes_accessed=2**10, transcendentals=0),
        name="attend_%d" % chunk,
    )(order, *bias, *held, *carried, *dbias)
    return outs[:8], outs[8:]


def block_diagonal(w_ref, count):
    turned = w_ref[...].astype(F32).T
    rows = jnp.broadcast_to(turned[:, None, :], (16, count, 128)).reshape(16 * count, 128)
    at = lax.broadcasted_iota(jnp.int32, (16 * count, 128), 0) % count
    return jnp.concatenate([jnp.where(at == i, rows, 0.0) for i in range(count)], axis=1).astype(BF16)


def bias_body(pair_ref, w_ref, out_ref):
    w = block_diagonal(w_ref, 8)
    for g in range(8):
        cols = jnp.concatenate([pair_ref[g * 8 + r] for r in range(8)], axis=1)
        t = lax.dot_general(w, cols, (((1,), (1,)), ((), ())), preferred_element_type=F32)
        t = t * LOG2E
        for h in range(16):
            block = t[h * 8:h * 8 + 8, :]
            out_ref[h, g * 8:g * 8 + 8, :] = block
            out_ref[h + 16, g * 8:g * 8 + 8, :] = block


def bias_part(pair, w_pair):
    vm = pl.BlockSpec(memory_space=pltpu.VMEM)
    return pl.pallas_call(
        bias_body, out_shape=jax.ShapeDtypeStruct((32, 64, 128), F32),
        in_specs=[vm, vm], out_specs=vm,
        compiler_params=pltpu.CompilerParams(vmem_limit_bytes=32 * 2**20), name="bias_part",
    )(pair, w_pair)


def gpair_body(x_ref, w_ref, out_ref):
    w = block_diagonal(w_ref, 16)
    for g in range(4):
        rows = slice(g * 16, g * 16 + 16)
        x = (x_ref[0, :, rows, :].astype(F32) + x_ref[1, :, rows, :].astype(F32)).astype(BF16).reshape(256, 128)
        t = lax.dot_general(x, w, (((0,), (0,)), ((), ())), preferred_element_type=F32)
        for r in range(16):
            out_ref[g * 16 + r] = t[:, r * 128:r * 128 + 128].astype(BF16)


def gpair(x, w_pair):
    vm = pl.BlockSpec(memory_space=pltpu.VMEM)
    return pl.pallas_call(
        gpair_body, out_shape=jax.ShapeDtypeStruct((64, 128, 128), BF16),
        in_specs=[vm, vm], out_specs=vm,
        compiler_params=pltpu.CompilerParams(vmem_limit_bytes=32 * 2**20), name="gpair",
    )(x, w_pair)


def project_body(x_ref, c_ref, wq_ref, wk_ref, wv_ref, wo_ref, out_ref):
    x = x_ref[...].reshape(NB * 64, WIDTH)
    c = c_ref[...].reshape(NB * 64, WIDTH)
    for slot, w_ref in enumerate((wq_ref, wk_ref, wv_ref)):
        t = jnp.dot(x, w_ref[...], preferred_element_type=F32).T.astype(BF16)
        for h in range(HEADS):
            out_ref[h, slot] = t[h * HD:h * HD + HD, :]
    t = lax.dot_general(wo_ref[...], c, (((1,), (1,)), ((), ())), preferred_element_type=F32).astype(BF16)
    for h in range(HEADS):
        out_ref[h, 3] = t[h * HD:h * HD + HD, :]


def project(single, cotangent, w_query, w_key, w_value, w_out):
    vm = pl.BlockSpec(memory_space=pltpu.VMEM)
    return pl.pallas_call(
        project_body, out_shape=jax.ShapeDtypeStruct((HEADS, 4, HD, NB * 64), BF16),
        in_specs=[vm] * 6, out_specs=vm,
        compiler_params=pltpu.CompilerParams(vmem_limit_bytes=40 * 2**20), name="project",
    )(single, cotangent, w_query, w_key, w_value, w_out)


def final_body(g_ref, wq_ref, wk_ref, wv_ref, out_ref):
    total = None
    for slot, w_ref in enumerate((wq_ref, wk_ref, wv_ref)):
        part = jnp.dot(w_ref[...], g_ref[:, slot].reshape(WIDTH, NB * 64), preferred_element_type=F32)
        total = part if total is None else total + part
    out_ref[...] = total.T.astype(BF16).reshape(NB, 64, WIDTH)


def final(g, w_query, w_key, w_value):
    vm = pl.BlockSpec(memory_space=pltpu.VMEM)
    return pl.pallas_call(
        final_body, out_shape=jax.ShapeDtypeStruct((NB, 64, WIDTH), BF16),
        in_specs=[vm] * 4, out_specs=vm,
        compiler_params=pltpu.CompilerParams(vmem_limit_bytes=40 * 2**20), name="final",
    )(g, w_query, w_key, w_value)


def shift_y(x, d):
    return lax.ppermute(x, "sample", [(i, ((i // 2 + d) % 4) * 2 + i % 2) for i in range(8)])


def exchange(x):
    groups = [[(2 * y + e) * 16 + t for e in range(2) for t in range(16)] for y in range(4)]
    return lax.all_to_all(x, ("sample", "tok"), 0, 0, axis_index_groups=groups)


def gather_blocks(own, after):
    if after is not None:
        own = lax.optimization_barrier((own, after))[0]
    up, down = shift_y(own, 1), shift_y(own, -1)
    return [own, up, down, shift_y(up[0], 1), shift_y(down[1], -1)]


def key_order():
    y = lax.axis_index("sample") // 2
    return jnp.stack([((y + d) % 4) * 2 + e for d in (0, 3, 1, 2) for e in (0, 1)]).astype(jnp.int32)


def plus(*terms):
    total = terms[0].astype(F32)
    for term in terms[1:]:
        total = total + term.astype(F32)
    return total.astype(BF16)


def scatter_blocks(blocks):
    own0, own1, down0, down1, up0, up1, far0, far1 = blocks
    far0, far1 = shift_y(far0, 1), shift_y(far1, -1)
    up1, down0 = shift_y(up1, 1), shift_y(down0, -1)
    up0, down1 = shift_y(plus(up0, far0), 1), shift_y(plus(down1, far1), -1)
    return own_sum(own0, up0, down0, own1, up1, down1)


def own_sum_body(a0, b0, c0, a1, b1, c1, out_ref):
    out_ref[0] = plus(a0[...], b0[...], c0[...])
    out_ref[1] = plus(a1[...], b1[...], c1[...])


def own_sum(*terms):
    vm = pl.BlockSpec(memory_space=pltpu.VMEM)
    return pl.pallas_call(
        own_sum_body, out_shape=jax.ShapeDtypeStruct((2, TOK, 128), BF16), in_specs=[vm] * 6, out_specs=vm,
        compiler_params=pltpu.CompilerParams(vmem_limit_bytes=16 * 2**20), name="own_sum",
    )(*terms)


def local(single, pair, w_query, w_key, w_value, w_out, w_pair, cotangent):
    order = key_order()
    sent = project(single, cotangent, w_query, w_key, w_value, w_out)
    bias = exchange(bias_part(pair, w_pair)).reshape(2, TOK, 128)
    bias, sent = lax.optimization_barrier((bias, sent))
    received = lax.all_to_all(sent, "tok", 0, 0)
    held = prep(order, received)
    dbias, carried, blocks, rows = (), (), None, TOK // CHUNKS
    for c in range(CHUNKS):
        blocks = gather_blocks(bias[:, c * rows:c * rows + rows], blocks[1] if blocks else None)
        dbias, carried = attend(c, order, blocks, held, dbias, carried)
    grads = lax.all_to_all(carried[0], "tok", 0, 0)
    dbias = scatter_blocks(dbias)
    grads, dbias = lax.optimization_barrier((grads, dbias))
    grad_single = final(grads, w_query, w_key, w_value)
    dbias = exchange(dbias.reshape(32, 64, 128)).reshape(2, 16, 64, 128)
    return (grad_single, gpair(dbias, w_pair))


def solution(mesh):
    rows, keys = P("sample", "tok", None), P("tok", "sample", None)
    return jax.shard_map(
        local, mesh=mesh, in_specs=(rows, keys, P(), P(), P(), P(), P(), rows),
        out_specs=(rows, keys), check_vma=False,
    )
```

time: 185 us -> 139 us (0.75)
  waiting for transfers between devices: 65.7 us -> 46.4 us
  blocking collectives: 12.6 us -> 0 us
  other arithmetic: 7.27 us -> 0.14 us
  local copies, waits for them, and re-layouts: 21.4 us -> 15.8 us
    ppermute x2 -> x0, waiting for transfers between devices: 33.2 us -> none  [swap_x(): return lax.ppermute(x, 'sample', [(i, i ^ 1) for i in range(8)])]
    ppermute x16 -> x14, waiting for transfers between devices: 11.2 us -> 27.2 us  [shift_y(): lax.ppermute(x, 'sample', [(i, (i // 2 + d) % 4 * 2 + i % 2) for i in ran...]
    all_to_all x1 -> x0, blocking collectives: 12.6 us -> none  [local(): grad_pair = gpair(lax.all_to_all(dbias, 'tok', 0, 0), w_pair)]
    all_to_all x3 -> x4, starting transfers between devices: 14.7 us -> 22.5 us  [the longest x2 14.3 us: exchange(): return lax.all_to_all(x, ('sample', 'tok'), 0, 0, axis_index_groups=groups)]
    unnamed x29 -> x47, local copies, waits for them, and re-layouts: 15.9 us -> 8.88 us
    ppermute x16 -> x14, starting transfers between devices: 25.3 us -> 20.1 us  [shift_y(): lax.ppermute(x, 'sample', [(i, (i // 2 + d) % 4 * 2 + i % 2) for i in ran...]
    squeeze x0 -> x4, local copies, waits for them, and re-layouts: none -> 4.78 us  [gather_blocks(): return [own, up, down, shift_y(up[0], 1), shift_y(down[1], -1)]]
    ppermute x2 -> x0, starting transfers between devices: 3.7 us -> none  [swap_x(): return lax.ppermute(x, 'sample', [(i, i ^ 1) for i in range(8)])]
  transfers between devices with their start and end apart: 21 -> 18, of which waited for: 11 -> 8; matrix products, arithmetic and copies ran while one was open for 9% -> 4% of each run, Pallas kernels for 4% -> 14%
where the time goes in v2:
time: 139 us; the launch traced here: 138 us
  waiting for transfers between devices  46.4 us (33%)
  starting transfers between devices  42.7 us (31%)
  Pallas kernels  31.7 us (23%)
  local copies, waits for them, and re-layouts  15.8 us (11%)
    ppermute x14, waiting for transfers between devices, shift_y(): lax.ppermute(x, 'sample', [(i, (i // 2 + d) % 4 * 2 + i % 2) for i in ran...  27.2 us
    ppermute x14, starting transfers between devices, shift_y(): lax.ppermute(x, 'sample', [(i, (i // 2 + d) % 4 * 2 + i % 2) for i in ran...  20.1 us
    pallas_call x2, Pallas kernels, attend(): pl.pallas_call(functools.partial(attend_body, scale, steps, chunk), grid=...  19.3 us
    all_to_all x2, waiting for transfers between devices, exchange(): return lax.all_to_all(x, ('sample', 'tok'), 0, 0, axis_index_groups=groups)  19.2 us
    all_to_all x2, starting transfers between devices, exchange(): return lax.all_to_all(x, ('sample', 'tok'), 0, 0, axis_index_groups=groups)  14.3 us
    unnamed x47, local copies, waits for them, and re-layouts  8.88 us
    squeeze x4, local copies, waits for them, and re-layouts, gather_blocks(): return [own, up, down, shift_y(up[0], 1), shift_y(down[1], -1)]  4.78 us
    all_to_all x1, starting transfers between devices, local(): grads = lax.all_to_all(carried[0], 'tok', 0, 0)  4.53 us
  transfers between devices with their start and end apart: 18, of which 8 were waited for; matrix products, arithmetic and copies ran while one was open for 4% of the time, Pallas kernels for 14%

profile of v2, /device:TPU:0, one launch (start us, length us, event | category | flops | bytes accessed | tf_op | source)
XLA Modules:
  0.0 137.7 jit_solution(2882749381093360089)
XLA Ops:
  0.6 0.8 copy.18.w_ref
  1.4 1.6 %copy-done.6 = bf16[64,128,128]{2,1,0:T(8,128)(2,1)S(1)} copy-done((bf16[64,128,128]{2,1,0:T(8,128)(2,1)S(1)}, bf16[64,128,128]{2,1,0:T(8,128)(2,1)}, u32[]{:S(2)}) %copy-start.6) | copy-done | bytes 2097176
  3.0 0.7 bias_part.1
  3.8 1.0 copy-done.5
  4.8 8.5 %all-to-all-start = ((f32[32,64,128]{2,1,0:T(8,128)}), f32[32,64,128]{2,1,0:T(8,128)}, u32[]{:S(2)}, u32[]{:S(2)}) async-start(f32[32,64,128]{2,1,0:T(8,128)} %copy-done.5), calls=%async_computation | async-start | bytes 2097152 | tf_op jit(solution)/shard_map/all_to_all | solution.py:284
  13.4 1.3 copy-done.3
  14.6 1.3 copy-done.8
  15.9 2.5 %project.1 = bf16[16,4,48,256]{3,2,1,0:T(8,128)(2,1)} custom-call(bf16[4,64,768]{2,1,0:T(8,128)(2,1)S(1)} %copy-done.15, bf16[4,64,768]{2,1,0:T(8,128)(2,1)S(1)} %copy-done.16, bf16[768,768]{1,0:T(8,128)(2,1)S(1)} %copy-done, bf16[768,768]{1,0:T(8,128)(2,1)S(1)} %copy-done.1, bf16[768,768]{1,0:T(8,128)(2,1)S(1)} %copy-done.3, bf16[768,768]{1,0:T(8,128)(2,1)S(1)} %copy-done.8), custom_call_target="tpu_custom_call" | custom-call | tf_op jit(solution)/shard_map/project/pallas_call | solution.py:254
  18.4 11.7 %all-to-all-done = f32[32,64,128]{2,1,0:T(8,128)} async-done(((f32[32,64,128]{2,1,0:T(8,128)}), f32[32,64,128]{2,1,0:T(8,128)}, u32[]{:S(2)}, u32[]{:S(2)}) %all-to-all-start) | async-done | bytes 1048608 | tf_op jit(solution)/shard_map/all_to_all | solution.py:284
  30.2 2.1 %fusion = (f32[2,512,128]{2,1,0:T(8,128)S(1)}, f32[2,512,128]{2,1,0:T(8,128)}) fusion(f32[2,1024,128]{2,1,0:T(8,128)} %bitcast.8), kind=kLoop, calls=%fused_computation.6 | loop fusion | bytes 2097152 | tf_op jit(solution)/shard_map/slice | solution.py:336
  32.3 1.6 %collective-permute-start = (f32[2,512,128]{2,1,0:T(8,128)S(1)}, f32[2,512,128]{2,1,0:T(8,128)}, u32[]{:S(2)}, u32[]{:S(2)}) collective-permute-start(f32[2,512,128]{2,1,0:T(8,128)S(1)} %get-tuple-element.66.refs_0_), channel_id=1, source_target_pairs={{0,32},{16,48},{32,64},{48,80},{64,96},{80,112},{96,0},{112,16},{1... | collective-permute-start | bytes 1572872 | tf_op jit(solution)/shard_map/ppermute | solution.py:279
  33.8 1.7 %collective-permute-start.5 = (f32[2,512,128]{2,1,0:T(8,128)S(1)}, f32[2,512,128]{2,1,0:T(8,128)}, u32[]{:S(2)}, u32[]{:S(2)}) collective-permute-start(f32[2,512,128]{2,1,0:T(8,128)S(1)} %get-tuple-element.66.refs_0_), channel_id=1, source_target_pairs={{0,96},{16,112},{32,0},{48,16},{64,32},{80,48},{96,64},{112,80},{1... | collective-permute-start | bytes 1572872 | tf_op jit(solution)/shard_map/ppermute | solution.py:279
  35.5 3.7 %all-to-all-start.1 = ((bf16[16,4,48,256]{3,2,1,0:T(8,128)(2,1)}), bf16[16,4,48,256]{3,2,1,0:T(8,128)(2,1)S(1)}, u32[]{:S(2)}, u32[]{:S(2)}) async-start(bf16[16,4,48,256]{3,2,1,0:T(8,128)(2,1)} %project.1), calls=%async_computation.1 | async-start | bytes 3145728 | tf_op jit(solution)/shard_map/all_to_all | solution.py:332
  39.2 8.4 %collective-permute-done.refs_1_ = f32[2,512,128]{2,1,0:T(8,128)} collective-permute-done((f32[2,512,128]{2,1,0:T(8,128)S(1)}, f32[2,512,128]{2,1,0:T(8,128)}, u32[]{:S(2)}, u32[]{:S(2)}) %collective-permute-start) | collective-permute-done | bytes 524320 | tf_op jit(solution)/shard_map/ppermute | solution.py:279
  47.6 1.7 %collective-permute-start.2 = (f32[2,512,128]{2,1,0:T(8,128)}, f32[2,512,128]{2,1,0:T(8,128)S(1)}, u32[]{:S(2)}, u32[]{:S(2)}) collective-permute-start(f32[2,512,128]{2,1,0:T(8,128)} %get-tuple-element.35.refs_0_), channel_id=1, source_target_pairs={{0,96},{16,112},{32,0},{48,16},{64,32},{80,48},{96,64},{112,80},{1... | collective-permute-start | bytes 1572872 | tf_op jit(solution)/shard_map/ppermute | solution.py:279
  49.3 0.3 collective-permute-start.1
  49.6 1.7 %slice_bitcast_fusion = f32[512,128]{1,0:T(8,128)} fusion(f32[2,512,128]{2,1,0:T(8,128)} %collective-permute-done.5.refs_2_), kind=kLoop, calls=%fused_computation.2 | loop fusion | bytes 524288 | tf_op jit(solution)/shard_map/squeeze | solution.py:291
  51.3 3.0 %collective-permute-start.7 = (f32[512,128]{1,0:T(8,128)}, f32[512,128]{1,0:T(8,128)}, u32[]{:S(2)}, u32[]{:S(2)}) collective-permute-start(f32[512,128]{1,0:T(8,128)} %slice_bitcast_fusion), channel_id=1, source_target_pairs={{0,96},{16,112},{32,0},{48,16},{64,32},{80,48},{96,64},{112,80},{1... | collective-permute-start | bytes 786440 | tf_op jit(solution)/shard_map/ppermute | solution.py:279
  54.3 1.7 %slice_bitcast_fusion.1 = f32[512,128]{1,0:T(8,128)} fusion(f32[2,512,128]{2,1,0:T(8,128)} %collective-permute-done.refs_1_), kind=kLoop, calls=%fused_computation.3 | loop fusion | bytes 524288 | tf_op jit(solution)/shard_map/squeeze | solution.py:291
  55.9 6.7 %collective-permute-done.2.refs_2_ = f32[2,512,128]{2,1,0:T(8,128)S(1)} collective-permute-done((f32[2,512,128]{2,1,0:T(8,128)}, f32[2,512,128]{2,1,0:T(8,128)S(1)}, u32[]{:S(2)}, u32[]{:S(2)}) %collective-permute-start.2) | collective-permute-done | bytes 524320 | tf_op jit(solution)/shard_map/ppermute | solution.py:279
  62.7 0.7 slice_bitcast_fusion.2
  63.4 0.8 copy-done.9
  64.2 3.0 %collective-permute-start.4 = (f32[512,128]{1,0:T(8,128)}, f32[512,128]{1,0:T(8,128)}, u32[]{:S(2)}, u32[]{:S(2)}) collective-permute-start(f32[512,128]{1,0:T(8,128)} %slice_bitcast_fusion.2), channel_id=1, source_target_pairs={{0,96},{16,112},{32,0},{48,16},{64,32},{80,48},{96,64},{112,80},{1... | collective-permute-start | bytes 786440 | tf_op jit(solution)/shard_map/ppermute | solution.py:279
  67.2 0.7 slice_bitcast_fusion.3
  67.9 0.8 copy-done.11
  68.7 0.1 stack.35.order_ref
  68.8 2.8 %prep.1 = (bf16[4,1024,48]{2,1,0:T(8,128)(2,1)S(1)}, bf16[4,1024,48]{2,1,0:T(8,128)(2,1)S(1)}, bf16[4,48,1024]{2,1,0:T(8,128)(2,1)S(1)}, bf16[4,48,1024]{2,1,0:T...) custom-call(s32[8]{0:T(128)S(1)} %stack.35.order_ref, ...), custom_call_target="tpu_custom_call" | custom-call | tf_op jit(solution)/shard_map/prep/pallas_call | solution.py:47
  71.7 9.3 %attend_0.1 = (bf16[1024,128]{1,0:T(8,128)(2,1)}, bf16[1024,128]{1,0:T(8,128)(2,1)}, bf16[1024,128]{1,0:T(8,128)(2,1)}, bf16[1024,128]{1,0:T(8,128)(2,1)}, bf16[...) custom-call(s32[8]{0:T(128)S(1)} %stack.35.order_ref, ...), custom_call_target="tpu_custom_call" | custom-call | flops 1000000 | bytes 1024 | tf_op jit(solution)/shard_map/attend_0/pallas_call | solution.py:181
  81.0 10.0 %attend_1.1 = (bf16[1024,128]{1,0:T(8,128)(2,1)}, bf16[1024,128]{1,0:T(8,128)(2,1)}, bf16[1024,128]{1,0:T(8,128)(2,1)}, bf16[1024,128]{1,0:T(8,128)(2,1)}, bf16[...) custom-call(s32[8]{0:T(128)S(1)} %stack.35.order_ref, ...), custom_call_target="tpu_custom_call", output_to_operand_aliasing={{0}: (16, {}), {1}: (17, {}), {2}: (18, {}), {3}: (19, {}),... | custom-call | flops 1000000 | bytes 1024 | tf_op jit(solution)/shard_map/attend_1/pallas_call | solution.py:181
  91.1 4.5 %all-to-all-start.2 = ((bf16[16,3,48,256]{3,2,1,0:T(8,128)(2,1)}), bf16[16,3,48,256]{3,2,1,0:T(8,128)(2,1)}, u32[]{:S(2)}, u32[]{:S(2)}) async-start(bf16[16,3,48,256]{3,2,1,0:T(8,128)(2,1)} %get-tuple-element.55), calls=%async_computation.2 | async-start | bytes 2359296 | tf_op jit(solution)/shard_map/all_to_all | solution.py:338
  95.7 0.1 collective-permute-start.8
  95.8 3.3 %collective-permute-start.12 = (bf16[1024,128]{1,0:T(8,128)(2,1)S(1)}, bf16[1024,128]{1,0:T(8,128)(2,1)S(1)}, u32[]{:S(2)}, u32[]{:S(2)}) collective-permute-start(bf16[1024,128]{1,0:T(8,128)(2,1)S(1)} %copy-done.22), channel_id=1, source_target_pairs={{0,96},{16,112},{32,0},{48,16},{64,32},{80,48},{96,64},{112,80},{1... | collective-permute-start | bytes 786440 | tf_op jit(solution)/shard_map/ppermute | solution.py:279
  99.1 1.9 %collective-permute-start.10 = (bf16[1024,128]{1,0:T(8,128)(2,1)S(1)}, bf16[1024,128]{1,0:T(8,128)(2,1)S(1)}, u32[]{:S(2)}, u32[]{:S(2)}) collective-permute-start(bf16[1024,128]{1,0:T(8,128)(2,1)S(1)} %copy-done.19), channel_id=1, source_target_pairs={{0,96},{16,112},{32,0},{48,16},{64,32},{80,48},{96,64},{112,80},{1... | collective-permute-start | bytes 786440 | tf_op jit(solution)/shard_map/ppermute | solution.py:279
  101.0 0.1 collective-permute-start.11
  101.1 5.0 %collective-permute-done.8 = bf16[1024,128]{1,0:T(8,128)(2,1)S(1)} collective-permute-done((bf16[1024,128]{1,0:T(8,128)(2,1)S(1)}, bf16[1024,128]{1,0:T(8,128)(2,1)S(1)}, u32[]{:S(2)}, u32[]{:S(2)}) %collective-permute-start.8) | collective-permute-done | bytes 262176 | tf_op jit(solution)/shard_map/ppermute | solution.py:279
  106.0 0.1 add_convert_fusion.1
  106.1 0.3 collective-permute-start.9
  106.4 0.1 add_convert_fusion
  106.5 3.3 %collective-permute-start.13 = (bf16[1024,128]{1,0:T(8,128)(2,1)S(1)}, bf16[1024,128]{1,0:T(8,128)(2,1)S(1)}, u32[]{:S(2)}, u32[]{:S(2)}) collective-permute-start(bf16[1024,128]{1,0:T(8,128)(2,1)S(1)} %add_convert_fusion), channel_id=1, source_target_pairs={{0,96},{16,112},{32,0},{48,16},{64,32},{80,48},{96,64},{112,80},{1... | collective-permute-start | bytes 786440 | tf_op jit(solution)/shard_map/ppermute | solution.py:279
  109.8 1.5 %collective-permute-done.10.c0 = bf16[1024,128]{1,0:T(8,128)(2,1)S(1)} collective-permute-done((bf16[1024,128]{1,0:T(8,128)(2,1)S(1)}, bf16[1024,128]{1,0:T(8,128)(2,1)S(1)}, u32[]{:S(2)}, u32[]{:S(2)}) %collective-permute-start.10) | collective-permute-done | bytes 262176 | tf_op jit(solution)/shard_map/ppermute | solution.py:279
  111.3 0.3 collective-permute-done.11.b1
  111.7 5.2 %collective-permute-done.9.b0 = bf16[1024,128]{1,0:T(8,128)(2,1)S(1)} collective-permute-done((bf16[1024,128]{1,0:T(8,128)(2,1)S(1)}, bf16[1024,128]{1,0:T(8,128)(2,1)S(1)}, u32[]{:S(2)}, u32[]{:S(2)}) %collective-permute-start.9) | collective-permute-done | bytes 262176 | tf_op jit(solution)/shard_map/ppermute | solution.py:279
  116.9 1.0 own_sum.1
  117.9 5.8 %all-to-all-start.3 = ((bf16[32,64,128]{2,1,0:T(8,128)(2,1)}), bf16[32,64,128]{2,1,0:T(8,128)(2,1)S(1)}, u32[]{:S(2)}, u32[]{:S(2)}) async-start(bf16[32,64,128]{2,1,0:T(8,128)(2,1)} %bitcast.13), calls=%async_computation.3 | async-start | bytes 1048576 | tf_op jit(solution)/shard_map/all_to_all | solution.py:284
  123.7 1.3 copy-done.4
  125.0 3.2 %final.1 = bf16[4,64,768]{2,1,0:T(8,128)(2,1)} custom-call(bf16[16,3,48,256]{3,2,1,0:T(8,128)(2,1)} %all-to-all-done.2.g_ref, bf16[768,768]{1,0:T(8,128)(2,1)S(1)} %copy-done, bf16[768,768]{1,0:T(8,128)(2,1)S(1)} %copy-done.2, bf16[768,768]{1,0:T(8,128)(2,1)S(1)} %copy-done.4), custom_call_target="tpu_custom_call" | custom-call | tf_op jit(solution)/shard_map/final/pallas_call | solution.py:271
  128.2 7.4 %all-to-all-done.3 = bf16[32,64,128]{2,1,0:T(8,128)(2,1)S(1)} async-done(((bf16[32,64,128]{2,1,0:T(8,128)(2,1)}), bf16[32,64,128]{2,1,0:T(8,128)(2,1)S(1)}, u32[]{:S(2)}, u32[]{:S(2)}) %all-to-all-start.3) | async-done | bytes 524320 | tf_op jit(solution)/shard_map/all_to_all | solution.py:284
  135.6 2.1 %gpair.1 = bf16[64,128,128]{2,1,0:T(8,128)(2,1)} custom-call(bf16[2,16,64,128]{3,2,1,0:T(8,128)(2,1)S(1)} %bitcast.19, bf16[128,16]{1,0:T(8,128)(2,1)S(1)} %copy.18.w_ref), custom_call_target="tpu_custom_call" | custom-call | tf_op jit(solution)/shard_map/gpair/pallas_call | solution.py:233
  (51 shorter events, 0.1 us)
Async XLA Ops:
  1.4 1.6 %copy-start.6 = (bf16[64,128,128]{2,1,0:T(8,128)(2,1)S(1)}, bf16[64,128,128]{2,1,0:T(8,128)(2,1)}, u32[]{:S(2)}) copy-start(bf16[64,128,128]{2,1,0:T(8,128)(2,1)} %pair_ref.1) | copy-start | bytes 6291460
  3.0 10.3 %copy-start.1 = (bf16[768,768]{1,0:T(8,128)(2,1)S(1)}, bf16[768,768]{1,0:T(8,128)(2,1)}, u32[]{:S(2)}) copy-start(bf16[768,768]{1,0:T(8,128)(2,1)} %wk_ref.3) | copy-start | bytes 3538948
  3.8 1.0 copy-start.5
  4.8 8.5 %copy-start = (bf16[768,768]{1,0:T(8,128)(2,1)S(1)}, bf16[768,768]{1,0:T(8,128)(2,1)}, u32[]{:S(2)}) copy-start(bf16[768,768]{1,0:T(8,128)(2,1)} %wq_ref.3) | copy-start | bytes 3538948
  4.8 8.5 %copy-start.15 = (bf16[4,64,768]{2,1,0:T(8,128)(2,1)S(1)}, bf16[4,64,768]{2,1,0:T(8,128)(2,1)}, u32[]{:S(2)}) copy-start(bf16[4,64,768]{2,1,0:T(8,128)(2,1)} %x_ref.1) | copy-start | bytes 1179652
  4.8 8.5 %copy-start.16 = (bf16[4,64,768]{2,1,0:T(8,128)(2,1)S(1)}, bf16[4,64,768]{2,1,0:T(8,128)(2,1)}, u32[]{:S(2)}) copy-start(bf16[4,64,768]{2,1,0:T(8,128)(2,1)} %c_ref.1) | copy-start | bytes 1179652
  4.8 25.4 %all-to-all-start = ((f32[32,64,128]{2,1,0:T(8,128)}), f32[32,64,128]{2,1,0:T(8,128)}, u32[]{:S(2)}, u32[]{:S(2)}) async-start(f32[32,64,128]{2,1,0:T(8,128)} %copy-done.5), calls=%async_computation | async-start | bytes 2097152 | tf_op jit(solution)/shard_map/all_to_all | solution.py:284
  13.3 1.3 copy-start.3
  14.6 1.3 copy-start.8
  32.3 15.3 %collective-permute-start = (f32[2,512,128]{2,1,0:T(8,128)S(1)}, f32[2,512,128]{2,1,0:T(8,128)}, u32[]{:S(2)}, u32[]{:S(2)}) collective-permute-start(f32[2,512,128]{2,1,0:T(8,128)S(1)} %get-tuple-element.66.refs_0_), channel_id=1, source_target_pairs={{0,32},{16,48},{32,64},{48,80},{64,96},{80,112},{96,0},{112,16},{1... | collective-permute-start | bytes 1572872 | tf_op jit(solution)/shard_map/ppermute | solution.py:279
  33.8 15.8 %collective-permute-start.5 = (f32[2,512,128]{2,1,0:T(8,128)S(1)}, f32[2,512,128]{2,1,0:T(8,128)}, u32[]{:S(2)}, u32[]{:S(2)}) collective-permute-start(f32[2,512,128]{2,1,0:T(8,128)S(1)} %get-tuple-element.66.refs_0_), channel_id=1, source_target_pairs={{0,96},{16,112},{32,0},{48,16},{64,32},{80,48},{96,64},{112,80},{1... | collective-permute-start | bytes 1572872 | tf_op jit(solution)/shard_map/ppermute | solution.py:279
  35.5 33.3 %all-to-all-start.1 = ((bf16[16,4,48,256]{3,2,1,0:T(8,128)(2,1)}), bf16[16,4,48,256]{3,2,1,0:T(8,128)(2,1)S(1)}, u32[]{:S(2)}, u32[]{:S(2)}) async-start(bf16[16,4,48,256]{3,2,1,0:T(8,128)(2,1)} %project.1), calls=%async_computation.1 | async-start | bytes 3145728 | tf_op jit(solution)/shard_map/all_to_all | solution.py:332
  47.6 15.1 %collective-permute-start.2 = (f32[2,512,128]{2,1,0:T(8,128)}, f32[2,512,128]{2,1,0:T(8,128)S(1)}, u32[]{:S(2)}, u32[]{:S(2)}) collective-permute-start(f32[2,512,128]{2,1,0:T(8,128)} %get-tuple-element.35.refs_0_), channel_id=1, source_target_pairs={{0,96},{16,112},{32,0},{48,16},{64,32},{80,48},{96,64},{112,80},{1... | collective-permute-start | bytes 1572872 | tf_op jit(solution)/shard_map/ppermute | solution.py:279
  49.3 17.8 %collective-permute-start.1 = (f32[2,512,128]{2,1,0:T(8,128)}, f32[2,512,128]{2,1,0:T(8,128)S(1)}, u32[]{:S(2)}, u32[]{:S(2)}) collective-permute-start(f32[2,512,128]{2,1,0:T(8,128)} %get-tuple-element.35.refs_0_), channel_id=1, source_target_pairs={{0,32},{16,48},{32,64},{48,80},{64,96},{80,112},{96,0},{112,16},{1... | collective-permute-start | bytes 1572872 | tf_op jit(solution)/shard_map/ppermute | solution.py:279
  51.3 20.3 %collective-permute-start.7 = (f32[512,128]{1,0:T(8,128)}, f32[512,128]{1,0:T(8,128)}, u32[]{:S(2)}, u32[]{:S(2)}) collective-permute-start(f32[512,128]{1,0:T(8,128)} %slice_bitcast_fusion), channel_id=1, source_target_pairs={{0,96},{16,112},{32,0},{48,16},{64,32},{80,48},{96,64},{112,80},{1... | collective-permute-start | bytes 786440 | tf_op jit(solution)/shard_map/ppermute | solution.py:279
  55.9 15.7 %collective-permute-start.6 = (f32[512,128]{1,0:T(8,128)}, f32[512,128]{1,0:T(8,128)}, u32[]{:S(2)}, u32[]{:S(2)}) collective-permute-start(f32[512,128]{1,0:T(8,128)} %slice_bitcast_fusion.1), channel_id=1, source_target_pairs={{0,32},{16,48},{32,64},{48,80},{64,96},{80,112},{96,0},{112,16},{1... | collective-permute-start | bytes 786440 | tf_op jit(solution)/shard_map/ppermute | solution.py:279
  63.4 0.8 copy-start.9
  64.2 16.8 %collective-permute-start.4 = (f32[512,128]{1,0:T(8,128)}, f32[512,128]{1,0:T(8,128)}, u32[]{:S(2)}, u32[]{:S(2)}) collective-permute-start(f32[512,128]{1,0:T(8,128)} %slice_bitcast_fusion.2), channel_id=1, source_target_pairs={{0,96},{16,112},{32,0},{48,16},{64,32},{80,48},{96,64},{112,80},{1... | collective-permute-start | bytes 786440 | tf_op jit(solution)/shard_map/ppermute | solution.py:279
  67.9 0.8 copy-start.11
  68.7 12.3 %collective-permute-start.3 = (f32[512,128]{1,0:T(8,128)}, f32[512,128]{1,0:T(8,128)}, u32[]{:S(2)}, u32[]{:S(2)}) collective-permute-start(f32[512,128]{1,0:T(8,128)} %slice_bitcast_fusion.3), channel_id=1, source_target_pairs={{0,32},{16,48},{32,64},{48,80},{64,96},{80,112},{96,0},{112,16},{1... | collective-permute-start | bytes 786440 | tf_op jit(solution)/shard_map/ppermute | solution.py:279
  71.6 9.4 %copy-start.7 = (f32[2,512,128]{2,1,0:T(8,128)S(1)}, f32[2,512,128]{2,1,0:T(8,128)}, u32[]{:S(2)}) copy-start(f32[2,512,128]{2,1,0:T(8,128)} %get-tuple-element.35.refs_0_) | copy-start | bytes 1572868
  71.6 9.4 %copy-start.10 = (f32[2,512,128]{2,1,0:T(8,128)S(1)}, f32[2,512,128]{2,1,0:T(8,128)}, u32[]{:S(2)}) copy-start(f32[2,512,128]{2,1,0:T(8,128)} %copy-done.9) | copy-start | bytes 1572868
  71.6 9.4 %copy-start.12 = (f32[2,512,128]{2,1,0:T(8,128)S(1)}, f32[2,512,128]{2,1,0:T(8,128)}, u32[]{:S(2)}) copy-start(f32[2,512,128]{2,1,0:T(8,128)} %copy-done.11) | copy-start | bytes 1572868
  91.0 4.6 %copy-start.21 = (bf16[1024,128]{1,0:T(8,128)(2,1)S(1)}, bf16[1024,128]{1,0:T(8,128)(2,1)}, u32[]{:S(2)}) copy-start(bf16[1024,128]{1,0:T(8,128)(2,1)} %get-tuple-element.58) | copy-start | bytes 786436
  91.0 4.7 %copy-start.22 = (bf16[1024,128]{1,0:T(8,128)(2,1)S(1)}, bf16[1024,128]{1,0:T(8,128)(2,1)}, u32[]{:S(2)}) copy-start(bf16[1024,128]{1,0:T(8,128)(2,1)} %get-tuple-element.63) | copy-start | bytes 786436
  91.1 8.0 %copy-start.19 = (bf16[1024,128]{1,0:T(8,128)(2,1)S(1)}, bf16[1024,128]{1,0:T(8,128)(2,1)}, u32[]{:S(2)}) copy-start(bf16[1024,128]{1,0:T(8,128)(2,1)} %get-tuple-element.59) | copy-start | bytes 786436
  91.1 9.9 %copy-start.20 = (bf16[1024,128]{1,0:T(8,128)(2,1)S(1)}, bf16[1024,128]{1,0:T(8,128)(2,1)}, u32[]{:S(2)}) copy-start(bf16[1024,128]{1,0:T(8,128)(2,1)} %get-tuple-element.61) | copy-start | bytes 786436
  91.1 15.0 %copy-start.18 = (bf16[1024,128]{1,0:T(8,128)(2,1)S(1)}, bf16[1024,128]{1,0:T(8,128)(2,1)}, u32[]{:S(2)}) copy-start(bf16[1024,128]{1,0:T(8,128)(2,1)} %get-tuple-element.57) | copy-start | bytes 786436
  91.1 15.4 %copy-start.17 = (bf16[1024,128]{1,0:T(8,128)(2,1)S(1)}, bf16[1024,128]{1,0:T(8,128)(2,1)}, u32[]{:S(2)}) copy-start(bf16[1024,128]{1,0:T(8,128)(2,1)} %get-tuple-element.62) | copy-start | bytes 786436
  91.1 26.8 %all-to-all-start.2 = ((bf16[16,3,48,256]{3,2,1,0:T(8,128)(2,1)}), bf16[16,3,48,256]{3,2,1,0:T(8,128)(2,1)}, u32[]{:S(2)}, u32[]{:S(2)}) async-start(bf16[16,3,48,256]{3,2,1,0:T(8,128)(2,1)} %get-tuple-element.55), calls=%async_computation.2 | async-start | bytes 2359296 | tf_op jit(solution)/shard_map/all_to_all | solution.py:338
  95.6 21.3 %copy-start.13 = (bf16[1024,128]{1,0:T(8,128)(2,1)S(1)}, bf16[1024,128]{1,0:T(8,128)(2,1)}, u32[]{:S(2)}) copy-start(bf16[1024,128]{1,0:T(8,128)(2,1)} %get-tuple-element.56.a0) | copy-start | bytes 786436
  95.6 21.3 %copy-start.14 = (bf16[1024,128]{1,0:T(8,128)(2,1)S(1)}, bf16[1024,128]{1,0:T(8,128)(2,1)}, u32[]{:S(2)}) copy-start(bf16[1024,128]{1,0:T(8,128)(2,1)} %get-tuple-element.60.a1) | copy-start | bytes 786436
  95.7 10.4 %collective-permute-start.8 = (bf16[1024,128]{1,0:T(8,128)(2,1)S(1)}, bf16[1024,128]{1,0:T(8,128)(2,1)S(1)}, u32[]{:S(2)}, u32[]{:S(2)}) collective-permute-start(bf16[1024,128]{1,0:T(8,128)(2,1)S(1)} %copy-done.21), channel_id=1, source_target_pairs={{0,32},{16,48},{32,64},{48,80},{64,96},{80,112},{96,0},{112,16},{1... | collective-permute-start | bytes 786440 | tf_op jit(solution)/shard_map/ppermute | solution.py:279
  95.8 10.7 %collective-permute-start.12 = (bf16[1024,128]{1,0:T(8,128)(2,1)S(1)}, bf16[1024,128]{1,0:T(8,128)(2,1)S(1)}, u32[]{:S(2)}, u32[]{:S(2)}) collective-permute-start(bf16[1024,128]{1,0:T(8,128)(2,1)S(1)} %copy-done.22), channel_id=1, source_target_pairs={{0,96},{16,112},{32,0},{48,16},{64,32},{80,48},{96,64},{112,80},{1... | collective-permute-start | bytes 786440 | tf_op jit(solution)/shard_map/ppermute | solution.py:279
  99.1 12.3 %collective-permute-start.10 = (bf16[1024,128]{1,0:T(8,128)(2,1)S(1)}, bf16[1024,128]{1,0:T(8,128)(2,1)S(1)}, u32[]{:S(2)}, u32[]{:S(2)}) collective-permute-start(bf16[1024,128]{1,0:T(8,128)(2,1)S(1)} %copy-done.19), channel_id=1, source_target_pairs={{0,96},{16,112},{32,0},{48,16},{64,32},{80,48},{96,64},{112,80},{1... | collective-permute-start | bytes 786440 | tf_op jit(solution)/shard_map/ppermute | solution.py:279
  101.0 10.7 %collective-permute-start.11 = (bf16[1024,128]{1,0:T(8,128)(2,1)S(1)}, bf16[1024,128]{1,0:T(8,128)(2,1)S(1)}, u32[]{:S(2)}, u32[]{:S(2)}) collective-permute-start(bf16[1024,128]{1,0:T(8,128)(2,1)S(1)} %copy-done.20), channel_id=1, source_target_pairs={{0,32},{16,48},{32,64},{48,80},{64,96},{80,112},{96,0},{112,16},{1... | collective-permute-start | bytes 786440 | tf_op jit(solution)/shard_map/ppermute | solution.py:279
  106.1 10.8 %collective-permute-start.9 = (bf16[1024,128]{1,0:T(8,128)(2,1)S(1)}, bf16[1024,128]{1,0:T(8,128)(2,1)S(1)}, u32[]{:S(2)}, u32[]{:S(2)}) collective-permute-start(bf16[1024,128]{1,0:T(8,128)(2,1)S(1)} %add_convert_fusion.1), channel_id=1, source_target_pairs={{0,32},{16,48},{32,64},{48,80},{64,96},{80,112},{96,0},{112,16},{1... | collective-permute-start | bytes 786440 | tf_op jit(solution)/shard_map/ppermute | solution.py:279
  106.5 10.4 %collective-permute-start.13 = (bf16[1024,128]{1,0:T(8,128)(2,1)S(1)}, bf16[1024,128]{1,0:T(8,128)(2,1)S(1)}, u32[]{:S(2)}, u32[]{:S(2)}) collective-permute-start(bf16[1024,128]{1,0:T(8,128)(2,1)S(1)} %add_convert_fusion), channel_id=1, source_target_pairs={{0,96},{16,112},{32,0},{48,16},{64,32},{80,48},{96,64},{112,80},{1... | collective-permute-start | bytes 786440 | tf_op jit(solution)/shard_map/ppermute | solution.py:279
  116.9 6.8 %copy-start.2 = (bf16[768,768]{1,0:T(8,128)(2,1)S(1)}, bf16[768,768]{1,0:T(8,128)(2,1)}, u32[]{:S(2)}) copy-start(bf16[768,768]{1,0:T(8,128)(2,1)} %wk_ref.3) | copy-start | bytes 3538948
  117.9 17.7 %all-to-all-start.3 = ((bf16[32,64,128]{2,1,0:T(8,128)(2,1)}), bf16[32,64,128]{2,1,0:T(8,128)(2,1)S(1)}, u32[]{:S(2)}, u32[]{:S(2)}) async-start(bf16[32,64,128]{2,1,0:T(8,128)(2,1)} %bitcast.13), calls=%async_computation.3 | async-start | bytes 1048576 | tf_op jit(solution)/shard_map/all_to_all | solution.py:284
  123.7 1.3 copy-start.4

commit v3 on v2

--- a/solution.py
+++ b/solution.py
@@ -61,7 +61,7 @@
 
 def attend_body(scale, steps, chunk, order_ref, *refs):
     first, last = chunk == 0, chunk == CHUNKS - 1
-    bias_refs, refs = refs[:5], refs[5:]
+    bias_refs, refs = refs[:4], refs[4:]
     (q_ref, o_ref, qt_ref, ot_ref, kt_ref, vt_ref, k_ref), refs = refs[:7], refs[7:]
     if not first:
         (g_in, dk_in, dv_in), refs = refs[:3], refs[11:]
@@ -82,8 +82,7 @@
         group = 16
         for g in range(TILE // group):
             rows = slice(g * group, g * group + group)
-            bias = [ref[e, rows, :] for ref in bias_refs[:3] for e in range(2)] + [ref[rows, :] for ref in bias_refs[3:]]
-            bias = jnp.concatenate(bias, axis=1)
+            bias = jnp.concatenate([ref[e, rows, :] for ref in bias_refs for e in range(2)], axis=1)
             s = s_ref[b % 2, rows, :] * (scale * LOG2E) + bias
             m = jnp.max(s, axis=1, keepdims=True)
             e = jnp.exp2(s - m)
@@ -155,7 +154,7 @@
     tr_t = pl.BlockSpec((NB, HD, TILE), lambda i: (0, 0, i + at))
     tr_w = pl.BlockSpec((NB, HD, TOK), lambda i: (0, 0, 0))
     nat_w = pl.BlockSpec((NB, TOK, HD), lambda i: (0, 0, 0))
-    bias_t = [pl.BlockSpec((2, TILE, 128), lambda i: (0, i, 0))] * 3 + [pl.BlockSpec((TILE, 128), lambda i: (i, 0))] * 2
+    bias_t = [pl.BlockSpec((2, TILE, 128), lambda i: (0, i, 0))] * 4
     dbias_t = pl.BlockSpec((TILE, 128), lambda i: (i + at, 0))
     g_spec = pl.BlockSpec((16, 3, HD, 256), lambda i: (0, 0, 0, 0))
     dq_spec = pl.BlockSpec((16 // CHUNKS, HD, 256), lambda i: (0, 0, 0))
@@ -284,11 +283,17 @@
     return lax.all_to_all(x, ("sample", "tok"), 0, 0, axis_index_groups=groups)
 
 
-def gather_blocks(own, after):
-    if after is not None:
-        own = lax.optimization_barrier((own, after))[0]
-    up, down = shift_y(own, 1), shift_y(own, -1)
-    return [own, up, down, shift_y(up[0], 1), shift_y(down[1], -1)]
+def tie(*values):
+    return lax.optimization_barrier(values)
+
+
+def gather_blocks(first, second):
+    up, down = shift_y(first, 1), shift_y(first, -1)
+    far = shift_y(up, 1)
+    later, far = tie(second, far)
+    sooner, down = tie(second, down)
+    up2, down2 = shift_y(later, 1), shift_y(sooner, -1)
+    return [first, up, down, far], [second, up2, down2, shift_y(down2, -1)]
 
 
 def key_order():
@@ -331,10 +336,10 @@
     bias, sent = lax.optimization_barrier((bias, sent))
     received = lax.all_to_all(sent, "tok", 0, 0)
     held = prep(order, received)
-    dbias, carried, blocks, rows = (), (), None, TOK // CHUNKS
+    blocks = gather_blocks(bias[:, :TOK // 2], bias[:, TOK // 2:])
+    dbias, carried = (), ()
     for c in range(CHUNKS):
-        blocks = gather_blocks(bias[:, c * rows:c * rows + rows], blocks[1] if blocks else None)
-        dbias, carried = attend(c, order, blocks, held, dbias, carried)
+        dbias, carried = attend(c, order, blocks[c], held, dbias, carried)
     grads = lax.all_to_all(carried[0], "tok", 0, 0)
     dbias = scatter_blocks(dbias)
     grads, dbias = lax.optimization_barrier((grads, dbias))

time: 139 us -> 137 us (0.986)
  local copies, waits for them, and re-layouts: 15.8 us -> 10.2 us
  waiting for transfers between devices: 46.4 us -> 51.9 us
  starting transfers between devices: 42.7 us -> 40.2 us
    ppermute x14 -> x12, waiting for transfers between devices: 27.2 us -> 32.7 us  [shift_y(): lax.ppermute(x, 'sample', [(i, (i // 2 + d) % 4 * 2 + i % 2) for i in ran...]
    squeeze x4 -> x0, local copies, waits for them, and re-layouts: 4.78 us -> none  [gather_blocks(): return [own, up, down, shift_y(up[0], 1), shift_y(down[1], -1)]]
    ppermute x14 -> x12, starting transfers between devices: 20.1 us -> 17.6 us  [shift_y(): lax.ppermute(x, 'sample', [(i, (i // 2 + d) % 4 * 2 + i % 2) for i in ran...]
    unnamed x47 -> x43, local copies, waits for them, and re-layouts: 8.88 us -> 8.03 us
  transfers between devices with their start and end apart: 18 -> 16, of which waited for: 8 -> 9; matrix products, arithmetic and copies ran while one was open for 4% -> 0% of each run, Pallas kernels for 14% -> 14%
where the time goes in v3:
time: 137 us; the launch traced here: 135 us
  waiting for transfers between devices  51.9 us (38%)
  starting transfers between devices  40.2 us (29%)
  Pallas kernels  31.7 us (23%)
  local copies, waits for them, and re-layouts  10.2 us (7%)
    ppermute x12, waiting for transfers between devices, shift_y(): lax.ppermute(x, 'sample', [(i, (i // 2 + d) % 4 * 2 + i % 2) for i in ran...  32.7 us
    pallas_call x2, Pallas kernels, attend(): pl.pallas_call(functools.partial(attend_body, scale, steps, chunk), grid=...  19.3 us
    all_to_all x2, waiting for transfers between devices, exchange(): return lax.all_to_all(x, ('sample', 'tok'), 0, 0, axis_index_groups=groups)  19.2 us
    ppermute x12, starting transfers between devices, shift_y(): lax.ppermute(x, 'sample', [(i, (i // 2 + d) % 4 * 2 + i % 2) for i in ran...  17.6 us
    all_to_all x2, starting transfers between devices, exchange(): return lax.all_to_all(x, ('sample', 'tok'), 0, 0, axis_index_groups=groups)  14.3 us
    unnamed x43, local copies, waits for them, and re-layouts  8.03 us
    all_to_all x1, starting transfers between devices, local(): grads = lax.all_to_all(carried[0], 'tok', 0, 0)  4.53 us
    all_to_all x1, starting transfers between devices, local(): received = lax.all_to_all(sent, 'tok', 0, 0)  3.71 us
  transfers between devices with their start and end apart: 16, of which 9 were waited for; matrix products, arithmetic and copies ran while one was open for 0% of the time, Pallas kernels for 14%

profile of v3, /device:TPU:0, one launch (start us, length us, event | category | flops | bytes accessed | tf_op | source)
XLA Modules:
  0.0 135.0 jit_solution(208430735655896746)
XLA Ops:
  0.6 0.8 copy.18.w_ref
  1.4 1.6 %copy-done.6 = bf16[64,128,128]{2,1,0:T(8,128)(2,1)S(1)} copy-done((bf16[64,128,128]{2,1,0:T(8,128)(2,1)S(1)}, bf16[64,128,128]{2,1,0:T(8,128)(2,1)}, u32[]{:S(2)}) %copy-start.6) | copy-done | bytes 2097176
  3.0 0.7 bias_part.1
  3.8 1.0 copy-done.5
  4.8 8.5 %all-to-all-start = ((f32[32,64,128]{2,1,0:T(8,128)}), f32[32,64,128]{2,1,0:T(8,128)}, u32[]{:S(2)}, u32[]{:S(2)}) async-start(f32[32,64,128]{2,1,0:T(8,128)} %copy-done.5), calls=%async_computation | async-start | bytes 2097152 | tf_op jit(solution)/shard_map/all_to_all | solution.py:283
  13.3 0.0 copy-start.3
  13.3 1.3 copy-done.3
  14.6 1.3 copy-done.8
  15.9 2.5 %project.1 = bf16[16,4,48,256]{3,2,1,0:T(8,128)(2,1)} custom-call(bf16[4,64,768]{2,1,0:T(8,128)(2,1)S(1)} %copy-done.13, bf16[4,64,768]{2,1,0:T(8,128)(2,1)S(1)} %copy-done.14, bf16[768,768]{1,0:T(8,128)(2,1)S(1)} %copy-done, bf16[768,768]{1,0:T(8,128)(2,1)S(1)} %copy-done.1, bf16[768,768]{1,0:T(8,128)(2,1)S(1)} %copy-done.3, bf16[768,768]{1,0:T(8,128)(2,1)S(1)} %copy-done.8), custom_call_target="tpu_custom_call" | custom-call | tf_op jit(solution)/shard_map/project/pallas_call | solution.py:253
  18.4 11.7 %all-to-all-done = f32[32,64,128]{2,1,0:T(8,128)} async-done(((f32[32,64,128]{2,1,0:T(8,128)}), f32[32,64,128]{2,1,0:T(8,128)}, u32[]{:S(2)}, u32[]{:S(2)}) %all-to-all-start) | async-done | bytes 1048608 | tf_op jit(solution)/shard_map/all_to_all | solution.py:283
  30.2 2.1 %fusion = (f32[2,512,128]{2,1,0:T(8,128)S(1)}, f32[2,512,128]{2,1,0:T(8,128)}) fusion(f32[2,1024,128]{2,1,0:T(8,128)} %bitcast.8), kind=kLoop, calls=%fused_computation.2 | loop fusion | bytes 2097152 | tf_op jit(solution)/shard_map/slice | solution.py:339
  32.2 1.6 %collective-permute-start = (f32[2,512,128]{2,1,0:T(8,128)S(1)}, f32[2,512,128]{2,1,0:T(8,128)}, u32[]{:S(2)}, u32[]{:S(2)}) collective-permute-start(f32[2,512,128]{2,1,0:T(8,128)S(1)} %get-tuple-element.72.refs_0_), channel_id=1, source_target_pairs={{0,32},{16,48},{32,64},{48,80},{64,96},{80,112},{96,0},{112,16},{1... | collective-permute-start | bytes 1572872 | tf_op jit(solution)/shard_map/ppermute | solution.py:278
  33.8 1.7 %collective-permute-start.3 = (f32[2,512,128]{2,1,0:T(8,128)S(1)}, f32[2,512,128]{2,1,0:T(8,128)}, u32[]{:S(2)}, u32[]{:S(2)}) collective-permute-start(f32[2,512,128]{2,1,0:T(8,128)S(1)} %get-tuple-element.72.refs_0_), channel_id=1, source_target_pairs={{0,96},{16,112},{32,0},{48,16},{64,32},{80,48},{96,64},{112,80},{1... | collective-permute-start | bytes 1572872 | tf_op jit(solution)/shard_map/ppermute | solution.py:278
  35.5 3.7 %all-to-all-start.1 = ((bf16[16,4,48,256]{3,2,1,0:T(8,128)(2,1)}), bf16[16,4,48,256]{3,2,1,0:T(8,128)(2,1)S(1)}, u32[]{:S(2)}, u32[]{:S(2)}) async-start(bf16[16,4,48,256]{3,2,1,0:T(8,128)(2,1)} %project.1), calls=%async_computation.1 | async-start | bytes 3145728 | tf_op jit(solution)/shard_map/all_to_all | solution.py:337
  39.2 8.4 %collective-permute-done.refs_1_ = f32[2,512,128]{2,1,0:T(8,128)} collective-permute-done((f32[2,512,128]{2,1,0:T(8,128)S(1)}, f32[2,512,128]{2,1,0:T(8,128)}, u32[]{:S(2)}, u32[]{:S(2)}) %collective-permute-start) | collective-permute-done | bytes 524320 | tf_op jit(solution)/shard_map/ppermute | solution.py:278
  47.6 0.3 collective-permute-start.1
  47.9 2.9 %collective-permute-start.4 = (f32[2,512,128]{2,1,0:T(8,128)}, f32[2,512,128]{2,1,0:T(8,128)}, u32[]{:S(2)}, u32[]{:S(2)}) collective-permute-start(f32[2,512,128]{2,1,0:T(8,128)} %get-tuple-element.39.refs_0_), channel_id=1, source_target_pairs={{0,96},{16,112},{32,0},{48,16},{64,32},{80,48},{96,64},{112,80},{1... | collective-permute-start | bytes 1572872 | tf_op jit(solution)/shard_map/ppermute | solution.py:278
  50.8 11.4 %collective-permute-done.1.refs_3_ = f32[2,512,128]{2,1,0:T(8,128)S(1)} collective-permute-done((f32[2,512,128]{2,1,0:T(8,128)}, f32[2,512,128]{2,1,0:T(8,128)S(1)}, u32[]{:S(2)}, u32[]{:S(2)}) %collective-permute-start.1) | collective-permute-done | bytes 524320 | tf_op jit(solution)/shard_map/ppermute | solution.py:278
  62.2 0.8 copy-done.11
  63.0 2.3 %collective-permute-start.5 = (f32[2,512,128]{2,1,0:T(8,128)}, f32[2,512,128]{2,1,0:T(8,128)}, u32[]{:S(2)}, u32[]{:S(2)}) collective-permute-start(f32[2,512,128]{2,1,0:T(8,128)} %collective-permute-done.4.refs_2_), channel_id=1, source_target_pairs={{0,96},{16,112},{32,0},{48,16},{64,32},{80,48},{96,64},{112,80},{1... | collective-permute-start | bytes 1572872 | tf_op jit(solution)/shard_map/ppermute | solution.py:278
  65.3 0.0 collective-permute-start.2
  65.3 0.1 stack.35.order_ref
  65.4 2.8 %prep.1 = (bf16[4,1024,48]{2,1,0:T(8,128)(2,1)S(1)}, bf16[4,1024,48]{2,1,0:T(8,128)(2,1)S(1)}, bf16[4,48,1024]{2,1,0:T(8,128)(2,1)S(1)}, bf16[4,48,1024]{2,1,0:T...) custom-call(s32[8]{0:T(128)S(1)} %stack.35.order_ref, ...), custom_call_target="tpu_custom_call" | custom-call | tf_op jit(solution)/shard_map/prep/pallas_call | solution.py:47
  68.2 9.2 %attend_0.1 = (bf16[1024,128]{1,0:T(8,128)(2,1)}, bf16[1024,128]{1,0:T(8,128)(2,1)}, bf16[1024,128]{1,0:T(8,128)(2,1)}, bf16[1024,128]{1,0:T(8,128)(2,1)}, bf16[...) custom-call(s32[8]{0:T(128)S(1)} %stack.35.order_ref, ...), custom_call_target="tpu_custom_call" | custom-call | flops 1000000 | bytes 1024 | tf_op jit(solution)/shard_map/attend_0/pallas_call | solution.py:180
  77.5 1.1 collective-permute-done.2.refs_1_
  78.5 10.0 %attend_1.1 = (bf16[1024,128]{1,0:T(8,128)(2,1)}, bf16[1024,128]{1,0:T(8,128)(2,1)}, bf16[1024,128]{1,0:T(8,128)(2,1)}, bf16[1024,128]{1,0:T(8,128)(2,1)}, bf16[...) custom-call(s32[8]{0:T(128)S(1)} %stack.35.order_ref, ...), custom_call_target="tpu_custom_call", output_to_operand_aliasing={{0}: (15, {}), {1}: (16, {}), {2}: (17, {}), {3}: (18, {}),... | custom-call | flops 1000000 | bytes 1024 | tf_op jit(solution)/shard_map/attend_1/pallas_call | solution.py:180
  88.6 4.5 %all-to-all-start.2 = ((bf16[16,3,48,256]{3,2,1,0:T(8,128)(2,1)}), bf16[16,3,48,256]{3,2,1,0:T(8,128)(2,1)}, u32[]{:S(2)}, u32[]{:S(2)}) async-start(bf16[16,3,48,256]{3,2,1,0:T(8,128)(2,1)} %get-tuple-element.61), calls=%async_computation.2 | async-start | bytes 2359296 | tf_op jit(solution)/shard_map/all_to_all | solution.py:343
  93.1 0.0 copy-start.9
  93.2 0.1 collective-permute-start.6
  93.3 3.2 %collective-permute-start.10 = (bf16[1024,128]{1,0:T(8,128)(2,1)S(1)}, bf16[1024,128]{1,0:T(8,128)(2,1)S(1)}, u32[]{:S(2)}, u32[]{:S(2)}) collective-permute-start(bf16[1024,128]{1,0:T(8,128)(2,1)S(1)} %copy-done.20), channel_id=1, source_target_pairs={{0,96},{16,112},{32,0},{48,16},{64,32},{80,48},{96,64},{112,80},{1... | collective-permute-start | bytes 786440 | tf_op jit(solution)/shard_map/ppermute | solution.py:278
  96.5 1.0 collective-permute-start.8
  97.5 1.0 collective-permute-start.9
  98.5 5.1 %collective-permute-done.6 = bf16[1024,128]{1,0:T(8,128)(2,1)S(1)} collective-permute-done((bf16[1024,128]{1,0:T(8,128)(2,1)S(1)}, bf16[1024,128]{1,0:T(8,128)(2,1)S(1)}, u32[]{:S(2)}, u32[]{:S(2)}) %collective-permute-start.6) | collective-permute-done | bytes 262176 | tf_op jit(solution)/shard_map/ppermute | solution.py:278
  103.6 0.1 add_convert_fusion.1
  103.7 0.3 collective-permute-start.7
  104.0 0.1 add_convert_fusion
  104.1 3.3 %collective-permute-start.11 = (bf16[1024,128]{1,0:T(8,128)(2,1)S(1)}, bf16[1024,128]{1,0:T(8,128)(2,1)S(1)}, u32[]{:S(2)}, u32[]{:S(2)}) collective-permute-start(bf16[1024,128]{1,0:T(8,128)(2,1)S(1)} %add_convert_fusion), channel_id=1, source_target_pairs={{0,96},{16,112},{32,0},{48,16},{64,32},{80,48},{96,64},{112,80},{1... | collective-permute-start | bytes 786440 | tf_op jit(solution)/shard_map/ppermute | solution.py:278
  107.4 1.4 %collective-permute-done.8.c0 = bf16[1024,128]{1,0:T(8,128)(2,1)S(1)} collective-permute-done((bf16[1024,128]{1,0:T(8,128)(2,1)S(1)}, bf16[1024,128]{1,0:T(8,128)(2,1)S(1)}, u32[]{:S(2)}, u32[]{:S(2)}) %collective-permute-start.8) | collective-permute-done | bytes 262176 | tf_op jit(solution)/shard_map/ppermute | solution.py:278
  108.8 0.4 collective-permute-done.9.b1
  109.2 4.9 %collective-permute-done.7.b0 = bf16[1024,128]{1,0:T(8,128)(2,1)S(1)} collective-permute-done((bf16[1024,128]{1,0:T(8,128)(2,1)S(1)}, bf16[1024,128]{1,0:T(8,128)(2,1)S(1)}, u32[]{:S(2)}, u32[]{:S(2)}) %collective-permute-start.7) | collective-permute-done | bytes 262176 | tf_op jit(solution)/shard_map/ppermute | solution.py:278
  114.2 0.0 copy-start.2
  114.2 1.0 own_sum.1
  115.2 5.8 %all-to-all-start.3 = ((bf16[32,64,128]{2,1,0:T(8,128)(2,1)}), bf16[32,64,128]{2,1,0:T(8,128)(2,1)S(1)}, u32[]{:S(2)}, u32[]{:S(2)}) async-start(bf16[32,64,128]{2,1,0:T(8,128)(2,1)} %bitcast.9), calls=%async_computation.3 | async-start | bytes 1048576 | tf_op jit(solution)/shard_map/all_to_all | solution.py:283
  121.0 0.0 copy-start.4
  121.0 1.3 copy-done.4
  122.3 3.2 %final.1 = bf16[4,64,768]{2,1,0:T(8,128)(2,1)} custom-call(bf16[16,3,48,256]{3,2,1,0:T(8,128)(2,1)} %all-to-all-done.2.g_ref, bf16[768,768]{1,0:T(8,128)(2,1)S(1)} %copy-done, bf16[768,768]{1,0:T(8,128)(2,1)S(1)} %copy-done.2, bf16[768,768]{1,0:T(8,128)(2,1)S(1)} %copy-done.4), custom_call_target="tpu_custom_call" | custom-call | tf_op jit(solution)/shard_map/final/pallas_call | solution.py:270
  125.4 7.4 %all-to-all-done.3 = bf16[32,64,128]{2,1,0:T(8,128)(2,1)S(1)} async-done(((bf16[32,64,128]{2,1,0:T(8,128)(2,1)}), bf16[32,64,128]{2,1,0:T(8,128)(2,1)S(1)}, u32[]{:S(2)}, u32[]{:S(2)}) %all-to-all-start.3) | async-done | bytes 524320 | tf_op jit(solution)/shard_map/all_to_all | solution.py:283
  132.9 2.1 %gpair.1 = bf16[64,128,128]{2,1,0:T(8,128)(2,1)} custom-call(bf16[2,16,64,128]{3,2,1,0:T(8,128)(2,1)S(1)} %bitcast.11, bf16[128,16]{1,0:T(8,128)(2,1)S(1)} %copy.18.w_ref), custom_call_target="tpu_custom_call" | custom-call | tf_op jit(solution)/shard_map/gpair/pallas_call | solution.py:232
  (39 shorter events, 0.1 us)
Async XLA Ops:
  1.4 1.6 %copy-start.6 = (bf16[64,128,128]{2,1,0:T(8,128)(2,1)S(1)}, bf16[64,128,128]{2,1,0:T(8,128)(2,1)}, u32[]{:S(2)}) copy-start(bf16[64,128,128]{2,1,0:T(8,128)(2,1)} %pair_ref.1) | copy-start | bytes 6291460
  3.0 10.3 %copy-start.1 = (bf16[768,768]{1,0:T(8,128)(2,1)S(1)}, bf16[768,768]{1,0:T(8,128)(2,1)}, u32[]{:S(2)}) copy-start(bf16[768,768]{1,0:T(8,128)(2,1)} %wk_ref.3) | copy-start | bytes 3538948
  3.8 1.0 copy-start.5
  4.8 8.5 %copy-start = (bf16[768,768]{1,0:T(8,128)(2,1)S(1)}, bf16[768,768]{1,0:T(8,128)(2,1)}, u32[]{:S(2)}) copy-start(bf16[768,768]{1,0:T(8,128)(2,1)} %wq_ref.3) | copy-start | bytes 3538948
  4.8 8.5 %copy-start.13 = (bf16[4,64,768]{2,1,0:T(8,128)(2,1)S(1)}, bf16[4,64,768]{2,1,0:T(8,128)(2,1)}, u32[]{:S(2)}) copy-start(bf16[4,64,768]{2,1,0:T(8,128)(2,1)} %x_ref.1) | copy-start | bytes 1179652
  4.8 8.5 %copy-start.14 = (bf16[4,64,768]{2,1,0:T(8,128)(2,1)S(1)}, bf16[4,64,768]{2,1,0:T(8,128)(2,1)}, u32[]{:S(2)}) copy-start(bf16[4,64,768]{2,1,0:T(8,128)(2,1)} %c_ref.1) | copy-start | bytes 1179652
  4.8 25.4 %all-to-all-start = ((f32[32,64,128]{2,1,0:T(8,128)}), f32[32,64,128]{2,1,0:T(8,128)}, u32[]{:S(2)}, u32[]{:S(2)}) async-start(f32[32,64,128]{2,1,0:T(8,128)} %copy-done.5), calls=%async_computation | async-start | bytes 2097152 | tf_op jit(solution)/shard_map/all_to_all | solution.py:283
  13.3 1.3 copy-start.3
  14.6 1.3 copy-start.8
  32.2 15.3 %collective-permute-start = (f32[2,512,128]{2,1,0:T(8,128)S(1)}, f32[2,512,128]{2,1,0:T(8,128)}, u32[]{:S(2)}, u32[]{:S(2)}) collective-permute-start(f32[2,512,128]{2,1,0:T(8,128)S(1)} %get-tuple-element.72.refs_0_), channel_id=1, source_target_pairs={{0,32},{16,48},{32,64},{48,80},{64,96},{80,112},{96,0},{112,16},{1... | collective-permute-start | bytes 1572872 | tf_op jit(solution)/shard_map/ppermute | solution.py:278
  33.8 14.1 %collective-permute-start.3 = (f32[2,512,128]{2,1,0:T(8,128)S(1)}, f32[2,512,128]{2,1,0:T(8,128)}, u32[]{:S(2)}, u32[]{:S(2)}) collective-permute-start(f32[2,512,128]{2,1,0:T(8,128)S(1)} %get-tuple-element.72.refs_0_), channel_id=1, source_target_pairs={{0,96},{16,112},{32,0},{48,16},{64,32},{80,48},{96,64},{112,80},{1... | collective-permute-start | bytes 1572872 | tf_op jit(solution)/shard_map/ppermute | solution.py:278
  35.5 29.9 %all-to-all-start.1 = ((bf16[16,4,48,256]{3,2,1,0:T(8,128)(2,1)}), bf16[16,4,48,256]{3,2,1,0:T(8,128)(2,1)S(1)}, u32[]{:S(2)}, u32[]{:S(2)}) async-start(bf16[16,4,48,256]{3,2,1,0:T(8,128)(2,1)} %project.1), calls=%async_computation.1 | async-start | bytes 3145728 | tf_op jit(solution)/shard_map/all_to_all | solution.py:337
  47.6 14.6 %collective-permute-start.1 = (f32[2,512,128]{2,1,0:T(8,128)}, f32[2,512,128]{2,1,0:T(8,128)S(1)}, u32[]{:S(2)}, u32[]{:S(2)}) collective-permute-start(f32[2,512,128]{2,1,0:T(8,128)} %collective-permute-done.refs_1_), channel_id=1, source_target_pairs={{0,32},{16,48},{32,64},{48,80},{64,96},{80,112},{96,0},{112,16},{1... | collective-permute-start | bytes 1572872 | tf_op jit(solution)/shard_map/ppermute | solution.py:278
  47.9 15.1 %collective-permute-start.4 = (f32[2,512,128]{2,1,0:T(8,128)}, f32[2,512,128]{2,1,0:T(8,128)}, u32[]{:S(2)}, u32[]{:S(2)}) collective-permute-start(f32[2,512,128]{2,1,0:T(8,128)} %get-tuple-element.39.refs_0_), channel_id=1, source_target_pairs={{0,96},{16,112},{32,0},{48,16},{64,32},{80,48},{96,64},{112,80},{1... | collective-permute-start | bytes 1572872 | tf_op jit(solution)/shard_map/ppermute | solution.py:278
  62.2 0.8 copy-start.11
  63.0 14.5 %collective-permute-start.5 = (f32[2,512,128]{2,1,0:T(8,128)}, f32[2,512,128]{2,1,0:T(8,128)}, u32[]{:S(2)}, u32[]{:S(2)}) collective-permute-start(f32[2,512,128]{2,1,0:T(8,128)} %collective-permute-done.4.refs_2_), channel_id=1, source_target_pairs={{0,96},{16,112},{32,0},{48,16},{64,32},{80,48},{96,64},{112,80},{1... | collective-permute-start | bytes 1572872 | tf_op jit(solution)/shard_map/ppermute | solution.py:278
  65.3 13.2 %collective-permute-start.2 = (f32[2,512,128]{2,1,0:T(8,128)}, f32[2,512,128]{2,1,0:T(8,128)}, u32[]{:S(2)}, u32[]{:S(2)}) collective-permute-start(f32[2,512,128]{2,1,0:T(8,128)} %get-tuple-element.39.refs_0_), channel_id=1, source_target_pairs={{0,32},{16,48},{32,64},{48,80},{64,96},{80,112},{96,0},{112,16},{1... | collective-permute-start | bytes 1572872 | tf_op jit(solution)/shard_map/ppermute | solution.py:278
  65.4 2.8 %copy-start.12 = (f32[2,512,128]{2,1,0:T(8,128)S(1)}, f32[2,512,128]{2,1,0:T(8,128)}, u32[]{:S(2)}) copy-start(f32[2,512,128]{2,1,0:T(8,128)} %copy-done.11) | copy-start | bytes 1572868
  68.2 10.3 %copy-start.7 = (f32[2,512,128]{2,1,0:T(8,128)S(1)}, f32[2,512,128]{2,1,0:T(8,128)}, u32[]{:S(2)}) copy-start(f32[2,512,128]{2,1,0:T(8,128)} %get-tuple-element.39.refs_0_) | copy-start | bytes 1572868
  88.6 4.6 %copy-start.19 = (bf16[1024,128]{1,0:T(8,128)(2,1)S(1)}, bf16[1024,128]{1,0:T(8,128)(2,1)}, u32[]{:S(2)}) copy-start(bf16[1024,128]{1,0:T(8,128)(2,1)} %get-tuple-element.64) | copy-start | bytes 786436
  88.6 4.7 %copy-start.20 = (bf16[1024,128]{1,0:T(8,128)(2,1)S(1)}, bf16[1024,128]{1,0:T(8,128)(2,1)}, u32[]{:S(2)}) copy-start(bf16[1024,128]{1,0:T(8,128)(2,1)} %get-tuple-element.69) | copy-start | bytes 786436
  88.6 7.9 %copy-start.17 = (bf16[1024,128]{1,0:T(8,128)(2,1)S(1)}, bf16[1024,128]{1,0:T(8,128)(2,1)}, u32[]{:S(2)}) copy-start(bf16[1024,128]{1,0:T(8,128)(2,1)} %get-tuple-element.65) | copy-start | bytes 786436
  88.6 9.0 %copy-start.18 = (bf16[1024,128]{1,0:T(8,128)(2,1)S(1)}, bf16[1024,128]{1,0:T(8,128)(2,1)}, u32[]{:S(2)}) copy-start(bf16[1024,128]{1,0:T(8,128)(2,1)} %get-tuple-element.67) | copy-start | bytes 786436
  88.6 15.0 %copy-start.16 = (bf16[1024,128]{1,0:T(8,128)(2,1)S(1)}, bf16[1024,128]{1,0:T(8,128)(2,1)}, u32[]{:S(2)}) copy-start(bf16[1024,128]{1,0:T(8,128)(2,1)} %get-tuple-element.63) | copy-start | bytes 786436
  88.6 15.4 %copy-start.15 = (bf16[1024,128]{1,0:T(8,128)(2,1)S(1)}, bf16[1024,128]{1,0:T(8,128)(2,1)}, u32[]{:S(2)}) copy-start(bf16[1024,128]{1,0:T(8,128)(2,1)} %get-tuple-element.68) | copy-start | bytes 786436
  88.6 26.6 %all-to-all-start.2 = ((bf16[16,3,48,256]{3,2,1,0:T(8,128)(2,1)}), bf16[16,3,48,256]{3,2,1,0:T(8,128)(2,1)}, u32[]{:S(2)}, u32[]{:S(2)}) async-start(bf16[16,3,48,256]{3,2,1,0:T(8,128)(2,1)} %get-tuple-element.61), calls=%async_computation.2 | async-start | bytes 2359296 | tf_op jit(solution)/shard_map/all_to_all | solution.py:343
  93.1 21.0 %copy-start.9 = (bf16[1024,128]{1,0:T(8,128)(2,1)S(1)}, bf16[1024,128]{1,0:T(8,128)(2,1)}, u32[]{:S(2)}) copy-start(bf16[1024,128]{1,0:T(8,128)(2,1)} %get-tuple-element.62.a0) | copy-start | bytes 786436
  93.2 21.0 %copy-start.10 = (bf16[1024,128]{1,0:T(8,128)(2,1)S(1)}, bf16[1024,128]{1,0:T(8,128)(2,1)}, u32[]{:S(2)}) copy-start(bf16[1024,128]{1,0:T(8,128)(2,1)} %get-tuple-element.66.a1) | copy-start | bytes 786436
  93.2 10.4 %collective-permute-start.6 = (bf16[1024,128]{1,0:T(8,128)(2,1)S(1)}, bf16[1024,128]{1,0:T(8,128)(2,1)S(1)}, u32[]{:S(2)}, u32[]{:S(2)}) collective-permute-start(bf16[1024,128]{1,0:T(8,128)(2,1)S(1)} %copy-done.19), channel_id=1, source_target_pairs={{0,32},{16,48},{32,64},{48,80},{64,96},{80,112},{96,0},{112,16},{1... | collective-permute-start | bytes 786440 | tf_op jit(solution)/shard_map/ppermute | solution.py:278
  93.3 10.7 %collective-permute-start.10 = (bf16[1024,128]{1,0:T(8,128)(2,1)S(1)}, bf16[1024,128]{1,0:T(8,128)(2,1)S(1)}, u32[]{:S(2)}, u32[]{:S(2)}) collective-permute-start(bf16[1024,128]{1,0:T(8,128)(2,1)S(1)} %copy-done.20), channel_id=1, source_target_pairs={{0,96},{16,112},{32,0},{48,16},{64,32},{80,48},{96,64},{112,80},{1... | collective-permute-start | bytes 786440 | tf_op jit(solution)/shard_map/ppermute | solution.py:278
  96.5 12.3 %collective-permute-start.8 = (bf16[1024,128]{1,0:T(8,128)(2,1)S(1)}, bf16[1024,128]{1,0:T(8,128)(2,1)S(1)}, u32[]{:S(2)}, u32[]{:S(2)}) collective-permute-start(bf16[1024,128]{1,0:T(8,128)(2,1)S(1)} %copy-done.17), channel_id=1, source_target_pairs={{0,96},{16,112},{32,0},{48,16},{64,32},{80,48},{96,64},{112,80},{1... | collective-permute-start | bytes 786440 | tf_op jit(solution)/shard_map/ppermute | solution.py:278
  97.5 11.7 %collective-permute-start.9 = (bf16[1024,128]{1,0:T(8,128)(2,1)S(1)}, bf16[1024,128]{1,0:T(8,128)(2,1)S(1)}, u32[]{:S(2)}, u32[]{:S(2)}) collective-permute-start(bf16[1024,128]{1,0:T(8,128)(2,1)S(1)} %copy-done.18), channel_id=1, source_target_pairs={{0,32},{16,48},{32,64},{48,80},{64,96},{80,112},{96,0},{112,16},{1... | collective-permute-start | bytes 786440 | tf_op jit(solution)/shard_map/ppermute | solution.py:278
  103.7 10.5 %collective-permute-start.7 = (bf16[1024,128]{1,0:T(8,128)(2,1)S(1)}, bf16[1024,128]{1,0:T(8,128)(2,1)S(1)}, u32[]{:S(2)}, u32[]{:S(2)}) collective-permute-start(bf16[1024,128]{1,0:T(8,128)(2,1)S(1)} %add_convert_fusion.1), channel_id=1, source_target_pairs={{0,32},{16,48},{32,64},{48,80},{64,96},{80,112},{96,0},{112,16},{1... | collective-permute-start | bytes 786440 | tf_op jit(solution)/shard_map/ppermute | solution.py:278
  104.1 10.1 %collective-permute-start.11 = (bf16[1024,128]{1,0:T(8,128)(2,1)S(1)}, bf16[1024,128]{1,0:T(8,128)(2,1)S(1)}, u32[]{:S(2)}, u32[]{:S(2)}) collective-permute-start(bf16[1024,128]{1,0:T(8,128)(2,1)S(1)} %add_convert_fusion), channel_id=1, source_target_pairs={{0,96},{16,112},{32,0},{48,16},{64,32},{80,48},{96,64},{112,80},{1... | collective-permute-start | bytes 786440 | tf_op jit(solution)/shard_map/ppermute | solution.py:278
  114.2 6.8 %copy-start.2 = (bf16[768,768]{1,0:T(8,128)(2,1)S(1)}, bf16[768,768]{1,0:T(8,128)(2,1)}, u32[]{:S(2)}) copy-start(bf16[768,768]{1,0:T(8,128)(2,1)} %wk_ref.3) | copy-start | bytes 3538948
  115.2 17.7 %all-to-all-start.3 = ((bf16[32,64,128]{2,1,0:T(8,128)(2,1)}), bf16[32,64,128]{2,1,0:T(8,128)(2,1)S(1)}, u32[]{:S(2)}, u32[]{:S(2)}) async-start(bf16[32,64,128]{2,1,0:T(8,128)(2,1)} %bitcast.9), calls=%async_computation.3 | async-start | bytes 1048576 | tf_op jit(solution)/shard_map/all_to_all | solution.py:283
  121.0 1.3 copy-start.4

commit v4 on v2

--- a/solution.py
+++ b/solution.py
@@ -56,23 +56,30 @@
 
 TILE = 256
 VMEM_ATT = 40
-CHUNKS = 2
-
-
-def attend_body(scale, steps, chunk, order_ref, *refs):
-    first, last = chunk == 0, chunk == CHUNKS - 1
-    bias_refs, refs = refs[:5], refs[5:]
+NEAR = 8.0
+STEEP = 18.8
+
+
+def attend_body(scale, steps, order_ref, *refs):
+    bias_refs, refs = refs[:8], refs[8:]
     (q_ref, o_ref, qt_ref, ot_ref, kt_ref, vt_ref, k_ref), refs = refs[:7], refs[7:]
-    if not first:
-        (g_in, dk_in, dv_in), refs = refs[:3], refs[11:]
     dbias_refs, refs = refs[:8], refs[8:]
-    g_ref, dkt_ref, dvt_ref, s_ref, dp_ref, p_ref, ds_ref, acc_ref, dqt_ref = refs
+    g_ref, s_ref, dp_ref, p_ref, ds_ref, acc_ref, dqt_ref, dkt_ref, dvt_ref, bias_scr = refs
     step = pl.program_id(0)
 
     @pl.when(step == 0)
     def _():
-        dkt_ref[...] = jnp.zeros_like(dkt_ref) if first else dk_in[...]
-        dvt_ref[...] = jnp.zeros_like(dvt_ref) if first else dv_in[...]
+        dkt_ref[...] = jnp.zeros_like(dkt_ref)
+        dvt_ref[...] = jnp.zeros_like(dvt_ref)
+
+    def all_bias():
+        mark = marks(64)[1]
+        for t in range(TILE // 64):
+            for u in range(8):
+                tops = bias_refs[u][t, 64:80].astype(F32)[:8]
+                tops = jnp.broadcast_to(tops[:, None, :], (8, 8, 128)).reshape(64, 128)
+                top = jnp.sum(jnp.where(mark, tops, 0.0), axis=1, keepdims=True)
+                bias_scr[t * 64:t * 64 + 64, u * 128:u * 128 + 128] = decode(bias_refs[u][t, :64], top)
 
     def products(b):
         s_ref[b % 2] = jnp.dot(q_ref[b], kt_ref[b], preferred_element_type=F32)
@@ -82,9 +89,7 @@
         group = 16
         for g in range(TILE // group):
             rows = slice(g * group, g * group + group)
-            bias = [ref[e, rows, :] for ref in bias_refs[:3] for e in range(2)] + [ref[rows, :] for ref in bias_refs[3:]]
-            bias = jnp.concatenate(bias, axis=1)
-            s = s_ref[b % 2, rows, :] * (scale * LOG2E) + bias
+            s = s_ref[b % 2, rows, :] * (scale * LOG2E) + bias_scr[rows, :]
             m = jnp.max(s, axis=1, keepdims=True)
             e = jnp.exp2(s - m)
             inv = 1.0 / jnp.sum(e, axis=1, keepdims=True)
@@ -110,6 +115,7 @@
         dq = jnp.dot(ds_low, k_ref[b], preferred_element_type=F32)
         dqt_ref[step, b] = (dq * scale).T.astype(BF16)
 
+    all_bias()
     products(0)
     for b in range(NB):
         if b + 1 < NB:
@@ -122,72 +128,48 @@
     @pl.when(step == steps - 1)
     def _():
         each = TILE // 64
-        if not first:
-            for t in range(chunk * steps * each):
-                g_ref[t, 0] = g_in[t]
         for b in range(NB):
             lanes = slice(b * 64, b * 64 + 64)
-            for t in range(steps * each):
+            for t in range(16):
                 c = (t % each) * 64
-                block = dqt_ref[t // each, b, :, c:c + 64]
-                if last:
-                    g_ref[chunk * steps * each + t, 0, :, lanes] = block
-                else:
-                    g_ref[t, :, lanes] = block
-            if last:
-                for u in range(8):
-                    one = order_ref[u] * 2
-                    dk = (dkt_ref[b, :, u * 128:u * 128 + 128] * scale).astype(BF16)
-                    dv = dvt_ref[b, :, u * 128:u * 128 + 128].astype(BF16)
-                    g_ref[one, 1, :, lanes] = dk[:, :64]
-                    g_ref[one + 1, 1, :, lanes] = dk[:, 64:]
-                    g_ref[one, 2, :, lanes] = dv[:, :64]
-                    g_ref[one + 1, 2, :, lanes] = dv[:, 64:]
-
-
-def attend(chunk, order, bias, held, dbias, carried):
-    rows = TOK // CHUNKS
-    steps = rows // TILE
-    at = chunk * steps
-    last = chunk == CHUNKS - 1
+                g_ref[t, 0, :, lanes] = dqt_ref[t // each, b, :, c:c + 64]
+            for u in range(8):
+                first = order_ref[u] * 2
+                dk = (dkt_ref[b, :, u * 128:u * 128 + 128] * scale).astype(BF16)
+                dv = dvt_ref[b, :, u * 128:u * 128 + 128].astype(BF16)
+                g_ref[first, 1, :, lanes] = dk[:, :64]
+                g_ref[first + 1, 1, :, lanes] = dk[:, 64:]
+                g_ref[first, 2, :, lanes] = dv[:, :64]
+                g_ref[first + 1, 2, :, lanes] = dv[:, 64:]
+
+
+def attend(order, bias, held):
+    steps = TOK // TILE
     scale = 1.0 / math.sqrt(HD)
-    nat_t = pl.BlockSpec((NB, TILE, HD), lambda i: (0, i + at, 0))
-    tr_t = pl.BlockSpec((NB, HD, TILE), lambda i: (0, 0, i + at))
+    nat_t = pl.BlockSpec((NB, TILE, HD), lambda i: (0, i, 0))
+    tr_t = pl.BlockSpec((NB, HD, TILE), lambda i: (0, 0, i))
     tr_w = pl.BlockSpec((NB, HD, TOK), lambda i: (0, 0, 0))
     nat_w = pl.BlockSpec((NB, TOK, HD), lambda i: (0, 0, 0))
-    bias_t = [pl.BlockSpec((2, TILE, 128), lambda i: (0, i, 0))] * 3 + [pl.BlockSpec((TILE, 128), lambda i: (i, 0))] * 2
-    dbias_t = pl.BlockSpec((TILE, 128), lambda i: (i + at, 0))
+    dbias_t = pl.BlockSpec((TILE, 128), lambda i: (i, 0))
+    one_t = pl.BlockSpec((TILE // 64, 80, 128), lambda i: (i, 0, 0))
     g_spec = pl.BlockSpec((16, 3, HD, 256), lambda i: (0, 0, 0, 0))
-    dq_spec = pl.BlockSpec((16 // CHUNKS, HD, 256), lambda i: (0, 0, 0))
-    sums = jax.ShapeDtypeStruct((NB, HD, TOK), F32)
-    in_specs = [pl.BlockSpec(memory_space=pltpu.SMEM)] + bias_t + [nat_t, nat_t, tr_t, tr_t, tr_w, tr_w, nat_w]
-    aliases = {}
-    if chunk:
-        in_specs += [dq_spec, tr_w, tr_w]
-        aliases = {len(in_specs) + u: u for u in range(8)}
-        in_specs += [pl.BlockSpec(memory_space=pl.ANY)] * 8
-    out_shape, out_specs = [pltpu.HBM((TOK, 128), BF16)] * 8, [dbias_t] * 8
-    scratch = [
-        pltpu.VMEM((2, TILE, TOK), F32), pltpu.VMEM((2, TILE, TOK), F32),
-        pltpu.VMEM((2, TILE, TOK), BF16), pltpu.VMEM((2, TILE, TOK), BF16),
-        pltpu.VMEM((TILE, TOK), F32), pltpu.VMEM((steps, NB, HD, TILE), BF16),
-    ]
-    if last:
-        out_shape, out_specs = out_shape + [jax.ShapeDtypeStruct((16, 3, HD, 256), BF16)], out_specs + [g_spec]
-        scratch = [pltpu.VMEM((NB, HD, TOK), F32)] * 2 + scratch
-    else:
-        out_shape = out_shape + [jax.ShapeDtypeStruct((16 // CHUNKS, HD, 256), BF16), sums, sums]
-        out_specs = out_specs + [dq_spec, tr_w, tr_w]
     outs = pl.pallas_call(
-        functools.partial(attend_body, scale, steps, chunk),
+        functools.partial(attend_body, scale, steps),
         grid=(steps,),
-        out_shape=out_shape, in_specs=in_specs, out_specs=out_specs, scratch_shapes=scratch,
-        input_output_aliases=aliases,
+        out_shape=[pltpu.HBM((TOK, 128), BF16)] * 8 + [jax.ShapeDtypeStruct((16, 3, HD, 256), BF16)],
+        in_specs=[pl.BlockSpec(memory_space=pltpu.SMEM)] + [one_t] * 8 + [nat_t, nat_t, tr_t, tr_t, tr_w, tr_w, nat_w],
+        out_specs=[dbias_t] * 8 + [g_spec],
+        scratch_shapes=[
+            pltpu.VMEM((2, TILE, TOK), F32), pltpu.VMEM((2, TILE, TOK), F32),
+            pltpu.VMEM((2, TILE, TOK), BF16), pltpu.VMEM((2, TILE, TOK), BF16),
+            pltpu.VMEM((TILE, TOK), F32), pltpu.VMEM((steps, NB, HD, TILE), BF16),
+            pltpu.VMEM((NB, HD, TOK), F32), pltpu.VMEM((NB, HD, TOK), F32), pltpu.VMEM((TILE, TOK), F32),
+        ],
         compiler_params=pltpu.CompilerParams(vmem_limit_bytes=VMEM_ATT * 2**20),
         cost_estimate=pl.CostEstimate(flops=10**6, bytes_accessed=2**10, transcendentals=0),
-        name="attend_%d" % chunk,
-    )(order, *bias, *held, *carried, *dbias)
-    return outs[:8], outs[8:]
+        name="attend",
+    )(order, *bias, *held)
+    return outs[:8], outs[8]
 
 
 def block_diagonal(w_ref, count):
@@ -197,22 +179,50 @@
     return jnp.concatenate([jnp.where(at == i, rows, 0.0) for i in range(count)], axis=1).astype(BF16)
 
 
+def encode(bias):
+    top = jnp.max(bias, axis=1, keepdims=True)
+    return jnp.exp2(126.0 - STEEP * jnp.log2(1.0 + (top - bias) * (1.0 / NEAR))).astype(BF16), top
+
+
+def decode(code, top):
+    return (top + NEAR) - NEAR * jnp.exp2((126.0 - jnp.log2(code.astype(F32))) * (1.0 / STEEP))
+
+
+def marks(count):
+    lane = lax.broadcasted_iota(jnp.int32, (count, 128), 1)
+    row = lax.broadcasted_iota(jnp.int32, (count, 128), 0)
+    return lane, (lane < 24) & (lane % 8 == row % 8)
+
+
 def bias_body(pair_ref, w_ref, out_ref):
     w = block_diagonal(w_ref, 8)
+    lane, mark = marks(128)
+    tops = []
     for g in range(8):
         cols = jnp.concatenate([pair_ref[g * 8 + r] for r in range(8)], axis=1)
         t = lax.dot_general(w, cols, (((1,), (1,)), ((), ())), preferred_element_type=F32)
-        t = t * LOG2E
+        code, top = encode(t * LOG2E)
+        high = top.astype(BF16).astype(F32)
+        middle = (top - high).astype(BF16).astype(F32)
+        terms = jnp.where(lane < 8, high, jnp.where(lane < 16, middle, top - high - middle))
+        tops.append(jnp.sum(jnp.where(mark, terms, 0.0).reshape(16, 8, 128), axis=1))
+        if g % 2 == 0:
+            even = code
+            continue
         for h in range(16):
-            block = t[h * 8:h * 8 + 8, :]
-            out_ref[h, g * 8:g * 8 + 8, :] = block
-            out_ref[h + 16, g * 8:g * 8 + 8, :] = block
+            block = jnp.concatenate([even[h * 8:h * 8 + 8, :], code[h * 8:h * 8 + 8, :]], axis=0)
+            out_ref[h, g * 8 - 8:g * 8 + 8, :] = block
+            out_ref[h + 16, g * 8 - 8:g * 8 + 8, :] = block
+    for h in range(16):
+        block = jnp.concatenate([top[h:h + 1, :] for top in tops] + [jnp.zeros((8, 128), F32)], axis=0).astype(BF16)
+        out_ref[h, 64:80, :] = block
+        out_ref[h + 16, 64:80, :] = block
 
 
 def bias_part(pair, w_pair):
     vm = pl.BlockSpec(memory_space=pltpu.VMEM)
     return pl.pallas_call(
-        bias_body, out_shape=jax.ShapeDtypeStruct((32, 64, 128), F32),
+        bias_body, out_shape=jax.ShapeDtypeStruct((32, 80, 128), BF16),
         in_specs=[vm, vm], out_specs=vm,
         compiler_params=pltpu.CompilerParams(vmem_limit_bytes=32 * 2**20), name="bias_part",
     )(pair, w_pair)
@@ -284,11 +294,10 @@
     return lax.all_to_all(x, ("sample", "tok"), 0, 0, axis_index_groups=groups)
 
 
-def gather_blocks(own, after):
-    if after is not None:
-        own = lax.optimization_barrier((own, after))[0]
-    up, down = shift_y(own, 1), shift_y(own, -1)
-    return [own, up, down, shift_y(up[0], 1), shift_y(down[1], -1)]
+def gather_blocks(own):
+    up0, down1 = shift_y(own[0], 1), shift_y(own[1], -1)
+    up1, down0 = shift_y(own[1], 1), shift_y(own[0], -1)
+    return [own[0], own[1], up0, up1, down0, down1, shift_y(up0, 1), shift_y(down1, -1)]
 
 
 def key_order():
@@ -327,15 +336,11 @@
 def local(single, pair, w_query, w_key, w_value, w_out, w_pair, cotangent):
     order = key_order()
     sent = project(single, cotangent, w_query, w_key, w_value, w_out)
-    bias = exchange(bias_part(pair, w_pair)).reshape(2, TOK, 128)
+    bias = exchange(bias_part(pair, w_pair)).reshape(2, 16, 80, 128)
     bias, sent = lax.optimization_barrier((bias, sent))
     received = lax.all_to_all(sent, "tok", 0, 0)
-    held = prep(order, received)
-    dbias, carried, blocks, rows = (), (), None, TOK // CHUNKS
-    for c in range(CHUNKS):
-        blocks = gather_blocks(bias[:, c * rows:c * rows + rows], blocks[1] if blocks else None)
-        dbias, carried = attend(c, order, blocks, held, dbias, carried)
-    grads = lax.all_to_all(carried[0], "tok", 0, 0)
+    dbias, grads = attend(order, gather_blocks(bias), prep(order, received))
+    grads = lax.all_to_all(grads, "tok", 0, 0)
     dbias = scatter_blocks(dbias)
     grads, dbias = lax.optimization_barrier((grads, dbias))
     grad_single = final(grads, w_query, w_key, w_value)

time: 139 us -> 128 us (0.921)
  local copies, waits for them, and re-layouts: 15.8 us -> 7.46 us
  waiting for transfers between devices: 46.4 us -> 42.6 us
    ppermute x14 -> x12, waiting for transfers between devices: 27.2 us -> 21.2 us  [shift_y(): lax.ppermute(x, 'sample', [(i, (i // 2 + d) % 4 * 2 + i % 2) for i in ran...]
    all_to_all x1, waiting for transfers between devices: 0.01 us -> 6.04 us  [local(): received = lax.all_to_all(sent, 'tok', 0, 0)]
    all_to_all x2, waiting for transfers between devices: 19.2 us -> 15.4 us  [exchange(): return lax.all_to_all(x, ('sample', 'tok'), 0, 0, axis_index_groups=groups)]
    squeeze x4 -> x1, local copies, waits for them, and re-layouts: 4.78 us -> 1.12 us  [gather_blocks(): own[1]]
    unnamed x47 -> x35, local copies, waits for them, and re-layouts: 8.88 us -> 6.25 us
    slice x1 -> x0, local copies, waits for them, and re-layouts: 2.09 us -> none  [local(): bias[:, c * rows:c * rows + rows]]
    ppermute x14 -> x12, starting transfers between devices: 20.1 us -> 18.8 us  [shift_y(): lax.ppermute(x, 'sample', [(i, (i // 2 + d) % 4 * 2 + i % 2) for i in ran...]
    pallas_call x3 -> x2, Pallas kernels: 20.1 us -> 21 us  [the longest x1 19.1 us: attend(): pl.pallas_call(functools.partial(attend_body, scale, steps), grid=(steps,...]
  transfers between devices with their start and end apart: 18 -> 16, of which waited for: 8 -> 10; matrix products, arithmetic and copies ran while one was open for 4% -> 1% of each run, Pallas kernels for 14% -> 8%
where the time goes in v4:
time: 128 us; the launch traced here: 126 us
  waiting for transfers between devices  42.6 us (33%)
  starting transfers between devices  42.5 us (33%)
  Pallas kernels  32.7 us (26%)
  local copies, waits for them, and re-layouts  7.46 us (6%)
    ppermute x12, waiting for transfers between devices, shift_y(): lax.ppermute(x, 'sample', [(i, (i // 2 + d) % 4 * 2 + i % 2) for i in ran...  21.2 us
    pallas_call x1, Pallas kernels, attend(): pl.pallas_call(functools.partial(attend_body, scale, steps), grid=(steps,...  19.1 us
    ppermute x12, starting transfers between devices, shift_y(): lax.ppermute(x, 'sample', [(i, (i // 2 + d) % 4 * 2 + i % 2) for i in ran...  18.8 us
    all_to_all x2, waiting for transfers between devices, exchange(): return lax.all_to_all(x, ('sample', 'tok'), 0, 0, axis_index_groups=groups)  15.4 us
    all_to_all x2, starting transfers between devices, exchange(): return lax.all_to_all(x, ('sample', 'tok'), 0, 0, axis_index_groups=groups)  14.2 us
    unnamed x35, local copies, waits for them, and re-layouts  6.25 us
    all_to_all x1, waiting for transfers between devices, local(): received = lax.all_to_all(sent, 'tok', 0, 0)  6.04 us
    all_to_all x1, starting transfers between devices, local(): grads = lax.all_to_all(grads, 'tok', 0, 0)  5.68 us
  transfers between devices with their start and end apart: 16, of which 10 were waited for; matrix products, arithmetic and copies ran while one was open for 1% of the time, Pallas kernels for 8%

profile of v4, /device:TPU:0, one launch (start us, length us, event | category | flops | bytes accessed | tf_op | source)
XLA Modules:
  0.0 126.2 jit_solution(12153888291875438830)
XLA Ops:
  0.6 0.8 copy.10.w_ref
  1.4 1.6 %copy-done.5 = bf16[64,128,128]{2,1,0:T(8,128)(2,1)S(1)} copy-done((bf16[64,128,128]{2,1,0:T(8,128)(2,1)S(1)}, bf16[64,128,128]{2,1,0:T(8,128)(2,1)}, u32[]{:S(2)}) %copy-start.5) | copy-done | bytes 2097176
  3.0 1.9 %bias_part.1 = bf16[32,80,128]{2,1,0:T(8,128)(2,1)} custom-call(bf16[64,128,128]{2,1,0:T(8,128)(2,1)S(1)} %copy-done.5, bf16[128,16]{1,0:T(8,128)(2,1)S(1)} %copy.10.w_ref), custom_call_target="tpu_custom_call" | custom-call | tf_op jit(solution)/shard_map/bias_part/pallas_call | solution.py:224
  5.0 8.5 %all-to-all-start = ((bf16[32,80,128]{2,1,0:T(8,128)(2,1)}), bf16[32,80,128]{2,1,0:T(8,128)(2,1)}, u32[]{:S(2)}, u32[]{:S(2)}) async-start(bf16[32,80,128]{2,1,0:T(8,128)(2,1)} %bias_part.1), calls=%async_computation | async-start | bytes 1310720 | tf_op jit(solution)/shard_map/all_to_all | solution.py:294
  13.5 0.0 copy-start.3
  13.5 1.3 copy-done.3
  14.8 1.3 %copy-done.6 = bf16[768,768]{1,0:T(8,128)(2,1)S(1)} copy-done((bf16[768,768]{1,0:T(8,128)(2,1)S(1)}, bf16[768,768]{1,0:T(8,128)(2,1)}, u32[]{:S(2)}) %copy-start.6) | copy-done | bytes 1179672
  16.1 2.5 %project.1 = bf16[16,4,48,256]{3,2,1,0:T(8,128)(2,1)} custom-call(bf16[4,64,768]{2,1,0:T(8,128)(2,1)S(1)} %copy-done.7, bf16[4,64,768]{2,1,0:T(8,128)(2,1)S(1)} %copy-done.8, bf16[768,768]{1,0:T(8,128)(2,1)S(1)} %copy-done, bf16[768,768]{1,0:T(8,128)(2,1)S(1)} %copy-done.1, bf16[768,768]{1,0:T(8,128)(2,1)S(1)} %copy-done.3, bf16[768,768]{1,0:T(8,128)(2,1)S(1)} %copy-done.6), custom_call_target="tpu_custom_call" | custom-call | tf_op jit(solution)/shard_map/project/pallas_call | solution.py:264
  18.6 8.0 %all-to-all-done = bf16[32,80,128]{2,1,0:T(8,128)(2,1)} async-done(((bf16[32,80,128]{2,1,0:T(8,128)(2,1)}), bf16[32,80,128]{2,1,0:T(8,128)(2,1)}, u32[]{:S(2)}, u32[]{:S(2)}) %all-to-all-start) | async-done | bytes 655392 | tf_op jit(solution)/shard_map/all_to_all | solution.py:294
  26.6 3.7 %all-to-all-start.1 = ((bf16[16,4,48,256]{3,2,1,0:T(8,128)(2,1)}), bf16[16,4,48,256]{3,2,1,0:T(8,128)(2,1)S(1)}, u32[]{:S(2)}, u32[]{:S(2)}) async-start(bf16[16,4,48,256]{3,2,1,0:T(8,128)(2,1)} %project.1), calls=%async_computation.1 | async-start | bytes 3145728 | tf_op jit(solution)/shard_map/all_to_all | solution.py:341
  30.3 1.1 slice_bitcast_fusion
  31.4 3.1 %collective-permute-start.3 = (bf16[16,80,128]{2,1,0:T(8,128)(2,1)S(1)}, bf16[16,80,128]{2,1,0:T(8,128)(2,1)}, u32[]{:S(2)}, u32[]{:S(2)}) collective-permute-start(bf16[16,80,128]{2,1,0:T(8,128)(2,1)S(1)} %get-tuple-element.42.refs_1_), channel_id=1, source_target_pairs={{0,96},{16,112},{32,0},{48,16},{64,32},{80,48},{96,64},{112,80},{1... | collective-permute-start | bytes 983048 | tf_op jit(solution)/shard_map/ppermute | solution.py:289
  34.5 0.0 collective-permute-start
  34.5 0.6 collective-permute-start.1
  35.1 2.7 %collective-permute-start.2 = (bf16[16,80,128]{2,1,0:T(8,128)(2,1)S(1)}, bf16[16,80,128]{2,1,0:T(8,128)(2,1)}, u32[]{:S(2)}, u32[]{:S(2)}) collective-permute-start(bf16[16,80,128]{2,1,0:T(8,128)(2,1)S(1)} %get-tuple-element.43.refs_0_), channel_id=1, source_target_pairs={{0,96},{16,112},{32,0},{48,16},{64,32},{80,48},{96,64},{112,80},{1... | collective-permute-start | bytes 983048 | tf_op jit(solution)/shard_map/ppermute | solution.py:289
  37.8 4.8 %collective-permute-done.3.refs_5_ = bf16[16,80,128]{2,1,0:T(8,128)(2,1)} collective-permute-done((bf16[16,80,128]{2,1,0:T(8,128)(2,1)S(1)}, bf16[16,80,128]{2,1,0:T(8,128)(2,1)}, u32[]{:S(2)}, u32[]{:S(2)}) %collective-permute-start.3) | collective-permute-done | bytes 327712 | tf_op jit(solution)/shard_map/ppermute | solution.py:289
  42.5 3.8 %collective-permute-start.5 = (bf16[16,80,128]{2,1,0:T(8,128)(2,1)}, bf16[16,80,128]{2,1,0:T(8,128)(2,1)}, u32[]{:S(2)}, u32[]{:S(2)}) collective-permute-start(bf16[16,80,128]{2,1,0:T(8,128)(2,1)} %collective-permute-done.3.refs_5_), channel_id=1, source_target_pairs={{0,96},{16,112},{32,0},{48,16},{64,32},{80,48},{96,64},{112,80},{1... | collective-permute-start | bytes 983048 | tf_op jit(solution)/shard_map/ppermute | solution.py:289
  46.3 0.0 collective-permute-done.refs_2_
  46.4 0.0 collective-permute-start.4
  46.4 0.1 stack.35.order_ref
  46.5 6.0 %all-to-all-done.1.r_ref = bf16[16,4,48,256]{3,2,1,0:T(8,128)(2,1)S(1)} async-done(((bf16[16,4,48,256]{3,2,1,0:T(8,128)(2,1)}), bf16[16,4,48,256]{3,2,1,0:T(8,128)(2,1)S(1)}, u32[]{:S(2)}, u32[]{:S(2)}) %all-to-all-start.1) | async-done | bytes 1572896 | tf_op jit(solution)/shard_map/all_to_all | solution.py:341
  52.5 2.8 %prep.1 = (bf16[4,1024,48]{2,1,0:T(8,128)(2,1)S(1)}, bf16[4,1024,48]{2,1,0:T(8,128)(2,1)S(1)}, bf16[4,48,1024]{2,1,0:T(8,128)(2,1)S(1)}, bf16[4,48,1024]{2,1,0:T...) custom-call(s32[8]{0:T(128)S(1)} %stack.35.order_ref, ...), custom_call_target="tpu_custom_call" | custom-call | tf_op jit(solution)/shard_map/prep/pallas_call | solution.py:47
  55.3 0.0 collective-permute-done.1.refs_3_
  55.3 0.7 collective-permute-done.5.refs_7_
  56.1 3.4 %collective-permute-done.4.refs_6_ = bf16[16,80,128]{2,1,0:T(8,128)(2,1)} collective-permute-done((bf16[16,80,128]{2,1,0:T(8,128)(2,1)}, bf16[16,80,128]{2,1,0:T(8,128)(2,1)}, u32[]{:S(2)}, u32[]{:S(2)}) %collective-permute-start.4) | collective-permute-done | bytes 327712 | tf_op jit(solution)/shard_map/ppermute | solution.py:289
  59.5 19.1 %attend.1 = (bf16[1024,128]{1,0:T(8,128)(2,1)}, bf16[1024,128]{1,0:T(8,128)(2,1)}, bf16[1024,128]{1,0:T(8,128)(2,1)}, bf16[1024,128]{1,0:T(8,128)(2,1)}, bf16[10...) custom-call(s32[8]{0:T(128)S(1)} %stack.35.order_ref, ...), custom_call_target="tpu_custom_call" | custom-call | flops 1000000 | bytes 1024 | tf_op jit(solution)/shard_map/attend/pallas_call | solution.py:156
  78.6 5.7 %all-to-all-start.2 = ((bf16[16,3,48,256]{3,2,1,0:T(8,128)(2,1)}), bf16[16,3,48,256]{3,2,1,0:T(8,128)(2,1)}, u32[]{:S(2)}, u32[]{:S(2)}) async-start(bf16[16,3,48,256]{3,2,1,0:T(8,128)(2,1)} %get-tuple-element.31), calls=%async_computation.2 | async-start | bytes 2359296 | tf_op jit(solution)/shard_map/all_to_all | solution.py:343
  84.3 0.0 copy-start.9
  84.4 0.1 collective-permute-start.6
  84.5 3.2 %collective-permute-start.10 = (bf16[1024,128]{1,0:T(8,128)(2,1)S(1)}, bf16[1024,128]{1,0:T(8,128)(2,1)S(1)}, u32[]{:S(2)}, u32[]{:S(2)}) collective-permute-start(bf16[1024,128]{1,0:T(8,128)(2,1)S(1)} %copy-done.15), channel_id=1, source_target_pairs={{0,96},{16,112},{32,0},{48,16},{64,32},{80,48},{96,64},{112,80},{1... | collective-permute-start | bytes 786440 | tf_op jit(solution)/shard_map/ppermute | solution.py:289
  87.7 0.1 collective-permute-start.8
  87.8 2.0 %collective-permute-start.9 = (bf16[1024,128]{1,0:T(8,128)(2,1)S(1)}, bf16[1024,128]{1,0:T(8,128)(2,1)S(1)}, u32[]{:S(2)}, u32[]{:S(2)}) collective-permute-start(bf16[1024,128]{1,0:T(8,128)(2,1)S(1)} %copy-done.13), channel_id=1, source_target_pairs={{0,32},{16,48},{32,64},{48,80},{64,96},{80,112},{96,0},{112,16},{1... | collective-permute-start | bytes 786440 | tf_op jit(solution)/shard_map/ppermute | solution.py:289
  89.7 5.1 %collective-permute-done.6 = bf16[1024,128]{1,0:T(8,128)(2,1)S(1)} collective-permute-done((bf16[1024,128]{1,0:T(8,128)(2,1)S(1)}, bf16[1024,128]{1,0:T(8,128)(2,1)S(1)}, u32[]{:S(2)}, u32[]{:S(2)}) %collective-permute-start.6) | collective-permute-done | bytes 262176 | tf_op jit(solution)/shard_map/ppermute | solution.py:289
  94.8 0.1 add_convert_fusion.1
  94.9 0.1 collective-permute-start.7
  95.0 0.1 add_convert_fusion
  95.0 3.3 %collective-permute-start.11 = (bf16[1024,128]{1,0:T(8,128)(2,1)S(1)}, bf16[1024,128]{1,0:T(8,128)(2,1)S(1)}, u32[]{:S(2)}, u32[]{:S(2)}) collective-permute-start(bf16[1024,128]{1,0:T(8,128)(2,1)S(1)} %add_convert_fusion), channel_id=1, source_target_pairs={{0,96},{16,112},{32,0},{48,16},{64,32},{80,48},{96,64},{112,80},{1... | collective-permute-start | bytes 786440 | tf_op jit(solution)/shard_map/ppermute | solution.py:289
  98.3 1.7 %collective-permute-done.8.c0 = bf16[1024,128]{1,0:T(8,128)(2,1)S(1)} collective-permute-done((bf16[1024,128]{1,0:T(8,128)(2,1)S(1)}, bf16[1024,128]{1,0:T(8,128)(2,1)S(1)}, u32[]{:S(2)}, u32[]{:S(2)}) %collective-permute-start.8) | collective-permute-done | bytes 262176 | tf_op jit(solution)/shard_map/ppermute | solution.py:289
  100.0 0.4 collective-permute-done.9.b1
  100.4 5.1 %collective-permute-done.7.b0 = bf16[1024,128]{1,0:T(8,128)(2,1)S(1)} collective-permute-done((bf16[1024,128]{1,0:T(8,128)(2,1)S(1)}, bf16[1024,128]{1,0:T(8,128)(2,1)S(1)}, u32[]{:S(2)}, u32[]{:S(2)}) %collective-permute-start.7) | collective-permute-done | bytes 262176 | tf_op jit(solution)/shard_map/ppermute | solution.py:289
  105.5 0.0 copy-start.2
  105.5 1.0 own_sum.1
  106.5 5.7 %all-to-all-start.3 = ((bf16[32,64,128]{2,1,0:T(8,128)(2,1)}), bf16[32,64,128]{2,1,0:T(8,128)(2,1)S(1)}, u32[]{:S(2)}, u32[]{:S(2)}) async-start(bf16[32,64,128]{2,1,0:T(8,128)(2,1)} %bitcast.11), calls=%async_computation.3 | async-start | bytes 1048576 | tf_op jit(solution)/shard_map/all_to_all | solution.py:294
  112.2 0.0 copy-start.4
  112.2 1.3 copy-done.4
  113.5 3.2 %final.1 = bf16[4,64,768]{2,1,0:T(8,128)(2,1)} custom-call(bf16[16,3,48,256]{3,2,1,0:T(8,128)(2,1)} %all-to-all-done.2.g_ref, bf16[768,768]{1,0:T(8,128)(2,1)S(1)} %copy-done, bf16[768,768]{1,0:T(8,128)(2,1)S(1)} %copy-done.2, bf16[768,768]{1,0:T(8,128)(2,1)S(1)} %copy-done.4), custom_call_target="tpu_custom_call" | custom-call | tf_op jit(solution)/shard_map/final/pallas_call | solution.py:281
  116.7 7.4 %all-to-all-done.3 = bf16[32,64,128]{2,1,0:T(8,128)(2,1)S(1)} async-done(((bf16[32,64,128]{2,1,0:T(8,128)(2,1)}), bf16[32,64,128]{2,1,0:T(8,128)(2,1)S(1)}, u32[]{:S(2)}, u32[]{:S(2)}) %all-to-all-start.3) | async-done | bytes 524320 | tf_op jit(solution)/shard_map/all_to_all | solution.py:294
  124.1 2.1 %gpair.1 = bf16[64,128,128]{2,1,0:T(8,128)(2,1)} custom-call(bf16[2,16,64,128]{3,2,1,0:T(8,128)(2,1)S(1)} %bitcast.15, bf16[128,16]{1,0:T(8,128)(2,1)S(1)} %copy.10.w_ref), custom_call_target="tpu_custom_call" | custom-call | tf_op jit(solution)/shard_map/gpair/pallas_call | solution.py:243
  (30 shorter events, 0.1 us)
Async XLA Ops:
  1.4 1.6 %copy-start.5 = (bf16[64,128,128]{2,1,0:T(8,128)(2,1)S(1)}, bf16[64,128,128]{2,1,0:T(8,128)(2,1)}, u32[]{:S(2)}) copy-start(bf16[64,128,128]{2,1,0:T(8,128)(2,1)} %pair_ref.1) | copy-start | bytes 6291460
  3.0 10.4 %copy-start.1 = (bf16[768,768]{1,0:T(8,128)(2,1)S(1)}, bf16[768,768]{1,0:T(8,128)(2,1)}, u32[]{:S(2)}) copy-start(bf16[768,768]{1,0:T(8,128)(2,1)} %wk_ref.3) | copy-start | bytes 3538948
  3.0 10.5 %copy-start.7 = (bf16[4,64,768]{2,1,0:T(8,128)(2,1)S(1)}, bf16[4,64,768]{2,1,0:T(8,128)(2,1)}, u32[]{:S(2)}) copy-start(bf16[4,64,768]{2,1,0:T(8,128)(2,1)} %x_ref.1) | copy-start | bytes 1179652
  3.0 10.5 %copy-start.8 = (bf16[4,64,768]{2,1,0:T(8,128)(2,1)S(1)}, bf16[4,64,768]{2,1,0:T(8,128)(2,1)}, u32[]{:S(2)}) copy-start(bf16[4,64,768]{2,1,0:T(8,128)(2,1)} %c_ref.1) | copy-start | bytes 1179652
  5.0 8.5 %copy-start = (bf16[768,768]{1,0:T(8,128)(2,1)S(1)}, bf16[768,768]{1,0:T(8,128)(2,1)}, u32[]{:S(2)}) copy-start(bf16[768,768]{1,0:T(8,128)(2,1)} %wq_ref.3) | copy-start | bytes 3538948
  5.0 21.6 %all-to-all-start = ((bf16[32,80,128]{2,1,0:T(8,128)(2,1)}), bf16[32,80,128]{2,1,0:T(8,128)(2,1)}, u32[]{:S(2)}, u32[]{:S(2)}) async-start(bf16[32,80,128]{2,1,0:T(8,128)(2,1)} %bias_part.1), calls=%async_computation | async-start | bytes 1310720 | tf_op jit(solution)/shard_map/all_to_all | solution.py:294
  13.5 1.3 %copy-start.3 = (bf16[768,768]{1,0:T(8,128)(2,1)S(1)}, bf16[768,768]{1,0:T(8,128)(2,1)}, u32[]{:S(2)}) copy-start(bf16[768,768]{1,0:T(8,128)(2,1)} %wv_ref.3) | copy-start | bytes 3538948
  14.8 1.3 %copy-start.6 = (bf16[768,768]{1,0:T(8,128)(2,1)S(1)}, bf16[768,768]{1,0:T(8,128)(2,1)}, u32[]{:S(2)}) copy-start(bf16[768,768]{1,0:T(8,128)(2,1)} %wo_ref.1) | copy-start | bytes 3538948
  26.6 26.0 %all-to-all-start.1 = ((bf16[16,4,48,256]{3,2,1,0:T(8,128)(2,1)}), bf16[16,4,48,256]{3,2,1,0:T(8,128)(2,1)S(1)}, u32[]{:S(2)}, u32[]{:S(2)}) async-start(bf16[16,4,48,256]{3,2,1,0:T(8,128)(2,1)} %project.1), calls=%async_computation.1 | async-start | bytes 3145728 | tf_op jit(solution)/shard_map/all_to_all | solution.py:341
  31.4 11.2 %collective-permute-start.3 = (bf16[16,80,128]{2,1,0:T(8,128)(2,1)S(1)}, bf16[16,80,128]{2,1,0:T(8,128)(2,1)}, u32[]{:S(2)}, u32[]{:S(2)}) collective-permute-start(bf16[16,80,128]{2,1,0:T(8,128)(2,1)S(1)} %get-tuple-element.42.refs_1_), channel_id=1, source_target_pairs={{0,96},{16,112},{32,0},{48,16},{64,32},{80,48},{96,64},{112,80},{1... | collective-permute-start | bytes 983048 | tf_op jit(solution)/shard_map/ppermute | solution.py:289
  34.5 11.9 %collective-permute-start = (bf16[16,80,128]{2,1,0:T(8,128)(2,1)S(1)}, bf16[16,80,128]{2,1,0:T(8,128)(2,1)}, u32[]{:S(2)}, u32[]{:S(2)}) collective-permute-start(bf16[16,80,128]{2,1,0:T(8,128)(2,1)S(1)} %get-tuple-element.43.refs_0_), channel_id=1, source_target_pairs={{0,32},{16,48},{32,64},{48,80},{64,96},{80,112},{96,0},{112,16},{1... | collective-permute-start | bytes 983048 | tf_op jit(solution)/shard_map/ppermute | solution.py:289
  34.5 20.8 %collective-permute-start.1 = (bf16[16,80,128]{2,1,0:T(8,128)(2,1)S(1)}, bf16[16,80,128]{2,1,0:T(8,128)(2,1)}, u32[]{:S(2)}, u32[]{:S(2)}) collective-permute-start(bf16[16,80,128]{2,1,0:T(8,128)(2,1)S(1)} %get-tuple-element.42.refs_1_), channel_id=1, source_target_pairs={{0,32},{16,48},{32,64},{48,80},{64,96},{80,112},{96,0},{112,16},{1... | collective-permute-start | bytes 983048 | tf_op jit(solution)/shard_map/ppermute | solution.py:289
  35.1 20.3 %collective-permute-start.2 = (bf16[16,80,128]{2,1,0:T(8,128)(2,1)S(1)}, bf16[16,80,128]{2,1,0:T(8,128)(2,1)}, u32[]{:S(2)}, u32[]{:S(2)}) collective-permute-start(bf16[16,80,128]{2,1,0:T(8,128)(2,1)S(1)} %get-tuple-element.43.refs_0_), channel_id=1, source_target_pairs={{0,96},{16,112},{32,0},{48,16},{64,32},{80,48},{96,64},{112,80},{1... | collective-permute-start | bytes 983048 | tf_op jit(solution)/shard_map/ppermute | solution.py:289
  42.5 13.5 %collective-permute-start.5 = (bf16[16,80,128]{2,1,0:T(8,128)(2,1)}, bf16[16,80,128]{2,1,0:T(8,128)(2,1)}, u32[]{:S(2)}, u32[]{:S(2)}) collective-permute-start(bf16[16,80,128]{2,1,0:T(8,128)(2,1)} %collective-permute-done.3.refs_5_), channel_id=1, source_target_pairs={{0,96},{16,112},{32,0},{48,16},{64,32},{80,48},{96,64},{112,80},{1... | collective-permute-start | bytes 983048 | tf_op jit(solution)/shard_map/ppermute | solution.py:289
  46.4 13.1 %collective-permute-start.4 = (bf16[16,80,128]{2,1,0:T(8,128)(2,1)}, bf16[16,80,128]{2,1,0:T(8,128)(2,1)}, u32[]{:S(2)}, u32[]{:S(2)}) collective-permute-start(bf16[16,80,128]{2,1,0:T(8,128)(2,1)} %collective-permute-done.refs_2_), channel_id=1, source_target_pairs={{0,32},{16,48},{32,64},{48,80},{64,96},{80,112},{96,0},{112,16},{1... | collective-permute-start | bytes 983048 | tf_op jit(solution)/shard_map/ppermute | solution.py:289
  78.6 5.8 %copy-start.16 = (bf16[1024,128]{1,0:T(8,128)(2,1)S(1)}, bf16[1024,128]{1,0:T(8,128)(2,1)}, u32[]{:S(2)}) copy-start(bf16[1024,128]{1,0:T(8,128)(2,1)} %get-tuple-element.34) | copy-start | bytes 786436
  78.6 5.9 %copy-start.15 = (bf16[1024,128]{1,0:T(8,128)(2,1)S(1)}, bf16[1024,128]{1,0:T(8,128)(2,1)}, u32[]{:S(2)}) copy-start(bf16[1024,128]{1,0:T(8,128)(2,1)} %get-tuple-element.39) | copy-start | bytes 786436
  78.6 9.1 %copy-start.14 = (bf16[1024,128]{1,0:T(8,128)(2,1)S(1)}, bf16[1024,128]{1,0:T(8,128)(2,1)}, u32[]{:S(2)}) copy-start(bf16[1024,128]{1,0:T(8,128)(2,1)} %get-tuple-element.35) | copy-start | bytes 786436
  78.6 9.2 %copy-start.13 = (bf16[1024,128]{1,0:T(8,128)(2,1)S(1)}, bf16[1024,128]{1,0:T(8,128)(2,1)}, u32[]{:S(2)}) copy-start(bf16[1024,128]{1,0:T(8,128)(2,1)} %get-tuple-element.37) | copy-start | bytes 786436
  78.6 16.2 %copy-start.12 = (bf16[1024,128]{1,0:T(8,128)(2,1)S(1)}, bf16[1024,128]{1,0:T(8,128)(2,1)}, u32[]{:S(2)}) copy-start(bf16[1024,128]{1,0:T(8,128)(2,1)} %get-tuple-element.33) | copy-start | bytes 786436
  78.6 16.3 %copy-start.11 = (bf16[1024,128]{1,0:T(8,128)(2,1)S(1)}, bf16[1024,128]{1,0:T(8,128)(2,1)}, u32[]{:S(2)}) copy-start(bf16[1024,128]{1,0:T(8,128)(2,1)} %get-tuple-element.38) | copy-start | bytes 786436
  78.6 27.8 %all-to-all-start.2 = ((bf16[16,3,48,256]{3,2,1,0:T(8,128)(2,1)}), bf16[16,3,48,256]{3,2,1,0:T(8,128)(2,1)}, u32[]{:S(2)}, u32[]{:S(2)}) async-start(bf16[16,3,48,256]{3,2,1,0:T(8,128)(2,1)} %get-tuple-element.31), calls=%async_computation.2 | async-start | bytes 2359296 | tf_op jit(solution)/shard_map/all_to_all | solution.py:343
  84.3 21.1 %copy-start.9 = (bf16[1024,128]{1,0:T(8,128)(2,1)S(1)}, bf16[1024,128]{1,0:T(8,128)(2,1)}, u32[]{:S(2)}) copy-start(bf16[1024,128]{1,0:T(8,128)(2,1)} %get-tuple-element.32.a0) | copy-start | bytes 786436
  84.3 21.1 %copy-start.10 = (bf16[1024,128]{1,0:T(8,128)(2,1)S(1)}, bf16[1024,128]{1,0:T(8,128)(2,1)}, u32[]{:S(2)}) copy-start(bf16[1024,128]{1,0:T(8,128)(2,1)} %get-tuple-element.36.a1) | copy-start | bytes 786436
  84.4 10.4 %collective-permute-start.6 = (bf16[1024,128]{1,0:T(8,128)(2,1)S(1)}, bf16[1024,128]{1,0:T(8,128)(2,1)S(1)}, u32[]{:S(2)}, u32[]{:S(2)}) collective-permute-start(bf16[1024,128]{1,0:T(8,128)(2,1)S(1)} %copy-done.16), channel_id=1, source_target_pairs={{0,32},{16,48},{32,64},{48,80},{64,96},{80,112},{96,0},{112,16},{1... | collective-permute-start | bytes 786440 | tf_op jit(solution)/shard_map/ppermute | solution.py:289
  84.5 10.5 %collective-permute-start.10 = (bf16[1024,128]{1,0:T(8,128)(2,1)S(1)}, bf16[1024,128]{1,0:T(8,128)(2,1)S(1)}, u32[]{:S(2)}, u32[]{:S(2)}) collective-permute-start(bf16[1024,128]{1,0:T(8,128)(2,1)S(1)} %copy-done.15), channel_id=1, source_target_pairs={{0,96},{16,112},{32,0},{48,16},{64,32},{80,48},{96,64},{112,80},{1... | collective-permute-start | bytes 786440 | tf_op jit(solution)/shard_map/ppermute | solution.py:289
  87.7 12.3 %collective-permute-start.8 = (bf16[1024,128]{1,0:T(8,128)(2,1)S(1)}, bf16[1024,128]{1,0:T(8,128)(2,1)S(1)}, u32[]{:S(2)}, u32[]{:S(2)}) collective-permute-start(bf16[1024,128]{1,0:T(8,128)(2,1)S(1)} %copy-done.14), channel_id=1, source_target_pairs={{0,96},{16,112},{32,0},{48,16},{64,32},{80,48},{96,64},{112,80},{1... | collective-permute-start | bytes 786440 | tf_op jit(solution)/shard_map/ppermute | solution.py:289
  87.8 12.6 %collective-permute-start.9 = (bf16[1024,128]{1,0:T(8,128)(2,1)S(1)}, bf16[1024,128]{1,0:T(8,128)(2,1)S(1)}, u32[]{:S(2)}, u32[]{:S(2)}) collective-permute-start(bf16[1024,128]{1,0:T(8,128)(2,1)S(1)} %copy-done.13), channel_id=1, source_target_pairs={{0,32},{16,48},{32,64},{48,80},{64,96},{80,112},{96,0},{112,16},{1... | collective-permute-start | bytes 786440 | tf_op jit(solution)/shard_map/ppermute | solution.py:289
  94.9 10.6 %collective-permute-start.7 = (bf16[1024,128]{1,0:T(8,128)(2,1)S(1)}, bf16[1024,128]{1,0:T(8,128)(2,1)S(1)}, u32[]{:S(2)}, u32[]{:S(2)}) collective-permute-start(bf16[1024,128]{1,0:T(8,128)(2,1)S(1)} %add_convert_fusion.1), channel_id=1, source_target_pairs={{0,32},{16,48},{32,64},{48,80},{64,96},{80,112},{96,0},{112,16},{1... | collective-permute-start | bytes 786440 | tf_op jit(solution)/shard_map/ppermute | solution.py:289
  95.0 10.4 %collective-permute-start.11 = (bf16[1024,128]{1,0:T(8,128)(2,1)S(1)}, bf16[1024,128]{1,0:T(8,128)(2,1)S(1)}, u32[]{:S(2)}, u32[]{:S(2)}) collective-permute-start(bf16[1024,128]{1,0:T(8,128)(2,1)S(1)} %add_convert_fusion), channel_id=1, source_target_pairs={{0,96},{16,112},{32,0},{48,16},{64,32},{80,48},{96,64},{112,80},{1... | collective-permute-start | bytes 786440 | tf_op jit(solution)/shard_map/ppermute | solution.py:289
  105.5 6.8 %copy-start.2 = (bf16[768,768]{1,0:T(8,128)(2,1)S(1)}, bf16[768,768]{1,0:T(8,128)(2,1)}, u32[]{:S(2)}) copy-start(bf16[768,768]{1,0:T(8,128)(2,1)} %wk_ref.3) | copy-start | bytes 3538948
  106.5 17.6 %all-to-all-start.3 = ((bf16[32,64,128]{2,1,0:T(8,128)(2,1)}), bf16[32,64,128]{2,1,0:T(8,128)(2,1)S(1)}, u32[]{:S(2)}, u32[]{:S(2)}) async-start(bf16[32,64,128]{2,1,0:T(8,128)(2,1)} %bitcast.11), calls=%async_computation.3 | async-start | bytes 1048576 | tf_op jit(solution)/shard_map/all_to_all | solution.py:294
  112.2 1.3 %copy-start.4 = (bf16[768,768]{1,0:T(8,128)(2,1)S(1)}, bf16[768,768]{1,0:T(8,128)(2,1)}, u32[]{:S(2)}) copy-start(bf16[768,768]{1,0:T(8,128)(2,1)} %wv_ref.3) | copy-start | bytes 3538948

commit v5 on v4

--- a/solution.py
+++ b/solution.py
@@ -16,27 +16,20 @@
 TOK = 1024
 
 
-def prep_body(order_ref, r_ref, q_ref, o_ref, qt_ref, ot_ref, kt_ref, vt_ref, k_ref):
+def prep_body(order_ref, r_ref, qt_ref, ot_ref, kt_ref, vt_ref, k_ref):
     def piece(slot, first, sample):
         lanes = slice(sample * 64, sample * 64 + 64)
         return jnp.concatenate([r_ref[first, slot, :, lanes], r_ref[first + 1, slot, :, lanes]], axis=1)
-
-    def turned(block):
-        return block.astype(F32).T.astype(BF16)
 
     for u in range(8):
         cols = slice(u * 128, u * 128 + 128)
         other = order_ref[u] * 2
         for b in range(NB):
-            qt = piece(0, 2 * u, b)
-            qt_ref[b, :, cols] = qt
-            q_ref[b, cols, :] = turned(qt)
-            ot = piece(3, 2 * u, b)
-            ot_ref[b, :, cols] = ot
-            o_ref[b, cols, :] = turned(ot)
+            qt_ref[b, :, cols] = piece(0, 2 * u, b)
+            ot_ref[b, :, cols] = piece(3, 2 * u, b)
             kt = piece(1, other, b)
             kt_ref[b, :, cols] = kt
-            k_ref[b, cols, :] = turned(kt)
+            k_ref[b, cols, :] = kt.astype(F32).T.astype(BF16)
             vt_ref[b, :, cols] = piece(2, other, b)
 
 
@@ -46,9 +39,9 @@
     vm = pl.BlockSpec(memory_space=pltpu.VMEM)
     return pl.pallas_call(
         prep_body,
-        out_shape=[nat, nat, tr, tr, tr, tr, nat],
+        out_shape=[tr, tr, tr, tr, nat],
         in_specs=[pl.BlockSpec(memory_space=pltpu.SMEM), vm],
-        out_specs=[vm] * 7,
+        out_specs=[vm] * 5,
         compiler_params=pltpu.CompilerParams(vmem_limit_bytes=32 * 2**20),
         name="prep",
     )(order, received)
@@ -58,14 +51,45 @@
 VMEM_ATT = 40
 NEAR = 8.0
 STEEP = 18.8
+EARLY, LATE = (0, 1, 2, 5), (3, 4, 6, 7)
+
+
+def decode_rows(codes, every, group):
+    tops = every[:8]
+    for n in range(1, 4):
+        tops = jnp.where(group == n, every[n * 8:n * 8 + 8], tops)
+    tops = jnp.broadcast_to(tops[:, None, :], (8, 8, 128)).reshape(64, 128)
+    for t in range(4):
+        top = jnp.sum(jnp.where(marks(64, t * 32)[1], tops, 0.0), axis=1, keepdims=True)
+        yield t * 64, decode(codes[t * 64:t * 64 + 64, :], top)
+
+
+def early_body(*refs):
+    count = len(refs) // 3
+    for n in range(count):
+        every = refs[count + n][...].astype(F32)
+        for at, block in decode_rows(refs[n], every, pl.program_id(0)):
+            refs[2 * count + n][at:at + 64, :] = block
+
+
+def early(blocks):
+    code_t = pl.BlockSpec((TILE, 128), lambda i: (i, 0))
+    top_t = pl.BlockSpec((32, 128), lambda i: (TOK // 32, 0))
+    count = len(blocks)
+    return pl.pallas_call(
+        early_body, grid=(TOK // TILE,), out_shape=[pltpu.HBM((TOK, 128), F32)] * count,
+        in_specs=[code_t] * count + [top_t] * count, out_specs=[code_t] * count,
+        compiler_params=pltpu.CompilerParams(vmem_limit_bytes=16 * 2**20), name="early",
+    )(*blocks, *blocks)
 
 
 def attend_body(scale, steps, order_ref, *refs):
-    bias_refs, refs = refs[:8], refs[8:]
-    (q_ref, o_ref, qt_ref, ot_ref, kt_ref, vt_ref, k_ref), refs = refs[:7], refs[7:]
+    early_refs, code_refs, top_refs, refs = refs[:4], refs[4:8], refs[8:12], refs[12:]
+    (qt_ref, ot_ref, kt_ref, vt_ref, k_ref), refs = refs[:5], refs[5:]
     dbias_refs, refs = refs[:8], refs[8:]
     g_ref, s_ref, dp_ref, p_ref, ds_ref, acc_ref, dqt_ref, dkt_ref, dvt_ref, bias_scr = refs
     step = pl.program_id(0)
+    here = pl.ds(pl.multiple_of(step * TILE, TILE), TILE)
 
     @pl.when(step == 0)
     def _():
@@ -73,23 +97,23 @@
         dvt_ref[...] = jnp.zeros_like(dvt_ref)
 
     def all_bias():
-        mark = marks(64)[1]
-        for t in range(TILE // 64):
-            for u in range(8):
-                tops = bias_refs[u][t, 64:80].astype(F32)[:8]
-                tops = jnp.broadcast_to(tops[:, None, :], (8, 8, 128)).reshape(64, 128)
-                top = jnp.sum(jnp.where(mark, tops, 0.0), axis=1, keepdims=True)
-                bias_scr[t * 64:t * 64 + 64, u * 128:u * 128 + 128] = decode(bias_refs[u][t, :64], top)
+        for n in range(4):
+            for at, block in decode_rows(code_refs[n], top_refs[n][...].astype(F32), step):
+                bias_scr[at:at + 64, n * 128:n * 128 + 128] = block
 
     def products(b):
-        s_ref[b % 2] = jnp.dot(q_ref[b], kt_ref[b], preferred_element_type=F32)
-        dp_ref[b % 2] = jnp.dot(o_ref[b], vt_ref[b], preferred_element_type=F32)
+        first = (((0,), (0,)), ((), ()))
+        s_ref[b % 2] = lax.dot_general(qt_ref[b, :, here], kt_ref[b], first, preferred_element_type=F32)
+        dp_ref[b % 2] = lax.dot_general(ot_ref[b, :, here], vt_ref[b], first, preferred_element_type=F32)
 
     def softmax(b):
         group = 16
         for g in range(TILE // group):
             rows = slice(g * group, g * group + group)
-            s = s_ref[b % 2, rows, :] * (scale * LOG2E) + bias_scr[rows, :]
+            late = [bias_scr[rows, n * 128:n * 128 + 128] for n in range(4)]
+            held = dict(zip(EARLY + LATE, [ref[rows, :] for ref in early_refs] + late))
+            bias = jnp.concatenate([held[u] for u in range(8)], axis=1)
+            s = s_ref[b % 2, rows, :] * (scale * LOG2E) + bias
             m = jnp.max(s, axis=1, keepdims=True)
             e = jnp.exp2(s - m)
             inv = 1.0 / jnp.sum(e, axis=1, keepdims=True)
@@ -110,8 +134,8 @@
 
     def gradients(b):
         p_low, ds_low = p_ref[b % 2], ds_ref[b % 2]
-        dkt_ref[b] += jnp.dot(qt_ref[b], ds_low, preferred_element_type=F32)
-        dvt_ref[b] += jnp.dot(ot_ref[b], p_low, preferred_element_type=F32)
+        dkt_ref[b] += jnp.dot(qt_ref[b, :, here], ds_low, preferred_element_type=F32)
+        dvt_ref[b] += jnp.dot(ot_ref[b, :, here], p_low, preferred_element_type=F32)
         dq = jnp.dot(ds_low, k_ref[b], preferred_element_type=F32)
         dqt_ref[step, b] = (dq * scale).T.astype(BF16)
 
@@ -143,32 +167,29 @@
                 g_ref[first + 1, 2, :, lanes] = dv[:, 64:]
 
 
-def attend(order, bias, held):
+def attend(order, ready, bias, held):
     steps = TOK // TILE
     scale = 1.0 / math.sqrt(HD)
-    nat_t = pl.BlockSpec((NB, TILE, HD), lambda i: (0, i, 0))
-    tr_t = pl.BlockSpec((NB, HD, TILE), lambda i: (0, 0, i))
-    tr_w = pl.BlockSpec((NB, HD, TOK), lambda i: (0, 0, 0))
-    nat_w = pl.BlockSpec((NB, TOK, HD), lambda i: (0, 0, 0))
+    vm = pl.BlockSpec(memory_space=pltpu.VMEM)
     dbias_t = pl.BlockSpec((TILE, 128), lambda i: (i, 0))
-    one_t = pl.BlockSpec((TILE // 64, 80, 128), lambda i: (i, 0, 0))
+    top_t = pl.BlockSpec((32, 128), lambda i: (TOK // 32, 0))
     g_spec = pl.BlockSpec((16, 3, HD, 256), lambda i: (0, 0, 0, 0))
     outs = pl.pallas_call(
         functools.partial(attend_body, scale, steps),
         grid=(steps,),
         out_shape=[pltpu.HBM((TOK, 128), BF16)] * 8 + [jax.ShapeDtypeStruct((16, 3, HD, 256), BF16)],
-        in_specs=[pl.BlockSpec(memory_space=pltpu.SMEM)] + [one_t] * 8 + [nat_t, nat_t, tr_t, tr_t, tr_w, tr_w, nat_w],
+        in_specs=[pl.BlockSpec(memory_space=pltpu.SMEM)] + [dbias_t] * 8 + [top_t] * 4 + [vm] * 5,
         out_specs=[dbias_t] * 8 + [g_spec],
         scratch_shapes=[
             pltpu.VMEM((2, TILE, TOK), F32), pltpu.VMEM((2, TILE, TOK), F32),
             pltpu.VMEM((2, TILE, TOK), BF16), pltpu.VMEM((2, TILE, TOK), BF16),
             pltpu.VMEM((TILE, TOK), F32), pltpu.VMEM((steps, NB, HD, TILE), BF16),
-            pltpu.VMEM((NB, HD, TOK), F32), pltpu.VMEM((NB, HD, TOK), F32), pltpu.VMEM((TILE, TOK), F32),
+            pltpu.VMEM((NB, HD, TOK), F32), pltpu.VMEM((NB, HD, TOK), F32), pltpu.VMEM((TILE, 512), F32),
         ],
         compiler_params=pltpu.CompilerParams(vmem_limit_bytes=VMEM_ATT * 2**20),
         cost_estimate=pl.CostEstimate(flops=10**6, bytes_accessed=2**10, transcendentals=0),
         name="attend",
-    )(order, *bias, *held)
+    )(order, *[pltpu.with_memory_space_constraint(v, pltpu.HBM) for v in ready], *bias, *bias, *held)
     return outs[:8], outs[8]
 
 
@@ -188,15 +209,15 @@
     return (top + NEAR) - NEAR * jnp.exp2((126.0 - jnp.log2(code.astype(F32))) * (1.0 / STEEP))
 
 
-def marks(count):
-    lane = lax.broadcasted_iota(jnp.int32, (count, 128), 1)
+def marks(count, start):
+    lane = lax.broadcasted_iota(jnp.int32, (count, 128), 1) - start
     row = lax.broadcasted_iota(jnp.int32, (count, 128), 0)
-    return lane, (lane < 24) & (lane % 8 == row % 8)
+    return lane, (lane >= 0) & (lane < 24) & (lane % 8 == row % 8)
 
 
 def bias_body(pair_ref, w_ref, out_ref):
     w = block_diagonal(w_ref, 8)
-    lane, mark = marks(128)
+    lane, mark = marks(128, 0)
     tops = []
     for g in range(8):
         cols = jnp.concatenate([pair_ref[g * 8 + r] for r in range(8)], axis=1)
@@ -228,6 +249,25 @@
     )(pair, w_pair)
 
 
+def unpack_body(x_ref, *out_refs):
+    for e in range(2):
+        for t in range(16):
+            out_refs[e][t * 64:t * 64 + 64, :] = x_ref[e, t, :64]
+        groups = []
+        for group in range(4):
+            tops = [x_ref[e, group * 4 + n, 64:80].astype(F32)[:8, :32] for n in range(4)]
+            groups.append(jnp.concatenate(tops, axis=1))
+        out_refs[e][TOK:TOK + 32, :] = jnp.concatenate(groups, axis=0).astype(BF16)
+
+
+def unpack(x):
+    vm = pl.BlockSpec(memory_space=pltpu.VMEM)
+    return pl.pallas_call(
+        unpack_body, out_shape=[jax.ShapeDtypeStruct((TOK + 32, 128), BF16)] * 2, in_specs=[vm], out_specs=[vm] * 2,
+        compiler_params=pltpu.CompilerParams(vmem_limit_bytes=16 * 2**20), name="unpack",
+    )(x)
+
+
 def gpair_body(x_ref, w_ref, out_ref):
     w = block_diagonal(w_ref, 16)
     for g in range(4):
@@ -336,10 +376,12 @@
 def local(single, pair, w_query, w_key, w_value, w_out, w_pair, cotangent):
     order = key_order()
     sent = project(single, cotangent, w_query, w_key, w_value, w_out)
-    bias = exchange(bias_part(pair, w_pair)).reshape(2, 16, 80, 128)
+    bias = exchange(bias_part(pair, w_pair))
     bias, sent = lax.optimization_barrier((bias, sent))
     received = lax.all_to_all(sent, "tok", 0, 0)
-    dbias, grads = attend(order, gather_blocks(bias), prep(order, received))
+    blocks = gather_blocks(unpack(bias.reshape(2, 16, 80, 128)))
+    received, ready = lax.optimization_barrier((received, early([blocks[u] for u in EARLY])))
+    dbias, grads = attend(order, ready, [blocks[u] for u in LATE], prep(order, received))
     grads = lax.all_to_all(grads, "tok", 0, 0)
     dbias = scatter_blocks(dbias)
     grads, dbias = lax.optimization_barrier((grads, dbias))

time: 128 us -> 120 us (0.938)
  waiting for transfers between devices: 42.6 us -> 34.6 us
  starting transfers between devices: 42.5 us -> 39.6 us
  local copies, waits for them, and re-layouts: 7.46 us -> 9.16 us
  Pallas kernels: 32.7 us -> 34.2 us
    pallas_call x1 -> x3, Pallas kernels: 2.8 us -> 6.31 us  [the longest x1 3.8 us: early(): pl.pallas_call(early_body, grid=(TOK // TILE,), out_shape=[pltpu.HBM((TOK...]
    ppermute x12, waiting for transfers between devices: 21.2 us -> 17.9 us  [shift_y(): lax.ppermute(x, 'sample', [(i, (i // 2 + d) % 4 * 2 + i % 2) for i in ran...]
    unnamed x35 -> x37, local copies, waits for them, and re-layouts: 6.25 us -> 9.08 us
    all_to_all x1, waiting for transfers between devices: 6.04 us -> 3.37 us  [local(): received = lax.all_to_all(sent, 'tok', 0, 0)]
    all_to_all x2, waiting for transfers between devices: 15.4 us -> 13.4 us  [exchange(): return lax.all_to_all(x, ('sample', 'tok'), 0, 0, axis_index_groups=groups)]
    ppermute x12, starting transfers between devices: 18.8 us -> 17.2 us  [shift_y(): lax.ppermute(x, 'sample', [(i, (i // 2 + d) % 4 * 2 + i % 2) for i in ran...]
  transfers between devices with their start and end apart: 16 -> 16, of which waited for: 10 -> 8; matrix products, arithmetic and copies ran while one was open for 1% -> 0% of each run, Pallas kernels for 8% -> 11%
where the time goes in v5:
time: 120 us; the launch traced here: 119 us
  starting transfers between devices  39.6 us (33%)
  waiting for transfers between devices  34.6 us (29%)
  Pallas kernels  34.2 us (29%)
  local copies, waits for them, and re-layouts  9.16 us (8%)
    pallas_call x1, Pallas kernels, attend(): pl.pallas_call(functools.partial(attend_body, scale, steps), grid=(steps,...  18 us
    ppermute x12, waiting for transfers between devices, shift_y(): lax.ppermute(x, 'sample', [(i, (i // 2 + d) % 4 * 2 + i % 2) for i in ran...  17.9 us
    ppermute x12, starting transfers between devices, shift_y(): lax.ppermute(x, 'sample', [(i, (i // 2 + d) % 4 * 2 + i % 2) for i in ran...  17.2 us
    all_to_all x2, starting transfers between devices, exchange(): return lax.all_to_all(x, ('sample', 'tok'), 0, 0, axis_index_groups=groups)  14.1 us
    all_to_all x2, waiting for transfers between devices, exchange(): return lax.all_to_all(x, ('sample', 'tok'), 0, 0, axis_index_groups=groups)  13.4 us
    unnamed x37, local copies, waits for them, and re-layouts  9.08 us
    all_to_all x1, starting transfers between devices, local(): grads = lax.all_to_all(grads, 'tok', 0, 0)  4.54 us
    pallas_call x1, Pallas kernels, early(): pl.pallas_call(early_body, grid=(TOK // TILE,), out_shape=[pltpu.HBM((TOK...  3.8 us
  transfers between devices with their start and end apart: 16, of which 8 were waited for; matrix products, arithmetic and copies ran while one was open for 0% of the time, Pallas kernels for 11%

profile of v5, /device:TPU:0, one launch (start us, length us, event | category | flops | bytes accessed | tf_op | source)
XLA Modules:
  0.0 118.6 jit_solution(220980199888420707)
XLA Ops:
  0.6 0.8 copy.10.w_ref
  1.4 1.6 %copy-done.6 = bf16[64,128,128]{2,1,0:T(8,128)(2,1)S(1)} copy-done((bf16[64,128,128]{2,1,0:T(8,128)(2,1)S(1)}, bf16[64,128,128]{2,1,0:T(8,128)(2,1)}, u32[]{:S(2)}) %copy-start.6) | copy-done | bytes 2097176
  3.0 1.1 bias_part.1
  4.1 0.8 copy-done.5
  5.0 8.4 %all-to-all-start = ((bf16[32,80,128]{2,1,0:T(8,128)(2,1)}), bf16[32,80,128]{2,1,0:T(8,128)(2,1)S(1)}, u32[]{:S(2)}, u32[]{:S(2)}) async-start(bf16[32,80,128]{2,1,0:T(8,128)(2,1)} %copy-done.5), calls=%async_computation | async-start | bytes 1310720 | tf_op jit(solution)/shard_map/all_to_all | solution.py:334
  13.4 0.0 copy-start.3
  13.4 1.3 %copy-done.3 = bf16[768,768]{1,0:T(8,128)(2,1)S(1)} copy-done((bf16[768,768]{1,0:T(8,128)(2,1)S(1)}, bf16[768,768]{1,0:T(8,128)(2,1)}, u32[]{:S(2)}) %copy-start.3) | copy-done | bytes 1179672
  14.6 1.3 %copy-done.7 = bf16[768,768]{1,0:T(8,128)(2,1)S(1)} copy-done((bf16[768,768]{1,0:T(8,128)(2,1)S(1)}, bf16[768,768]{1,0:T(8,128)(2,1)}, u32[]{:S(2)}) %copy-start.7) | copy-done | bytes 1179672
  15.9 1.0 copy-done.8
  16.9 1.0 copy-done.9
  17.9 2.5 %project.1 = bf16[16,4,48,256]{3,2,1,0:T(8,128)(2,1)} custom-call(bf16[4,64,768]{2,1,0:T(8,128)(2,1)S(1)} %copy-done.8, bf16[4,64,768]{2,1,0:T(8,128)(2,1)S(1)} %copy-done.9, bf16[768,768]{1,0:T(8,128)(2,1)S(1)} %copy-done, bf16[768,768]{1,0:T(8,128)(2,1)S(1)} %copy-done.1, bf16[768,768]{1,0:T(8,128)(2,1)S(1)} %copy-done.3, bf16[768,768]{1,0:T(8,128)(2,1)S(1)} %copy-done.7), custom_call_target="tpu_custom_call" | custom-call | tf_op jit(solution)/shard_map/project/pallas_call | solution.py:304
  20.4 6.0 %all-to-all-done = bf16[32,80,128]{2,1,0:T(8,128)(2,1)S(1)} async-done(((bf16[32,80,128]{2,1,0:T(8,128)(2,1)}), bf16[32,80,128]{2,1,0:T(8,128)(2,1)S(1)}, u32[]{:S(2)}, u32[]{:S(2)}) %all-to-all-start) | async-done | bytes 655392 | tf_op jit(solution)/shard_map/all_to_all | solution.py:334
  26.4 3.7 %all-to-all-start.1 = ((bf16[16,4,48,256]{3,2,1,0:T(8,128)(2,1)}), bf16[16,4,48,256]{3,2,1,0:T(8,128)(2,1)S(1)}, u32[]{:S(2)}, u32[]{:S(2)}) async-start(bf16[16,4,48,256]{3,2,1,0:T(8,128)(2,1)} %project.1), calls=%async_computation.1 | async-start | bytes 3145728 | tf_op jit(solution)/shard_map/all_to_all | solution.py:381
  30.2 0.9 unpack.1
  31.0 1.6 %collective-permute-start = (bf16[1056,128]{1,0:T(8,128)(2,1)}, bf16[1056,128]{1,0:T(8,128)(2,1)}, u32[]{:S(2)}, u32[]{:S(2)}) collective-permute-start(bf16[1056,128]{1,0:T(8,128)(2,1)} %get-tuple-element.33.refs_0_.refs_4_), channel_id=1, source_target_pairs={{0,32},{16,48},{32,64},{48,80},{64,96},{80,112},{96,0},{112,16},{1... | collective-permute-start | bytes 811016 | tf_op jit(solution)/shard_map/ppermute | solution.py:329
  32.6 1.7 %collective-permute-start.1 = (bf16[1056,128]{1,0:T(8,128)(2,1)}, bf16[1056,128]{1,0:T(8,128)(2,1)}, u32[]{:S(2)}, u32[]{:S(2)}) collective-permute-start(bf16[1056,128]{1,0:T(8,128)(2,1)} %get-tuple-element.34.refs_1_.refs_5_), channel_id=1, source_target_pairs={{0,96},{16,112},{32,0},{48,16},{64,32},{80,48},{96,64},{112,80},{1... | collective-permute-start | bytes 811016 | tf_op jit(solution)/shard_map/ppermute | solution.py:329
  34.3 1.8 %collective-permute-start.3 = (bf16[1056,128]{1,0:T(8,128)(2,1)}, bf16[1056,128]{1,0:T(8,128)(2,1)S(1)}, u32[]{:S(2)}, u32[]{:S(2)}) collective-permute-start(bf16[1056,128]{1,0:T(8,128)(2,1)} %get-tuple-element.33.refs_0_.refs_4_), channel_id=1, source_target_pairs={{0,96},{16,112},{32,0},{48,16},{64,32},{80,48},{96,64},{112,80},{1... | collective-permute-start | bytes 811016 | tf_op jit(solution)/shard_map/ppermute | solution.py:329
  36.1 0.2 collective-permute-start.2
  36.3 5.6 %collective-permute-done.refs_2_.refs_6_ = bf16[1056,128]{1,0:T(8,128)(2,1)} collective-permute-done((bf16[1056,128]{1,0:T(8,128)(2,1)}, bf16[1056,128]{1,0:T(8,128)(2,1)}, u32[]{:S(2)}, u32[]{:S(2)}) %collective-permute-start) | collective-permute-done | bytes 270368 | tf_op jit(solution)/shard_map/ppermute | solution.py:329
  41.9 0.4 collective-permute-start.4
  42.2 0.0 collective-permute-done.1.refs_3_.refs_7_
  42.3 2.9 %collective-permute-start.5 = (bf16[1056,128]{1,0:T(8,128)(2,1)}, bf16[1056,128]{1,0:T(8,128)(2,1)}, u32[]{:S(2)}, u32[]{:S(2)}) collective-permute-start(bf16[1056,128]{1,0:T(8,128)(2,1)} %collective-permute-done.1.refs_3_.refs_7_), channel_id=1, source_target_pairs={{0,96},{16,112},{32,0},{48,16},{64,32},{80,48},{96,64},{112,80},{1... | collective-permute-start | bytes 811016 | tf_op jit(solution)/shard_map/ppermute | solution.py:329
  45.1 0.1 stack.35.order_ref
  45.2 3.8 %early.1 = (f32[1024,128]{1,0:T(8,128)}, f32[1024,128]{1,0:T(8,128)}, f32[1024,128]{1,0:T(8,128)}, f32[1024,128]{1,0:T(8,128)}) custom-call(bf16[1056,128]{1,0:T(8,128)(2,1)} %get-tuple-element.33.refs_0_.refs_4_, bf16[1056,128]{1,0:T(8,128)(2,1)} %get-tuple-element.34.refs_1_.refs_5_, bf16[1056,128]{1,0:T(8,128)(2,1)} %collective-permute-done.refs_2_.refs_6_, ...), custom_call_target="tpu_custom_call" | custom-call | tf_op jit(solution)/shard_map/early/pallas_call | solution.py:79
  49.0 3.4 %all-to-all-done.1.r_ref = bf16[16,4,48,256]{3,2,1,0:T(8,128)(2,1)S(1)} async-done(((bf16[16,4,48,256]{3,2,1,0:T(8,128)(2,1)}), bf16[16,4,48,256]{3,2,1,0:T(8,128)(2,1)S(1)}, u32[]{:S(2)}, u32[]{:S(2)}) %all-to-all-start.1) | async-done | bytes 1572896 | tf_op jit(solution)/shard_map/all_to_all | solution.py:381
  52.4 1.6 %prep.1 = (bf16[4,48,1024]{2,1,0:T(8,128)(2,1)S(1)}, bf16[4,48,1024]{2,1,0:T(8,128)(2,1)S(1)}, bf16[4,48,1024]{2,1,0:T(8,128)(2,1)S(1)}, bf16[4,48,1024]{2,1,0:T(8,128)(2,1)S(1)}, bf16[4,1024,48]{2,1,0:T(8,128)(2,1)S(1)}) custom-call(s32[8]{0:T(128)S(1)} %stack.35.order_ref, bf16[16,4,48,256]{3,2,1,0:T(8,128)(2,1)S(1)} %all-to-all-done.1.r_ref), custom_call_target="tpu_custom_call" | custom-call | tf_op jit(solution)/shard_map/prep/pallas_call | solution.py:40
  54.1 18.0 %attend.1 = (bf16[1024,128]{1,0:T(8,128)(2,1)}, bf16[1024,128]{1,0:T(8,128)(2,1)}, bf16[1024,128]{1,0:T(8,128)(2,1)}, bf16[1024,128]{1,0:T(8,128)(2,1)}, bf16[10...) custom-call(s32[8]{0:T(128)S(1)} %stack.35.order_ref, ...), custom_call_target="tpu_custom_call" | custom-call | flops 1000000 | bytes 1024 | tf_op jit(solution)/shard_map/attend/pallas_call | solution.py:177
  72.1 4.5 %all-to-all-start.2 = ((bf16[16,3,48,256]{3,2,1,0:T(8,128)(2,1)}), bf16[16,3,48,256]{3,2,1,0:T(8,128)(2,1)}, u32[]{:S(2)}, u32[]{:S(2)}) async-start(bf16[16,3,48,256]{3,2,1,0:T(8,128)(2,1)} %get-tuple-element.49), calls=%async_computation.2 | async-start | bytes 2359296 | tf_op jit(solution)/shard_map/all_to_all | solution.py:385
  76.7 0.0 copy-start.10
  76.7 1.6 %collective-permute-start.6 = (bf16[1024,128]{1,0:T(8,128)(2,1)S(1)}, bf16[1024,128]{1,0:T(8,128)(2,1)S(1)}, u32[]{:S(2)}, u32[]{:S(2)}) collective-permute-start(bf16[1024,128]{1,0:T(8,128)(2,1)S(1)} %copy-done.17), channel_id=1, source_target_pairs={{0,32},{16,48},{32,64},{48,80},{64,96},{80,112},{96,0},{112,16},{1... | collective-permute-start | bytes 786440 | tf_op jit(solution)/shard_map/ppermute | solution.py:329
  78.4 1.7 %collective-permute-start.10 = (bf16[1024,128]{1,0:T(8,128)(2,1)S(1)}, bf16[1024,128]{1,0:T(8,128)(2,1)S(1)}, u32[]{:S(2)}, u32[]{:S(2)}) collective-permute-start(bf16[1024,128]{1,0:T(8,128)(2,1)S(1)} %copy-done.16), channel_id=1, source_target_pairs={{0,96},{16,112},{32,0},{48,16},{64,32},{80,48},{96,64},{112,80},{1... | collective-permute-start | bytes 786440 | tf_op jit(solution)/shard_map/ppermute | solution.py:329
  80.1 1.8 %collective-permute-start.8 = (bf16[1024,128]{1,0:T(8,128)(2,1)S(1)}, bf16[1024,128]{1,0:T(8,128)(2,1)S(1)}, u32[]{:S(2)}, u32[]{:S(2)}) collective-permute-start(bf16[1024,128]{1,0:T(8,128)(2,1)S(1)} %copy-done.15), channel_id=1, source_target_pairs={{0,96},{16,112},{32,0},{48,16},{64,32},{80,48},{96,64},{112,80},{1... | collective-permute-start | bytes 786440 | tf_op jit(solution)/shard_map/ppermute | solution.py:329
  81.8 0.3 collective-permute-start.9
  82.1 5.0 %collective-permute-done.6 = bf16[1024,128]{1,0:T(8,128)(2,1)S(1)} collective-permute-done((bf16[1024,128]{1,0:T(8,128)(2,1)S(1)}, bf16[1024,128]{1,0:T(8,128)(2,1)S(1)}, u32[]{:S(2)}, u32[]{:S(2)}) %collective-permute-start.6) | collective-permute-done | bytes 262176 | tf_op jit(solution)/shard_map/ppermute | solution.py:329
  87.1 0.1 add_convert_fusion.1
  87.2 0.4 collective-permute-start.7
  87.6 0.1 add_convert_fusion
  87.7 2.9 %collective-permute-start.11 = (bf16[1024,128]{1,0:T(8,128)(2,1)S(1)}, bf16[1024,128]{1,0:T(8,128)(2,1)S(1)}, u32[]{:S(2)}, u32[]{:S(2)}) collective-permute-start(bf16[1024,128]{1,0:T(8,128)(2,1)S(1)} %add_convert_fusion), channel_id=1, source_target_pairs={{0,96},{16,112},{32,0},{48,16},{64,32},{80,48},{96,64},{112,80},{1... | collective-permute-start | bytes 786440 | tf_op jit(solution)/shard_map/ppermute | solution.py:329
  90.6 2.5 %collective-permute-done.8.c0 = bf16[1024,128]{1,0:T(8,128)(2,1)S(1)} collective-permute-done((bf16[1024,128]{1,0:T(8,128)(2,1)S(1)}, bf16[1024,128]{1,0:T(8,128)(2,1)S(1)}, u32[]{:S(2)}, u32[]{:S(2)}) %collective-permute-start.8) | collective-permute-done | bytes 262176 | tf_op jit(solution)/shard_map/ppermute | solution.py:329
  93.1 4.6 %collective-permute-done.7.b0 = bf16[1024,128]{1,0:T(8,128)(2,1)S(1)} collective-permute-done((bf16[1024,128]{1,0:T(8,128)(2,1)S(1)}, bf16[1024,128]{1,0:T(8,128)(2,1)S(1)}, u32[]{:S(2)}, u32[]{:S(2)}) %collective-permute-start.7) | collective-permute-done | bytes 262176 | tf_op jit(solution)/shard_map/ppermute | solution.py:329
  97.8 0.1 collective-permute-done.11.c1
  97.9 1.0 own_sum.1
  98.9 5.7 %all-to-all-start.3 = ((bf16[32,64,128]{2,1,0:T(8,128)(2,1)}), bf16[32,64,128]{2,1,0:T(8,128)(2,1)S(1)}, u32[]{:S(2)}, u32[]{:S(2)}) async-start(bf16[32,64,128]{2,1,0:T(8,128)(2,1)} %bitcast.9), calls=%async_computation.3 | async-start | bytes 1048576 | tf_op jit(solution)/shard_map/all_to_all | solution.py:334
  104.7 0.0 copy-start.4
  104.7 1.3 %copy-done.4 = bf16[768,768]{1,0:T(8,128)(2,1)S(1)} copy-done((bf16[768,768]{1,0:T(8,128)(2,1)S(1)}, bf16[768,768]{1,0:T(8,128)(2,1)}, u32[]{:S(2)}) %copy-start.4) | copy-done | bytes 1179672
  105.9 3.2 %final.1 = bf16[4,64,768]{2,1,0:T(8,128)(2,1)} custom-call(bf16[16,3,48,256]{3,2,1,0:T(8,128)(2,1)} %all-to-all-done.2.g_ref, bf16[768,768]{1,0:T(8,128)(2,1)S(1)} %copy-done, bf16[768,768]{1,0:T(8,128)(2,1)S(1)} %copy-done.2, bf16[768,768]{1,0:T(8,128)(2,1)S(1)} %copy-done.4), custom_call_target="tpu_custom_call" | custom-call | tf_op jit(solution)/shard_map/final/pallas_call | solution.py:321
  109.1 7.4 %all-to-all-done.3 = bf16[32,64,128]{2,1,0:T(8,128)(2,1)S(1)} async-done(((bf16[32,64,128]{2,1,0:T(8,128)(2,1)}), bf16[32,64,128]{2,1,0:T(8,128)(2,1)S(1)}, u32[]{:S(2)}, u32[]{:S(2)}) %all-to-all-start.3) | async-done | bytes 524320 | tf_op jit(solution)/shard_map/all_to_all | solution.py:334
  116.5 2.1 %gpair.1 = bf16[64,128,128]{2,1,0:T(8,128)(2,1)} custom-call(bf16[2,16,64,128]{3,2,1,0:T(8,128)(2,1)S(1)} %bitcast.12, bf16[128,16]{1,0:T(8,128)(2,1)S(1)} %copy.10.w_ref), custom_call_target="tpu_custom_call" | custom-call | tf_op jit(solution)/shard_map/gpair/pallas_call | solution.py:283
  (33 shorter events, 0.1 us)
Async XLA Ops:
  1.4 1.6 %copy-start.6 = (bf16[64,128,128]{2,1,0:T(8,128)(2,1)S(1)}, bf16[64,128,128]{2,1,0:T(8,128)(2,1)}, u32[]{:S(2)}) copy-start(bf16[64,128,128]{2,1,0:T(8,128)(2,1)} %pair_ref.1) | copy-start | bytes 6291460
  3.0 10.3 %copy-start.1 = (bf16[768,768]{1,0:T(8,128)(2,1)S(1)}, bf16[768,768]{1,0:T(8,128)(2,1)}, u32[]{:S(2)}) copy-start(bf16[768,768]{1,0:T(8,128)(2,1)} %wk_ref.3) | copy-start | bytes 3538948
  4.1 0.9 copy-start.5
  5.0 8.4 %copy-start = (bf16[768,768]{1,0:T(8,128)(2,1)S(1)}, bf16[768,768]{1,0:T(8,128)(2,1)}, u32[]{:S(2)}) copy-start(bf16[768,768]{1,0:T(8,128)(2,1)} %wq_ref.3) | copy-start | bytes 3538948
  5.0 21.5 %all-to-all-start = ((bf16[32,80,128]{2,1,0:T(8,128)(2,1)}), bf16[32,80,128]{2,1,0:T(8,128)(2,1)S(1)}, u32[]{:S(2)}, u32[]{:S(2)}) async-start(bf16[32,80,128]{2,1,0:T(8,128)(2,1)} %copy-done.5), calls=%async_computation | async-start | bytes 1310720 | tf_op jit(solution)/shard_map/all_to_all | solution.py:334
  13.4 1.3 %copy-start.3 = (bf16[768,768]{1,0:T(8,128)(2,1)S(1)}, bf16[768,768]{1,0:T(8,128)(2,1)}, u32[]{:S(2)}) copy-start(bf16[768,768]{1,0:T(8,128)(2,1)} %wv_ref.3) | copy-start | bytes 3538948
  14.6 1.3 %copy-start.7 = (bf16[768,768]{1,0:T(8,128)(2,1)S(1)}, bf16[768,768]{1,0:T(8,128)(2,1)}, u32[]{:S(2)}) copy-start(bf16[768,768]{1,0:T(8,128)(2,1)} %wo_ref.1) | copy-start | bytes 3538948
  15.9 1.0 copy-start.8
  16.9 1.0 copy-start.9
  26.4 26.0 %all-to-all-start.1 = ((bf16[16,4,48,256]{3,2,1,0:T(8,128)(2,1)}), bf16[16,4,48,256]{3,2,1,0:T(8,128)(2,1)S(1)}, u32[]{:S(2)}, u32[]{:S(2)}) async-start(bf16[16,4,48,256]{3,2,1,0:T(8,128)(2,1)} %project.1), calls=%async_computation.1 | async-start | bytes 3145728 | tf_op jit(solution)/shard_map/all_to_all | solution.py:381
  31.0 10.8 %collective-permute-start = (bf16[1056,128]{1,0:T(8,128)(2,1)}, bf16[1056,128]{1,0:T(8,128)(2,1)}, u32[]{:S(2)}, u32[]{:S(2)}) collective-permute-start(bf16[1056,128]{1,0:T(8,128)(2,1)} %get-tuple-element.33.refs_0_.refs_4_), channel_id=1, source_target_pairs={{0,32},{16,48},{32,64},{48,80},{64,96},{80,112},{96,0},{112,16},{1... | collective-permute-start | bytes 811016 | tf_op jit(solution)/shard_map/ppermute | solution.py:329
  32.6 9.7 %collective-permute-start.1 = (bf16[1056,128]{1,0:T(8,128)(2,1)}, bf16[1056,128]{1,0:T(8,128)(2,1)}, u32[]{:S(2)}, u32[]{:S(2)}) collective-permute-start(bf16[1056,128]{1,0:T(8,128)(2,1)} %get-tuple-element.34.refs_1_.refs_5_), channel_id=1, source_target_pairs={{0,96},{16,112},{32,0},{48,16},{64,32},{80,48},{96,64},{112,80},{1... | collective-permute-start | bytes 811016 | tf_op jit(solution)/shard_map/ppermute | solution.py:329
  34.3 19.8 %collective-permute-start.3 = (bf16[1056,128]{1,0:T(8,128)(2,1)}, bf16[1056,128]{1,0:T(8,128)(2,1)S(1)}, u32[]{:S(2)}, u32[]{:S(2)}) collective-permute-start(bf16[1056,128]{1,0:T(8,128)(2,1)} %get-tuple-element.33.refs_0_.refs_4_), channel_id=1, source_target_pairs={{0,96},{16,112},{32,0},{48,16},{64,32},{80,48},{96,64},{112,80},{1... | collective-permute-start | bytes 811016 | tf_op jit(solution)/shard_map/ppermute | solution.py:329
  36.1 18.0 %collective-permute-start.2 = (bf16[1056,128]{1,0:T(8,128)(2,1)}, bf16[1056,128]{1,0:T(8,128)(2,1)S(1)}, u32[]{:S(2)}, u32[]{:S(2)}) collective-permute-start(bf16[1056,128]{1,0:T(8,128)(2,1)} %get-tuple-element.34.refs_1_.refs_5_), channel_id=1, source_target_pairs={{0,32},{16,48},{32,64},{48,80},{64,96},{80,112},{96,0},{112,16},{1... | collective-permute-start | bytes 811016 | tf_op jit(solution)/shard_map/ppermute | solution.py:329
  41.9 12.2 %collective-permute-start.4 = (bf16[1056,128]{1,0:T(8,128)(2,1)}, bf16[1056,128]{1,0:T(8,128)(2,1)}, u32[]{:S(2)}, u32[]{:S(2)}) collective-permute-start(bf16[1056,128]{1,0:T(8,128)(2,1)} %collective-permute-done.refs_2_.refs_6_), channel_id=1, source_target_pairs={{0,32},{16,48},{32,64},{48,80},{64,96},{80,112},{96,0},{112,16},{1... | collective-permute-start | bytes 811016 | tf_op jit(solution)/shard_map/ppermute | solution.py:329
  42.3 11.8 %collective-permute-start.5 = (bf16[1056,128]{1,0:T(8,128)(2,1)}, bf16[1056,128]{1,0:T(8,128)(2,1)}, u32[]{:S(2)}, u32[]{:S(2)}) collective-permute-start(bf16[1056,128]{1,0:T(8,128)(2,1)} %collective-permute-done.1.refs_3_.refs_7_), channel_id=1, source_target_pairs={{0,96},{16,112},{32,0},{48,16},{64,32},{80,48},{96,64},{112,80},{1... | collective-permute-start | bytes 811016 | tf_op jit(solution)/shard_map/ppermute | solution.py:329
  72.1 4.6 %copy-start.17 = (bf16[1024,128]{1,0:T(8,128)(2,1)S(1)}, bf16[1024,128]{1,0:T(8,128)(2,1)}, u32[]{:S(2)}) copy-start(bf16[1024,128]{1,0:T(8,128)(2,1)} %get-tuple-element.52) | copy-start | bytes 786436
  72.1 6.3 %copy-start.16 = (bf16[1024,128]{1,0:T(8,128)(2,1)S(1)}, bf16[1024,128]{1,0:T(8,128)(2,1)}, u32[]{:S(2)}) copy-start(bf16[1024,128]{1,0:T(8,128)(2,1)} %get-tuple-element.57) | copy-start | bytes 786436
  72.1 8.0 %copy-start.15 = (bf16[1024,128]{1,0:T(8,128)(2,1)S(1)}, bf16[1024,128]{1,0:T(8,128)(2,1)}, u32[]{:S(2)}) copy-start(bf16[1024,128]{1,0:T(8,128)(2,1)} %get-tuple-element.53) | copy-start | bytes 786436
  72.1 9.7 %copy-start.14 = (bf16[1024,128]{1,0:T(8,128)(2,1)S(1)}, bf16[1024,128]{1,0:T(8,128)(2,1)}, u32[]{:S(2)}) copy-start(bf16[1024,128]{1,0:T(8,128)(2,1)} %get-tuple-element.55) | copy-start | bytes 786436
  72.1 15.0 %copy-start.13 = (bf16[1024,128]{1,0:T(8,128)(2,1)S(1)}, bf16[1024,128]{1,0:T(8,128)(2,1)}, u32[]{:S(2)}) copy-start(bf16[1024,128]{1,0:T(8,128)(2,1)} %get-tuple-element.51) | copy-start | bytes 786436
  72.1 15.5 %copy-start.12 = (bf16[1024,128]{1,0:T(8,128)(2,1)S(1)}, bf16[1024,128]{1,0:T(8,128)(2,1)}, u32[]{:S(2)}) copy-start(bf16[1024,128]{1,0:T(8,128)(2,1)} %get-tuple-element.56) | copy-start | bytes 786436
  72.1 26.8 %all-to-all-start.2 = ((bf16[16,3,48,256]{3,2,1,0:T(8,128)(2,1)}), bf16[16,3,48,256]{3,2,1,0:T(8,128)(2,1)}, u32[]{:S(2)}, u32[]{:S(2)}) async-start(bf16[16,3,48,256]{3,2,1,0:T(8,128)(2,1)} %get-tuple-element.49), calls=%async_computation.2 | async-start | bytes 2359296 | tf_op jit(solution)/shard_map/all_to_all | solution.py:385
  76.7 21.2 %copy-start.10 = (bf16[1024,128]{1,0:T(8,128)(2,1)S(1)}, bf16[1024,128]{1,0:T(8,128)(2,1)}, u32[]{:S(2)}) copy-start(bf16[1024,128]{1,0:T(8,128)(2,1)} %get-tuple-element.50.a0) | copy-start | bytes 786436
  76.7 21.2 %copy-start.11 = (bf16[1024,128]{1,0:T(8,128)(2,1)S(1)}, bf16[1024,128]{1,0:T(8,128)(2,1)}, u32[]{:S(2)}) copy-start(bf16[1024,128]{1,0:T(8,128)(2,1)} %get-tuple-element.54.a1) | copy-start | bytes 786436
  76.7 10.4 %collective-permute-start.6 = (bf16[1024,128]{1,0:T(8,128)(2,1)S(1)}, bf16[1024,128]{1,0:T(8,128)(2,1)S(1)}, u32[]{:S(2)}, u32[]{:S(2)}) collective-permute-start(bf16[1024,128]{1,0:T(8,128)(2,1)S(1)} %copy-done.17), channel_id=1, source_target_pairs={{0,32},{16,48},{32,64},{48,80},{64,96},{80,112},{96,0},{112,16},{1... | collective-permute-start | bytes 786440 | tf_op jit(solution)/shard_map/ppermute | solution.py:329
  78.4 9.3 %collective-permute-start.10 = (bf16[1024,128]{1,0:T(8,128)(2,1)S(1)}, bf16[1024,128]{1,0:T(8,128)(2,1)S(1)}, u32[]{:S(2)}, u32[]{:S(2)}) collective-permute-start(bf16[1024,128]{1,0:T(8,128)(2,1)S(1)} %copy-done.16), channel_id=1, source_target_pairs={{0,96},{16,112},{32,0},{48,16},{64,32},{80,48},{96,64},{112,80},{1... | collective-permute-start | bytes 786440 | tf_op jit(solution)/shard_map/ppermute | solution.py:329
  80.1 13.1 %collective-permute-start.8 = (bf16[1024,128]{1,0:T(8,128)(2,1)S(1)}, bf16[1024,128]{1,0:T(8,128)(2,1)S(1)}, u32[]{:S(2)}, u32[]{:S(2)}) collective-permute-start(bf16[1024,128]{1,0:T(8,128)(2,1)S(1)} %copy-done.15), channel_id=1, source_target_pairs={{0,96},{16,112},{32,0},{48,16},{64,32},{80,48},{96,64},{112,80},{1... | collective-permute-start | bytes 786440 | tf_op jit(solution)/shard_map/ppermute | solution.py:329
  81.8 11.3 %collective-permute-start.9 = (bf16[1024,128]{1,0:T(8,128)(2,1)S(1)}, bf16[1024,128]{1,0:T(8,128)(2,1)S(1)}, u32[]{:S(2)}, u32[]{:S(2)}) collective-permute-start(bf16[1024,128]{1,0:T(8,128)(2,1)S(1)} %copy-done.14), channel_id=1, source_target_pairs={{0,32},{16,48},{32,64},{48,80},{64,96},{80,112},{96,0},{112,16},{1... | collective-permute-start | bytes 786440 | tf_op jit(solution)/shard_map/ppermute | solution.py:329
  87.2 10.6 %collective-permute-start.7 = (bf16[1024,128]{1,0:T(8,128)(2,1)S(1)}, bf16[1024,128]{1,0:T(8,128)(2,1)S(1)}, u32[]{:S(2)}, u32[]{:S(2)}) collective-permute-start(bf16[1024,128]{1,0:T(8,128)(2,1)S(1)} %add_convert_fusion.1), channel_id=1, source_target_pairs={{0,32},{16,48},{32,64},{48,80},{64,96},{80,112},{96,0},{112,16},{1... | collective-permute-start | bytes 786440 | tf_op jit(solution)/shard_map/ppermute | solution.py:329
  87.7 10.2 %collective-permute-start.11 = (bf16[1024,128]{1,0:T(8,128)(2,1)S(1)}, bf16[1024,128]{1,0:T(8,128)(2,1)S(1)}, u32[]{:S(2)}, u32[]{:S(2)}) collective-permute-start(bf16[1024,128]{1,0:T(8,128)(2,1)S(1)} %add_convert_fusion), channel_id=1, source_target_pairs={{0,96},{16,112},{32,0},{48,16},{64,32},{80,48},{96,64},{112,80},{1... | collective-permute-start | bytes 786440 | tf_op jit(solution)/shard_map/ppermute | solution.py:329
  97.9 6.8 %copy-start.2 = (bf16[768,768]{1,0:T(8,128)(2,1)S(1)}, bf16[768,768]{1,0:T(8,128)(2,1)}, u32[]{:S(2)}) copy-start(bf16[768,768]{1,0:T(8,128)(2,1)} %wk_ref.3) | copy-start | bytes 3538948
  98.9 17.6 %all-to-all-start.3 = ((bf16[32,64,128]{2,1,0:T(8,128)(2,1)}), bf16[32,64,128]{2,1,0:T(8,128)(2,1)S(1)}, u32[]{:S(2)}, u32[]{:S(2)}) async-start(bf16[32,64,128]{2,1,0:T(8,128)(2,1)} %bitcast.9), calls=%async_computation.3 | async-start | bytes 1048576 | tf_op jit(solution)/shard_map/all_to_all | solution.py:334
  104.7 1.3 %copy-start.4 = (bf16[768,768]{1,0:T(8,128)(2,1)S(1)}, bf16[768,768]{1,0:T(8,128)(2,1)}, u32[]{:S(2)}) copy-start(bf16[768,768]{1,0:T(8,128)(2,1)} %wv_ref.3) | copy-start | bytes 3538948

commit v6 on v5

--- a/solution.py
+++ b/solution.py
@@ -47,7 +47,8 @@
     )(order, received)
 
 
-TILE = 256
+TILE = 512
+GROUP = 256
 VMEM_ATT = 40
 NEAR = 8.0
 STEEP = 18.8
@@ -73,11 +74,11 @@
 
 
 def early(blocks):
-    code_t = pl.BlockSpec((TILE, 128), lambda i: (i, 0))
+    code_t = pl.BlockSpec((GROUP, 128), lambda i: (i, 0))
     top_t = pl.BlockSpec((32, 128), lambda i: (TOK // 32, 0))
     count = len(blocks)
     return pl.pallas_call(
-        early_body, grid=(TOK // TILE,), out_shape=[pltpu.HBM((TOK, 128), F32)] * count,
+        early_body, grid=(TOK // GROUP,), out_shape=[pltpu.HBM((TOK, 128), F32)] * count,
         in_specs=[code_t] * count + [top_t] * count, out_specs=[code_t] * count,
         compiler_params=pltpu.CompilerParams(vmem_limit_bytes=16 * 2**20), name="early",
     )(*blocks, *blocks)
@@ -98,8 +99,11 @@
 
     def all_bias():
         for n in range(4):
-            for at, block in decode_rows(code_refs[n], top_refs[n][...].astype(F32), step):
-                bias_scr[at:at + 64, n * 128:n * 128 + 128] = block
+            for part in range(TILE // GROUP):
+                start = part * GROUP
+                codes, group = code_refs[n][start:start + GROUP, :], step * (TILE // GROUP) + part
+                for at, block in decode_rows(codes, top_refs[n][...].astype(F32), group):
+                    bias_scr[start + at:start + at + 64, n * 128:n * 128 + 128] = block
 
     def products(b):
         first = (((0,), (0,)), ((), ()))
@@ -194,7 +198,7 @@
 
 
 def block_diagonal(w_ref, count):
-    turned = w_ref[...].astype(F32).T
+    turned = w_ref[...].astype(F32)
     rows = jnp.broadcast_to(turned[:, None, :], (16, count, 128)).reshape(16 * count, 128)
     at = lax.broadcasted_iota(jnp.int32, (16 * count, 128), 0) % count
     return jnp.concatenate([jnp.where(at == i, rows, 0.0) for i in range(count)], axis=1).astype(BF16)
@@ -215,38 +219,48 @@
     return lane, (lane >= 0) & (lane < 24) & (lane % 8 == row % 8)
 
 
-def bias_body(pair_ref, w_ref, out_ref):
-    w = block_diagonal(w_ref, 8)
+def bias_body(pair_ref, w_ref, out_ref, wide_ref, tops_ref):
+    step = pl.program_id(0)
+
+    @pl.when(step == 0)
+    def _():
+        wide_ref[...] = block_diagonal(w_ref, 8)
+
     lane, mark = marks(128, 0)
-    tops = []
-    for g in range(8):
+    for g in range(4):
         cols = jnp.concatenate([pair_ref[g * 8 + r] for r in range(8)], axis=1)
-        t = lax.dot_general(w, cols, (((1,), (1,)), ((), ())), preferred_element_type=F32)
+        t = lax.dot_general(wide_ref[...], cols, (((1,), (1,)), ((), ())), preferred_element_type=F32)
         code, top = encode(t * LOG2E)
         high = top.astype(BF16).astype(F32)
         middle = (top - high).astype(BF16).astype(F32)
         terms = jnp.where(lane < 8, high, jnp.where(lane < 16, middle, top - high - middle))
-        tops.append(jnp.sum(jnp.where(mark, terms, 0.0).reshape(16, 8, 128), axis=1))
+        tops_ref[step * 4 + g] = jnp.sum(jnp.where(mark, terms, 0.0).reshape(16, 8, 128), axis=1)
         if g % 2 == 0:
             even = code
             continue
+        rows = pl.ds(pl.multiple_of(step * 32 + g * 8 - 8, 16), 16)
         for h in range(16):
             block = jnp.concatenate([even[h * 8:h * 8 + 8, :], code[h * 8:h * 8 + 8, :]], axis=0)
-            out_ref[h, g * 8 - 8:g * 8 + 8, :] = block
-            out_ref[h + 16, g * 8 - 8:g * 8 + 8, :] = block
-    for h in range(16):
-        block = jnp.concatenate([top[h:h + 1, :] for top in tops] + [jnp.zeros((8, 128), F32)], axis=0).astype(BF16)
-        out_ref[h, 64:80, :] = block
-        out_ref[h + 16, 64:80, :] = block
+            out_ref[h, rows, :] = block
+            out_ref[h + 16, rows, :] = block
+
+    @pl.when(step == 1)
+    def _():
+        for h in range(16):
+            tops = [tops_ref[g, h:h + 1, :] for g in range(8)]
+            block = jnp.concatenate(tops + [jnp.zeros((8, 128), F32)], axis=0).astype(BF16)
+            out_ref[h, 64:80, :] = block
+            out_ref[h + 16, 64:80, :] = block
 
 
 def bias_part(pair, w_pair):
-    vm = pl.BlockSpec(memory_space=pltpu.VMEM)
-    return pl.pallas_call(
-        bias_body, out_shape=jax.ShapeDtypeStruct((32, 80, 128), BF16),
-        in_specs=[vm, vm], out_specs=vm,
+    return pl.pallas_call(
+        bias_body, grid=(2,), out_shape=pltpu.HBM((32, 80, 128), BF16),
+        in_specs=[pl.BlockSpec((32, 128, 128), lambda i: (i, 0, 0)), pl.BlockSpec((16, 128), lambda i: (0, 0))],
+        out_specs=pl.BlockSpec((32, 80, 128), lambda i: (0, 0, 0)),
+        scratch_shapes=[pltpu.VMEM((128, 1024), BF16), pltpu.VMEM((8, 16, 128), F32)],
         compiler_params=pltpu.CompilerParams(vmem_limit_bytes=32 * 2**20), name="bias_part",
-    )(pair, w_pair)
+    )(pltpu.with_memory_space_constraint(pair, pltpu.HBM), pltpu.with_memory_space_constraint(w_pair, pltpu.HBM))
 
 
 def unpack_body(x_ref, *out_refs):
@@ -268,12 +282,17 @@
     )(x)
 
 
-def gpair_body(x_ref, w_ref, out_ref):
-    w = block_diagonal(w_ref, 16)
-    for g in range(4):
-        rows = slice(g * 16, g * 16 + 16)
+def gpair_body(x_ref, w_ref, out_ref, wide_ref):
+    step = pl.program_id(0)
+
+    @pl.when(step == 0)
+    def _():
+        wide_ref[...] = block_diagonal(w_ref, 16)
+
+    for g in range(2):
+        rows = pl.ds(pl.multiple_of(step * 32 + g * 16, 16), 16)
         x = (x_ref[0, :, rows, :].astype(F32) + x_ref[1, :, rows, :].astype(F32)).astype(BF16).reshape(256, 128)
-        t = lax.dot_general(x, w, (((0,), (0,)), ((), ())), preferred_element_type=F32)
+        t = lax.dot_general(x, wide_ref[...], (((0,), (0,)), ((), ())), preferred_element_type=F32)
         for r in range(16):
             out_ref[g * 16 + r] = t[:, r * 128:r * 128 + 128].astype(BF16)
 
@@ -281,8 +300,9 @@
 def gpair(x, w_pair):
     vm = pl.BlockSpec(memory_space=pltpu.VMEM)
     return pl.pallas_call(
-        gpair_body, out_shape=jax.ShapeDtypeStruct((64, 128, 128), BF16),
-        in_specs=[vm, vm], out_specs=vm,
+        gpair_body, grid=(2,), out_shape=jax.ShapeDtypeStruct((64, 128, 128), BF16),
+        in_specs=[vm, vm], out_specs=pl.BlockSpec((32, 128, 128), lambda i: (i, 0, 0)),
+        scratch_shapes=[pltpu.VMEM((256, 2048), BF16)],
         compiler_params=pltpu.CompilerParams(vmem_limit_bytes=32 * 2**20), name="gpair",
     )(x, w_pair)
 
@@ -376,7 +396,7 @@
 def local(single, pair, w_query, w_key, w_value, w_out, w_pair, cotangent):
     order = key_order()
     sent = project(single, cotangent, w_query, w_key, w_value, w_out)
-    bias = exchange(bias_part(pair, w_pair))
+    bias = exchange(bias_part(pair, w_pair.T))
     bias, sent = lax.optimization_barrier((bias, sent))
     received = lax.all_to_all(sent, "tok", 0, 0)
     blocks = gather_blocks(unpack(bias.reshape(2, 16, 80, 128)))
@@ -387,7 +407,7 @@
     grads, dbias = lax.optimization_barrier((grads, dbias))
     grad_single = final(grads, w_query, w_key, w_value)
     dbias = exchange(dbias.reshape(32, 64, 128)).reshape(2, 16, 64, 128)
-    return (grad_single, gpair(dbias, w_pair))
+    return (grad_single, gpair(dbias, w_pair.T))
 
 
 def solution(mesh):

time: 120 us -> 119 us (level)
  local copies, waits for them, and re-layouts: 9.16 us -> 5.75 us
    unnamed x37 -> x36, local copies, waits for them, and re-layouts: 9.08 us -> 5.67 us
    pallas_call x3, Pallas kernels: 7 us -> 9.46 us  [the longest x1 3.8 us: early(): pl.pallas_call(early_body, grid=(TOK // GROUP,), out_shape=[pltpu.HBM((TO...]
  transfers between devices with their start and end apart: 16 -> 16, of which waited for: 8 -> 8; matrix products, arithmetic and copies ran while one was open for 0% -> 0% of each run, Pallas kernels for 11% -> 10%
where the time goes in v6:
time: 119 us; the launch traced here: 117 us
  starting transfers between devices  39.6 us (33%)
  waiting for transfers between devices  35.7 us (30%)
  Pallas kernels  35.3 us (30%)
  local copies, waits for them, and re-layouts  5.75 us (5%)
    ppermute x12, waiting for transfers between devices, shift_y(): lax.ppermute(x, 'sample', [(i, (i // 2 + d) % 4 * 2 + i % 2) for i in ran...  17.9 us
    pallas_call x1, Pallas kernels, attend(): pl.pallas_call(functools.partial(attend_body, scale, steps), grid=(steps,...  17.4 us
    ppermute x12, starting transfers between devices, shift_y(): lax.ppermute(x, 'sample', [(i, (i // 2 + d) % 4 * 2 + i % 2) for i in ran...  17.2 us
    all_to_all x2, waiting for transfers between devices, exchange(): return lax.all_to_all(x, ('sample', 'tok'), 0, 0, axis_index_groups=groups)  14.4 us
    all_to_all x2, starting transfers between devices, exchange(): return lax.all_to_all(x, ('sample', 'tok'), 0, 0, axis_index_groups=groups)  14.1 us
    unnamed x36, local copies, waits for them, and re-layouts  5.67 us
    all_to_all x1, starting transfers between devices, local(): grads = lax.all_to_all(grads, 'tok', 0, 0)  4.54 us
    pallas_call x1, Pallas kernels, early(): pl.pallas_call(early_body, grid=(TOK // GROUP,), out_shape=[pltpu.HBM((TO...  3.8 us
  transfers between devices with their start and end apart: 16, of which 8 were waited for; matrix products, arithmetic and copies ran while one was open for 0% of the time, Pallas kernels for 10%

profile of v6, /device:TPU:0, one launch (start us, length us, event | category | flops | bytes accessed | tf_op | source)
XLA Modules:
  0.0 117.3 jit_solution(12689558386566714664)
XLA Ops:
  0.6 0.0 copy-start.1
  0.7 3.6 %bias_part.1 = bf16[32,80,128]{2,1,0:T(8,128)(2,1)} custom-call(bf16[64,128,128]{2,1,0:T(8,128)(2,1)} %pair_ref.1, bf16[16,128]{1,0:T(8,128)(2,1)} %bitcast.15), custom_call_target="tpu_custom_call" | custom-call | tf_op jit(solution)/shard_map/bias_part/pallas_call | solution.py:257
  4.3 8.4 %all-to-all-start = ((bf16[32,80,128]{2,1,0:T(8,128)(2,1)}), bf16[32,80,128]{2,1,0:T(8,128)(2,1)S(1)}, u32[]{:S(2)}, u32[]{:S(2)}) async-start(bf16[32,80,128]{2,1,0:T(8,128)(2,1)} %bias_part.1), calls=%async_computation | async-start | bytes 1310720 | tf_op jit(solution)/shard_map/all_to_all | solution.py:354
  12.7 0.0 copy-start.3
  12.7 1.3 %copy-done.3 = bf16[768,768]{1,0:T(8,128)(2,1)S(1)} copy-done((bf16[768,768]{1,0:T(8,128)(2,1)S(1)}, bf16[768,768]{1,0:T(8,128)(2,1)}, u32[]{:S(2)}) %copy-start.3) | copy-done | bytes 1179672
  14.0 1.3 %copy-done.6 = bf16[768,768]{1,0:T(8,128)(2,1)S(1)} copy-done((bf16[768,768]{1,0:T(8,128)(2,1)S(1)}, bf16[768,768]{1,0:T(8,128)(2,1)}, u32[]{:S(2)}) %copy-start.6) | copy-done | bytes 1179672
  15.2 1.0 copy-done.8
  16.2 2.5 %project.1 = bf16[16,4,48,256]{3,2,1,0:T(8,128)(2,1)} custom-call(bf16[4,64,768]{2,1,0:T(8,128)(2,1)S(1)} %copy-done.7, bf16[4,64,768]{2,1,0:T(8,128)(2,1)S(1)} %copy-done.8, bf16[768,768]{1,0:T(8,128)(2,1)S(1)} %copy-done, bf16[768,768]{1,0:T(8,128)(2,1)S(1)} %copy-done.1, bf16[768,768]{1,0:T(8,128)(2,1)S(1)} %copy-done.3, bf16[768,768]{1,0:T(8,128)(2,1)S(1)} %copy-done.6), custom_call_target="tpu_custom_call" | custom-call | tf_op jit(solution)/shard_map/project/pallas_call | solution.py:324
  18.8 7.0 %all-to-all-done = bf16[32,80,128]{2,1,0:T(8,128)(2,1)S(1)} async-done(((bf16[32,80,128]{2,1,0:T(8,128)(2,1)}), bf16[32,80,128]{2,1,0:T(8,128)(2,1)S(1)}, u32[]{:S(2)}, u32[]{:S(2)}) %all-to-all-start) | async-done | bytes 655392 | tf_op jit(solution)/shard_map/all_to_all | solution.py:354
  25.7 3.7 %all-to-all-start.1 = ((bf16[16,4,48,256]{3,2,1,0:T(8,128)(2,1)}), bf16[16,4,48,256]{3,2,1,0:T(8,128)(2,1)S(1)}, u32[]{:S(2)}, u32[]{:S(2)}) async-start(bf16[16,4,48,256]{3,2,1,0:T(8,128)(2,1)} %project.1), calls=%async_computation.1 | async-start | bytes 3145728 | tf_op jit(solution)/shard_map/all_to_all | solution.py:401
  29.5 0.9 unpack.1
  30.3 1.6 %collective-permute-start = (bf16[1056,128]{1,0:T(8,128)(2,1)}, bf16[1056,128]{1,0:T(8,128)(2,1)}, u32[]{:S(2)}, u32[]{:S(2)}) collective-permute-start(bf16[1056,128]{1,0:T(8,128)(2,1)} %get-tuple-element.33.refs_0_.refs_4_), channel_id=1, source_target_pairs={{0,32},{16,48},{32,64},{48,80},{64,96},{80,112},{96,0},{112,16},{1... | collective-permute-start | bytes 811016 | tf_op jit(solution)/shard_map/ppermute | solution.py:349
  31.9 1.7 %collective-permute-start.1 = (bf16[1056,128]{1,0:T(8,128)(2,1)}, bf16[1056,128]{1,0:T(8,128)(2,1)}, u32[]{:S(2)}, u32[]{:S(2)}) collective-permute-start(bf16[1056,128]{1,0:T(8,128)(2,1)} %get-tuple-element.34.refs_1_.refs_5_), channel_id=1, source_target_pairs={{0,96},{16,112},{32,0},{48,16},{64,32},{80,48},{96,64},{112,80},{1... | collective-permute-start | bytes 811016 | tf_op jit(solution)/shard_map/ppermute | solution.py:349
  33.6 1.8 %collective-permute-start.3 = (bf16[1056,128]{1,0:T(8,128)(2,1)}, bf16[1056,128]{1,0:T(8,128)(2,1)S(1)}, u32[]{:S(2)}, u32[]{:S(2)}) collective-permute-start(bf16[1056,128]{1,0:T(8,128)(2,1)} %get-tuple-element.33.refs_0_.refs_4_), channel_id=1, source_target_pairs={{0,96},{16,112},{32,0},{48,16},{64,32},{80,48},{96,64},{112,80},{1... | collective-permute-start | bytes 811016 | tf_op jit(solution)/shard_map/ppermute | solution.py:349
  35.4 0.2 collective-permute-start.2
  35.6 5.6 %collective-permute-done.refs_2_.refs_6_ = bf16[1056,128]{1,0:T(8,128)(2,1)} collective-permute-done((bf16[1056,128]{1,0:T(8,128)(2,1)}, bf16[1056,128]{1,0:T(8,128)(2,1)}, u32[]{:S(2)}, u32[]{:S(2)}) %collective-permute-start) | collective-permute-done | bytes 270368 | tf_op jit(solution)/shard_map/ppermute | solution.py:349
  41.2 0.4 collective-permute-start.4
  41.5 0.0 collective-permute-done.1.refs_3_.refs_7_
  41.6 2.9 %collective-permute-start.5 = (bf16[1056,128]{1,0:T(8,128)(2,1)}, bf16[1056,128]{1,0:T(8,128)(2,1)}, u32[]{:S(2)}, u32[]{:S(2)}) collective-permute-start(bf16[1056,128]{1,0:T(8,128)(2,1)} %collective-permute-done.1.refs_3_.refs_7_), channel_id=1, source_target_pairs={{0,96},{16,112},{32,0},{48,16},{64,32},{80,48},{96,64},{112,80},{1... | collective-permute-start | bytes 811016 | tf_op jit(solution)/shard_map/ppermute | solution.py:349
  44.4 0.1 stack.35.order_ref
  44.5 3.8 %early.1 = (f32[1024,128]{1,0:T(8,128)}, f32[1024,128]{1,0:T(8,128)}, f32[1024,128]{1,0:T(8,128)}, f32[1024,128]{1,0:T(8,128)}) custom-call(bf16[1056,128]{1,0:T(8,128)(2,1)} %get-tuple-element.33.refs_0_.refs_4_, bf16[1056,128]{1,0:T(8,128)(2,1)} %get-tuple-element.34.refs_1_.refs_5_, bf16[1056,128]{1,0:T(8,128)(2,1)} %collective-permute-done.refs_2_.refs_6_, ...), custom_call_target="tpu_custom_call" | custom-call | tf_op jit(solution)/shard_map/early/pallas_call | solution.py:80
  48.3 3.4 %all-to-all-done.1.r_ref = bf16[16,4,48,256]{3,2,1,0:T(8,128)(2,1)S(1)} async-done(((bf16[16,4,48,256]{3,2,1,0:T(8,128)(2,1)}), bf16[16,4,48,256]{3,2,1,0:T(8,128)(2,1)S(1)}, u32[]{:S(2)}, u32[]{:S(2)}) %all-to-all-start.1) | async-done | bytes 1572896 | tf_op jit(solution)/shard_map/all_to_all | solution.py:401
  51.7 1.6 %prep.1 = (bf16[4,48,1024]{2,1,0:T(8,128)(2,1)S(1)}, bf16[4,48,1024]{2,1,0:T(8,128)(2,1)S(1)}, bf16[4,48,1024]{2,1,0:T(8,128)(2,1)S(1)}, bf16[4,48,1024]{2,1,0:T(8,128)(2,1)S(1)}, bf16[4,1024,48]{2,1,0:T(8,128)(2,1)S(1)}) custom-call(s32[8]{0:T(128)S(1)} %stack.35.order_ref, bf16[16,4,48,256]{3,2,1,0:T(8,128)(2,1)S(1)} %all-to-all-done.1.r_ref), custom_call_target="tpu_custom_call" | custom-call | tf_op jit(solution)/shard_map/prep/pallas_call | solution.py:40
  53.3 0.0 collective-permute-done.3.refs_5_.refs_9_
  53.4 0.0 collective-permute-done.4.refs_6_.refs_10_
  53.4 17.4 %attend.1 = (bf16[1024,128]{1,0:T(8,128)(2,1)}, bf16[1024,128]{1,0:T(8,128)(2,1)}, bf16[1024,128]{1,0:T(8,128)(2,1)}, bf16[1024,128]{1,0:T(8,128)(2,1)}, bf16[10...) custom-call(s32[8]{0:T(128)S(1)} %stack.35.order_ref, ...), custom_call_target="tpu_custom_call" | custom-call | flops 1000000 | bytes 1024 | tf_op jit(solution)/shard_map/attend/pallas_call | solution.py:181
  70.9 4.5 %all-to-all-start.2 = ((bf16[16,3,48,256]{3,2,1,0:T(8,128)(2,1)}), bf16[16,3,48,256]{3,2,1,0:T(8,128)(2,1)}, u32[]{:S(2)}, u32[]{:S(2)}) async-start(bf16[16,3,48,256]{3,2,1,0:T(8,128)(2,1)} %get-tuple-element.49), calls=%async_computation.2 | async-start | bytes 2359296 | tf_op jit(solution)/shard_map/all_to_all | solution.py:405
  75.4 0.0 copy-start.9
  75.4 1.6 %collective-permute-start.6 = (bf16[1024,128]{1,0:T(8,128)(2,1)S(1)}, bf16[1024,128]{1,0:T(8,128)(2,1)S(1)}, u32[]{:S(2)}, u32[]{:S(2)}) collective-permute-start(bf16[1024,128]{1,0:T(8,128)(2,1)S(1)} %copy-done.17), channel_id=1, source_target_pairs={{0,32},{16,48},{32,64},{48,80},{64,96},{80,112},{96,0},{112,16},{1... | collective-permute-start | bytes 786440 | tf_op jit(solution)/shard_map/ppermute | solution.py:349
  77.1 1.7 %collective-permute-start.10 = (bf16[1024,128]{1,0:T(8,128)(2,1)S(1)}, bf16[1024,128]{1,0:T(8,128)(2,1)S(1)}, u32[]{:S(2)}, u32[]{:S(2)}) collective-permute-start(bf16[1024,128]{1,0:T(8,128)(2,1)S(1)} %copy-done.16), channel_id=1, source_target_pairs={{0,96},{16,112},{32,0},{48,16},{64,32},{80,48},{96,64},{112,80},{1... | collective-permute-start | bytes 786440 | tf_op jit(solution)/shard_map/ppermute | solution.py:349
  78.7 1.8 %collective-permute-start.8 = (bf16[1024,128]{1,0:T(8,128)(2,1)S(1)}, bf16[1024,128]{1,0:T(8,128)(2,1)S(1)}, u32[]{:S(2)}, u32[]{:S(2)}) collective-permute-start(bf16[1024,128]{1,0:T(8,128)(2,1)S(1)} %copy-done.15), channel_id=1, source_target_pairs={{0,96},{16,112},{32,0},{48,16},{64,32},{80,48},{96,64},{112,80},{1... | collective-permute-start | bytes 786440 | tf_op jit(solution)/shard_map/ppermute | solution.py:349
  80.5 0.2 collective-permute-start.9
  80.8 5.1 %collective-permute-done.6 = bf16[1024,128]{1,0:T(8,128)(2,1)S(1)} collective-permute-done((bf16[1024,128]{1,0:T(8,128)(2,1)S(1)}, bf16[1024,128]{1,0:T(8,128)(2,1)S(1)}, u32[]{:S(2)}, u32[]{:S(2)}) %collective-permute-start.6) | collective-permute-done | bytes 262176 | tf_op jit(solution)/shard_map/ppermute | solution.py:349
  85.8 0.1 add_convert_fusion.1
  85.9 0.4 collective-permute-start.7
  86.4 0.1 add_convert_fusion
  86.4 2.9 %collective-permute-start.11 = (bf16[1024,128]{1,0:T(8,128)(2,1)S(1)}, bf16[1024,128]{1,0:T(8,128)(2,1)S(1)}, u32[]{:S(2)}, u32[]{:S(2)}) collective-permute-start(bf16[1024,128]{1,0:T(8,128)(2,1)S(1)} %add_convert_fusion), channel_id=1, source_target_pairs={{0,96},{16,112},{32,0},{48,16},{64,32},{80,48},{96,64},{112,80},{1... | collective-permute-start | bytes 786440 | tf_op jit(solution)/shard_map/ppermute | solution.py:349
  89.4 2.5 %collective-permute-done.8.c0 = bf16[1024,128]{1,0:T(8,128)(2,1)S(1)} collective-permute-done((bf16[1024,128]{1,0:T(8,128)(2,1)S(1)}, bf16[1024,128]{1,0:T(8,128)(2,1)S(1)}, u32[]{:S(2)}, u32[]{:S(2)}) %collective-permute-start.8) | collective-permute-done | bytes 262176 | tf_op jit(solution)/shard_map/ppermute | solution.py:349
  91.9 4.6 %collective-permute-done.7.b0 = bf16[1024,128]{1,0:T(8,128)(2,1)S(1)} collective-permute-done((bf16[1024,128]{1,0:T(8,128)(2,1)S(1)}, bf16[1024,128]{1,0:T(8,128)(2,1)S(1)}, u32[]{:S(2)}, u32[]{:S(2)}) %collective-permute-start.7) | collective-permute-done | bytes 262176 | tf_op jit(solution)/shard_map/ppermute | solution.py:349
  96.5 0.1 collective-permute-done.11.c1
  96.6 0.2 own_sum.1
  96.8 0.8 copy-done.5
  97.6 5.7 %all-to-all-start.3 = ((bf16[32,64,128]{2,1,0:T(8,128)(2,1)}), bf16[32,64,128]{2,1,0:T(8,128)(2,1)S(1)}, u32[]{:S(2)}, u32[]{:S(2)}) async-start(bf16[32,64,128]{2,1,0:T(8,128)(2,1)} %bitcast.14), calls=%async_computation.3 | async-start | bytes 1048576 | tf_op jit(solution)/shard_map/all_to_all | solution.py:354
  103.4 0.0 copy-start.4
  103.4 1.3 %copy-done.4 = bf16[768,768]{1,0:T(8,128)(2,1)S(1)} copy-done((bf16[768,768]{1,0:T(8,128)(2,1)S(1)}, bf16[768,768]{1,0:T(8,128)(2,1)}, u32[]{:S(2)}) %copy-start.4) | copy-done | bytes 1179672
  104.7 3.2 %final.1 = bf16[4,64,768]{2,1,0:T(8,128)(2,1)} custom-call(bf16[16,3,48,256]{3,2,1,0:T(8,128)(2,1)} %all-to-all-done.2.g_ref, bf16[768,768]{1,0:T(8,128)(2,1)S(1)} %copy-done, bf16[768,768]{1,0:T(8,128)(2,1)S(1)} %copy-done.2, bf16[768,768]{1,0:T(8,128)(2,1)S(1)} %copy-done.4), custom_call_target="tpu_custom_call" | custom-call | tf_op jit(solution)/shard_map/final/pallas_call | solution.py:341
  107.8 7.4 %all-to-all-done.3 = bf16[32,64,128]{2,1,0:T(8,128)(2,1)S(1)} async-done(((bf16[32,64,128]{2,1,0:T(8,128)(2,1)}), bf16[32,64,128]{2,1,0:T(8,128)(2,1)S(1)}, u32[]{:S(2)}, u32[]{:S(2)}) %all-to-all-start.3) | async-done | bytes 524320 | tf_op jit(solution)/shard_map/all_to_all | solution.py:354
  115.2 2.1 %gpair.1 = bf16[64,128,128]{2,1,0:T(8,128)(2,1)} custom-call(bf16[2,16,64,128]{3,2,1,0:T(8,128)(2,1)S(1)} %bitcast.13, bf16[16,128]{1,0:T(8,128)(2,1)S(1)} %bitcast.16), custom_call_target="tpu_custom_call" | custom-call | tf_op jit(solution)/shard_map/gpair/pallas_call | solution.py:302
  (32 shorter events, 0.1 us)
Async XLA Ops:
  0.6 12.0 %copy-start.1 = (bf16[768,768]{1,0:T(8,128)(2,1)S(1)}, bf16[768,768]{1,0:T(8,128)(2,1)}, u32[]{:S(2)}) copy-start(bf16[768,768]{1,0:T(8,128)(2,1)} %wk_ref.3) | copy-start | bytes 3538948
  0.6 12.0 %copy-start.7 = (bf16[4,64,768]{2,1,0:T(8,128)(2,1)S(1)}, bf16[4,64,768]{2,1,0:T(8,128)(2,1)}, u32[]{:S(2)}) copy-start(bf16[4,64,768]{2,1,0:T(8,128)(2,1)} %x_ref.1) | copy-start | bytes 1179652
  4.3 8.4 %copy-start = (bf16[768,768]{1,0:T(8,128)(2,1)S(1)}, bf16[768,768]{1,0:T(8,128)(2,1)}, u32[]{:S(2)}) copy-start(bf16[768,768]{1,0:T(8,128)(2,1)} %wq_ref.3) | copy-start | bytes 3538948
  4.3 21.5 %all-to-all-start = ((bf16[32,80,128]{2,1,0:T(8,128)(2,1)}), bf16[32,80,128]{2,1,0:T(8,128)(2,1)S(1)}, u32[]{:S(2)}, u32[]{:S(2)}) async-start(bf16[32,80,128]{2,1,0:T(8,128)(2,1)} %bias_part.1), calls=%async_computation | async-start | bytes 1310720 | tf_op jit(solution)/shard_map/all_to_all | solution.py:354
  12.7 1.3 %copy-start.3 = (bf16[768,768]{1,0:T(8,128)(2,1)S(1)}, bf16[768,768]{1,0:T(8,128)(2,1)}, u32[]{:S(2)}) copy-start(bf16[768,768]{1,0:T(8,128)(2,1)} %wv_ref.3) | copy-start | bytes 3538948
  14.0 1.3 %copy-start.6 = (bf16[768,768]{1,0:T(8,128)(2,1)S(1)}, bf16[768,768]{1,0:T(8,128)(2,1)}, u32[]{:S(2)}) copy-start(bf16[768,768]{1,0:T(8,128)(2,1)} %wo_ref.1) | copy-start | bytes 3538948
  15.2 1.0 copy-start.8
  25.7 26.0 %all-to-all-start.1 = ((bf16[16,4,48,256]{3,2,1,0:T(8,128)(2,1)}), bf16[16,4,48,256]{3,2,1,0:T(8,128)(2,1)S(1)}, u32[]{:S(2)}, u32[]{:S(2)}) async-start(bf16[16,4,48,256]{3,2,1,0:T(8,128)(2,1)} %project.1), calls=%async_computation.1 | async-start | bytes 3145728 | tf_op jit(solution)/shard_map/all_to_all | solution.py:401
  30.3 10.8 %collective-permute-start = (bf16[1056,128]{1,0:T(8,128)(2,1)}, bf16[1056,128]{1,0:T(8,128)(2,1)}, u32[]{:S(2)}, u32[]{:S(2)}) collective-permute-start(bf16[1056,128]{1,0:T(8,128)(2,1)} %get-tuple-element.33.refs_0_.refs_4_), channel_id=1, source_target_pairs={{0,32},{16,48},{32,64},{48,80},{64,96},{80,112},{96,0},{112,16},{1... | collective-permute-start | bytes 811016 | tf_op jit(solution)/shard_map/ppermute | solution.py:349
  31.9 9.7 %collective-permute-start.1 = (bf16[1056,128]{1,0:T(8,128)(2,1)}, bf16[1056,128]{1,0:T(8,128)(2,1)}, u32[]{:S(2)}, u32[]{:S(2)}) collective-permute-start(bf16[1056,128]{1,0:T(8,128)(2,1)} %get-tuple-element.34.refs_1_.refs_5_), channel_id=1, source_target_pairs={{0,96},{16,112},{32,0},{48,16},{64,32},{80,48},{96,64},{112,80},{1... | collective-permute-start | bytes 811016 | tf_op jit(solution)/shard_map/ppermute | solution.py:349
  33.6 19.8 %collective-permute-start.3 = (bf16[1056,128]{1,0:T(8,128)(2,1)}, bf16[1056,128]{1,0:T(8,128)(2,1)S(1)}, u32[]{:S(2)}, u32[]{:S(2)}) collective-permute-start(bf16[1056,128]{1,0:T(8,128)(2,1)} %get-tuple-element.33.refs_0_.refs_4_), channel_id=1, source_target_pairs={{0,96},{16,112},{32,0},{48,16},{64,32},{80,48},{96,64},{112,80},{1... | collective-permute-start | bytes 811016 | tf_op jit(solution)/shard_map/ppermute | solution.py:349
  35.4 18.0 %collective-permute-start.2 = (bf16[1056,128]{1,0:T(8,128)(2,1)}, bf16[1056,128]{1,0:T(8,128)(2,1)S(1)}, u32[]{:S(2)}, u32[]{:S(2)}) collective-permute-start(bf16[1056,128]{1,0:T(8,128)(2,1)} %get-tuple-element.34.refs_1_.refs_5_), channel_id=1, source_target_pairs={{0,32},{16,48},{32,64},{48,80},{64,96},{80,112},{96,0},{112,16},{1... | collective-permute-start | bytes 811016 | tf_op jit(solution)/shard_map/ppermute | solution.py:349
  41.2 12.2 %collective-permute-start.4 = (bf16[1056,128]{1,0:T(8,128)(2,1)}, bf16[1056,128]{1,0:T(8,128)(2,1)}, u32[]{:S(2)}, u32[]{:S(2)}) collective-permute-start(bf16[1056,128]{1,0:T(8,128)(2,1)} %collective-permute-done.refs_2_.refs_6_), channel_id=1, source_target_pairs={{0,32},{16,48},{32,64},{48,80},{64,96},{80,112},{96,0},{112,16},{1... | collective-permute-start | bytes 811016 | tf_op jit(solution)/shard_map/ppermute | solution.py:349
  41.6 11.8 %collective-permute-start.5 = (bf16[1056,128]{1,0:T(8,128)(2,1)}, bf16[1056,128]{1,0:T(8,128)(2,1)}, u32[]{:S(2)}, u32[]{:S(2)}) collective-permute-start(bf16[1056,128]{1,0:T(8,128)(2,1)} %collective-permute-done.1.refs_3_.refs_7_), channel_id=1, source_target_pairs={{0,96},{16,112},{32,0},{48,16},{64,32},{80,48},{96,64},{112,80},{1... | collective-permute-start | bytes 811016 | tf_op jit(solution)/shard_map/ppermute | solution.py:349
  70.8 4.6 %copy-start.17 = (bf16[1024,128]{1,0:T(8,128)(2,1)S(1)}, bf16[1024,128]{1,0:T(8,128)(2,1)}, u32[]{:S(2)}) copy-start(bf16[1024,128]{1,0:T(8,128)(2,1)} %get-tuple-element.52) | copy-start | bytes 786436
  70.8 6.3 %copy-start.16 = (bf16[1024,128]{1,0:T(8,128)(2,1)S(1)}, bf16[1024,128]{1,0:T(8,128)(2,1)}, u32[]{:S(2)}) copy-start(bf16[1024,128]{1,0:T(8,128)(2,1)} %get-tuple-element.57) | copy-start | bytes 786436
  70.8 7.9 %copy-start.15 = (bf16[1024,128]{1,0:T(8,128)(2,1)S(1)}, bf16[1024,128]{1,0:T(8,128)(2,1)}, u32[]{:S(2)}) copy-start(bf16[1024,128]{1,0:T(8,128)(2,1)} %get-tuple-element.53) | copy-start | bytes 786436
  70.8 9.7 %copy-start.14 = (bf16[1024,128]{1,0:T(8,128)(2,1)S(1)}, bf16[1024,128]{1,0:T(8,128)(2,1)}, u32[]{:S(2)}) copy-start(bf16[1024,128]{1,0:T(8,128)(2,1)} %get-tuple-element.55) | copy-start | bytes 786436
  70.8 15.0 %copy-start.13 = (bf16[1024,128]{1,0:T(8,128)(2,1)S(1)}, bf16[1024,128]{1,0:T(8,128)(2,1)}, u32[]{:S(2)}) copy-start(bf16[1024,128]{1,0:T(8,128)(2,1)} %get-tuple-element.51) | copy-start | bytes 786436
  70.8 15.5 %copy-start.12 = (bf16[1024,128]{1,0:T(8,128)(2,1)S(1)}, bf16[1024,128]{1,0:T(8,128)(2,1)}, u32[]{:S(2)}) copy-start(bf16[1024,128]{1,0:T(8,128)(2,1)} %get-tuple-element.56) | copy-start | bytes 786436
  70.9 26.8 %all-to-all-start.2 = ((bf16[16,3,48,256]{3,2,1,0:T(8,128)(2,1)}), bf16[16,3,48,256]{3,2,1,0:T(8,128)(2,1)}, u32[]{:S(2)}, u32[]{:S(2)}) async-start(bf16[16,3,48,256]{3,2,1,0:T(8,128)(2,1)} %get-tuple-element.49), calls=%async_computation.2 | async-start | bytes 2359296 | tf_op jit(solution)/shard_map/all_to_all | solution.py:405
  75.4 21.2 %copy-start.9 = (bf16[1024,128]{1,0:T(8,128)(2,1)S(1)}, bf16[1024,128]{1,0:T(8,128)(2,1)}, u32[]{:S(2)}) copy-start(bf16[1024,128]{1,0:T(8,128)(2,1)} %get-tuple-element.50.a0) | copy-start | bytes 786436
  75.4 21.2 %copy-start.10 = (bf16[1024,128]{1,0:T(8,128)(2,1)S(1)}, bf16[1024,128]{1,0:T(8,128)(2,1)}, u32[]{:S(2)}) copy-start(bf16[1024,128]{1,0:T(8,128)(2,1)} %get-tuple-element.54.a1) | copy-start | bytes 786436
  75.4 10.4 %collective-permute-start.6 = (bf16[1024,128]{1,0:T(8,128)(2,1)S(1)}, bf16[1024,128]{1,0:T(8,128)(2,1)S(1)}, u32[]{:S(2)}, u32[]{:S(2)}) collective-permute-start(bf16[1024,128]{1,0:T(8,128)(2,1)S(1)} %copy-done.17), channel_id=1, source_target_pairs={{0,32},{16,48},{32,64},{48,80},{64,96},{80,112},{96,0},{112,16},{1... | collective-permute-start | bytes 786440 | tf_op jit(solution)/shard_map/ppermute | solution.py:349
  77.1 9.3 %collective-permute-start.10 = (bf16[1024,128]{1,0:T(8,128)(2,1)S(1)}, bf16[1024,128]{1,0:T(8,128)(2,1)S(1)}, u32[]{:S(2)}, u32[]{:S(2)}) collective-permute-start(bf16[1024,128]{1,0:T(8,128)(2,1)S(1)} %copy-done.16), channel_id=1, source_target_pairs={{0,96},{16,112},{32,0},{48,16},{64,32},{80,48},{96,64},{112,80},{1... | collective-permute-start | bytes 786440 | tf_op jit(solution)/shard_map/ppermute | solution.py:349
  78.7 13.1 %collective-permute-start.8 = (bf16[1024,128]{1,0:T(8,128)(2,1)S(1)}, bf16[1024,128]{1,0:T(8,128)(2,1)S(1)}, u32[]{:S(2)}, u32[]{:S(2)}) collective-permute-start(bf16[1024,128]{1,0:T(8,128)(2,1)S(1)} %copy-done.15), channel_id=1, source_target_pairs={{0,96},{16,112},{32,0},{48,16},{64,32},{80,48},{96,64},{112,80},{1... | collective-permute-start | bytes 786440 | tf_op jit(solution)/shard_map/ppermute | solution.py:349
  80.5 11.3 %collective-permute-start.9 = (bf16[1024,128]{1,0:T(8,128)(2,1)S(1)}, bf16[1024,128]{1,0:T(8,128)(2,1)S(1)}, u32[]{:S(2)}, u32[]{:S(2)}) collective-permute-start(bf16[1024,128]{1,0:T(8,128)(2,1)S(1)} %copy-done.14), channel_id=1, source_target_pairs={{0,32},{16,48},{32,64},{48,80},{64,96},{80,112},{96,0},{112,16},{1... | collective-permute-start | bytes 786440 | tf_op jit(solution)/shard_map/ppermute | solution.py:349
  85.9 10.6 %collective-permute-start.7 = (bf16[1024,128]{1,0:T(8,128)(2,1)S(1)}, bf16[1024,128]{1,0:T(8,128)(2,1)S(1)}, u32[]{:S(2)}, u32[]{:S(2)}) collective-permute-start(bf16[1024,128]{1,0:T(8,128)(2,1)S(1)} %add_convert_fusion.1), channel_id=1, source_target_pairs={{0,32},{16,48},{32,64},{48,80},{64,96},{80,112},{96,0},{112,16},{1... | collective-permute-start | bytes 786440 | tf_op jit(solution)/shard_map/ppermute | solution.py:349
  86.4 10.2 %collective-permute-start.11 = (bf16[1024,128]{1,0:T(8,128)(2,1)S(1)}, bf16[1024,128]{1,0:T(8,128)(2,1)S(1)}, u32[]{:S(2)}, u32[]{:S(2)}) collective-permute-start(bf16[1024,128]{1,0:T(8,128)(2,1)S(1)} %add_convert_fusion), channel_id=1, source_target_pairs={{0,96},{16,112},{32,0},{48,16},{64,32},{80,48},{96,64},{112,80},{1... | collective-permute-start | bytes 786440 | tf_op jit(solution)/shard_map/ppermute | solution.py:349
  96.6 6.8 %copy-start.2 = (bf16[768,768]{1,0:T(8,128)(2,1)S(1)}, bf16[768,768]{1,0:T(8,128)(2,1)}, u32[]{:S(2)}) copy-start(bf16[768,768]{1,0:T(8,128)(2,1)} %wk_ref.3) | copy-start | bytes 3538948
  96.8 0.8 copy-start.5
  97.6 17.6 %all-to-all-start.3 = ((bf16[32,64,128]{2,1,0:T(8,128)(2,1)}), bf16[32,64,128]{2,1,0:T(8,128)(2,1)S(1)}, u32[]{:S(2)}, u32[]{:S(2)}) async-start(bf16[32,64,128]{2,1,0:T(8,128)(2,1)} %bitcast.14), calls=%async_computation.3 | async-start | bytes 1048576 | tf_op jit(solution)/shard_map/all_to_all | solution.py:354
  103.4 1.3 %copy-start.4 = (bf16[768,768]{1,0:T(8,128)(2,1)S(1)}, bf16[768,768]{1,0:T(8,128)(2,1)}, u32[]{:S(2)}) copy-start(bf16[768,768]{1,0:T(8,128)(2,1)} %wv_ref.3) | copy-start | bytes 3538948
  104.7 10.6 %copy-start.11 = (bf16[128,16]{0,1:T(8,128)(2,1)S(1)}, bf16[128,16]{0,1:T(8,128)(2,1)}, u32[]{:S(2)}) copy-start(bf16[128,16]{0,1:T(8,128)(2,1)} %param.14) | copy-start | bytes 12292

commit v7 on v6

--- a/solution.py
+++ b/solution.py
@@ -52,7 +52,7 @@
 VMEM_ATT = 40
 NEAR = 8.0
 STEEP = 18.8
-EARLY, LATE = (0, 1, 2, 5), (3, 4, 6, 7)
+EARLY, LATE = (0, 1, 2, 5, 3, 4), (6, 7)
 
 
 def decode_rows(codes, every, group):
@@ -85,7 +85,7 @@
 
 
 def attend_body(scale, steps, order_ref, *refs):
-    early_refs, code_refs, top_refs, refs = refs[:4], refs[4:8], refs[8:12], refs[12:]
+    early_refs, code_refs, top_refs, refs = refs[:6], refs[6:8], refs[8:10], refs[10:]
     (qt_ref, ot_ref, kt_ref, vt_ref, k_ref), refs = refs[:5], refs[5:]
     dbias_refs, refs = refs[:8], refs[8:]
     g_ref, s_ref, dp_ref, p_ref, ds_ref, acc_ref, dqt_ref, dkt_ref, dvt_ref, bias_scr = refs
@@ -98,7 +98,7 @@
         dvt_ref[...] = jnp.zeros_like(dvt_ref)
 
     def all_bias():
-        for n in range(4):
+        for n in range(2):
             for part in range(TILE // GROUP):
                 start = part * GROUP
                 codes, group = code_refs[n][start:start + GROUP, :], step * (TILE // GROUP) + part
@@ -114,7 +114,7 @@
         group = 16
         for g in range(TILE // group):
             rows = slice(g * group, g * group + group)
-            late = [bias_scr[rows, n * 128:n * 128 + 128] for n in range(4)]
+            late = [bias_scr[rows, n * 128:n * 128 + 128] for n in range(2)]
             held = dict(zip(EARLY + LATE, [ref[rows, :] for ref in early_refs] + late))
             bias = jnp.concatenate([held[u] for u in range(8)], axis=1)
             s = s_ref[b % 2, rows, :] * (scale * LOG2E) + bias
@@ -182,13 +182,13 @@
         functools.partial(attend_body, scale, steps),
         grid=(steps,),
         out_shape=[pltpu.HBM((TOK, 128), BF16)] * 8 + [jax.ShapeDtypeStruct((16, 3, HD, 256), BF16)],
-        in_specs=[pl.BlockSpec(memory_space=pltpu.SMEM)] + [dbias_t] * 8 + [top_t] * 4 + [vm] * 5,
+        in_specs=[pl.BlockSpec(memory_space=pltpu.SMEM)] + [dbias_t] * 8 + [top_t] * 2 + [vm] * 5,
         out_specs=[dbias_t] * 8 + [g_spec],
         scratch_shapes=[
             pltpu.VMEM((2, TILE, TOK), F32), pltpu.VMEM((2, TILE, TOK), F32),
             pltpu.VMEM((2, TILE, TOK), BF16), pltpu.VMEM((2, TILE, TOK), BF16),
             pltpu.VMEM((TILE, TOK), F32), pltpu.VMEM((steps, NB, HD, TILE), BF16),
-            pltpu.VMEM((NB, HD, TOK), F32), pltpu.VMEM((NB, HD, TOK), F32), pltpu.VMEM((TILE, 512), F32),
+            pltpu.VMEM((NB, HD, TOK), F32), pltpu.VMEM((NB, HD, TOK), F32), pltpu.VMEM((TILE, 256), F32),
         ],
         compiler_params=pltpu.CompilerParams(vmem_limit_bytes=VMEM_ATT * 2**20),
         cost_estimate=pl.CostEstimate(flops=10**6, bytes_accessed=2**10, transcendentals=0),
@@ -400,7 +400,7 @@
     bias, sent = lax.optimization_barrier((bias, sent))
     received = lax.all_to_all(sent, "tok", 0, 0)
     blocks = gather_blocks(unpack(bias.reshape(2, 16, 80, 128)))
-    received, ready = lax.optimization_barrier((received, early([blocks[u] for u in EARLY])))
+    received, ready = lax.optimization_barrier((received, early([blocks[u] for u in EARLY[:4]]) + early([blocks[u] for u in EARLY[4:]])))
     dbias, grads = attend(order, ready, [blocks[u] for u in LATE], prep(order, received))
     grads = lax.all_to_all(grads, "tok", 0, 0)
     dbias = scatter_blocks(dbias)

time: 119 us -> 120 us (level)
  waiting for transfers between devices: 35.7 us -> 32.2 us
  Pallas kernels: 35.3 us -> 38.7 us
    pallas_call x1 -> x2, Pallas kernels: 3.8 us -> 7.14 us  [early(): pl.pallas_call(early_body, grid=(TOK // GROUP,), out_shape=[pltpu.HBM((TO...]
    all_to_all x1, waiting for transfers between devices: 3.37 us -> 0.12 us  [local(): received = lax.all_to_all(sent, 'tok', 0, 0)]
    all_to_all x1, starting transfers between devices: 4.54 us -> 5.75 us  [local(): grads = lax.all_to_all(grads, 'tok', 0, 0)]
  transfers between devices with their start and end apart: 16 -> 16, of which waited for: 8 -> 8; matrix products, arithmetic and copies ran while one was open for 0% -> 0% of each run, Pallas kernels for 10% -> 13%
where the time goes in v7:
time: 120 us; the launch traced here: 119 us
  starting transfers between devices  40.8 us (34%)
  Pallas kernels  38.7 us (32%)
  waiting for transfers between devices  32.2 us (27%)
  local copies, waits for them, and re-layouts  5.75 us (5%)
    ppermute x12, waiting for transfers between devices, shift_y(): lax.ppermute(x, 'sample', [(i, (i // 2 + d) % 4 * 2 + i % 2) for i in ran...  17.7 us
    pallas_call x1, Pallas kernels, attend(): pl.pallas_call(functools.partial(attend_body, scale, steps), grid=(steps,...  17.5 us
    ppermute x12, starting transfers between devices, shift_y(): lax.ppermute(x, 'sample', [(i, (i // 2 + d) % 4 * 2 + i % 2) for i in ran...  17.2 us
    all_to_all x2, waiting for transfers between devices, exchange(): return lax.all_to_all(x, ('sample', 'tok'), 0, 0, axis_index_groups=groups)  14.4 us
    all_to_all x2, starting transfers between devices, exchange(): return lax.all_to_all(x, ('sample', 'tok'), 0, 0, axis_index_groups=groups)  14.1 us
    pallas_call x2, Pallas kernels, early(): pl.pallas_call(early_body, grid=(TOK // GROUP,), out_shape=[pltpu.HBM((TO...  7.14 us
    all_to_all x1, starting transfers between devices, local(): grads = lax.all_to_all(grads, 'tok', 0, 0)  5.75 us
    unnamed x36, local copies, waits for them, and re-layouts  5.66 us
  transfers between devices with their start and end apart: 16, of which 8 were waited for; matrix products, arithmetic and copies ran while one was open for 0% of the time, Pallas kernels for 13%

profile of v7, /device:TPU:0, one launch (start us, length us, event | category | flops | bytes accessed | tf_op | source)
XLA Modules:
  0.0 118.5 jit_solution(16104017106864231636)
XLA Ops:
  0.6 0.0 copy-start.1
  0.7 3.6 %bias_part.1 = bf16[32,80,128]{2,1,0:T(8,128)(2,1)} custom-call(bf16[64,128,128]{2,1,0:T(8,128)(2,1)} %pair_ref.1, bf16[16,128]{1,0:T(8,128)(2,1)} %bitcast.15), custom_call_target="tpu_custom_call" | custom-call | tf_op jit(solution)/shard_map/bias_part/pallas_call | solution.py:257
  4.3 8.4 %all-to-all-start = ((bf16[32,80,128]{2,1,0:T(8,128)(2,1)}), bf16[32,80,128]{2,1,0:T(8,128)(2,1)S(1)}, u32[]{:S(2)}, u32[]{:S(2)}) async-start(bf16[32,80,128]{2,1,0:T(8,128)(2,1)} %bias_part.1), calls=%async_computation | async-start | bytes 1310720 | tf_op jit(solution)/shard_map/all_to_all | solution.py:354
  12.7 0.0 copy-start.3
  12.7 1.3 %copy-done.3 = bf16[768,768]{1,0:T(8,128)(2,1)S(1)} copy-done((bf16[768,768]{1,0:T(8,128)(2,1)S(1)}, bf16[768,768]{1,0:T(8,128)(2,1)}, u32[]{:S(2)}) %copy-start.3) | copy-done | bytes 1179672
  14.0 1.3 %copy-done.6 = bf16[768,768]{1,0:T(8,128)(2,1)S(1)} copy-done((bf16[768,768]{1,0:T(8,128)(2,1)S(1)}, bf16[768,768]{1,0:T(8,128)(2,1)}, u32[]{:S(2)}) %copy-start.6) | copy-done | bytes 1179672
  15.2 1.0 copy-done.8
  16.2 2.5 %project.1 = bf16[16,4,48,256]{3,2,1,0:T(8,128)(2,1)} custom-call(bf16[4,64,768]{2,1,0:T(8,128)(2,1)S(1)} %copy-done.7, bf16[4,64,768]{2,1,0:T(8,128)(2,1)S(1)} %copy-done.8, bf16[768,768]{1,0:T(8,128)(2,1)S(1)} %copy-done, bf16[768,768]{1,0:T(8,128)(2,1)S(1)} %copy-done.1, bf16[768,768]{1,0:T(8,128)(2,1)S(1)} %copy-done.3, bf16[768,768]{1,0:T(8,128)(2,1)S(1)} %copy-done.6), custom_call_target="tpu_custom_call" | custom-call | tf_op jit(solution)/shard_map/project/pallas_call | solution.py:324
  18.8 7.0 %all-to-all-done = bf16[32,80,128]{2,1,0:T(8,128)(2,1)S(1)} async-done(((bf16[32,80,128]{2,1,0:T(8,128)(2,1)}), bf16[32,80,128]{2,1,0:T(8,128)(2,1)S(1)}, u32[]{:S(2)}, u32[]{:S(2)}) %all-to-all-start) | async-done | bytes 655392 | tf_op jit(solution)/shard_map/all_to_all | solution.py:354
  25.7 3.7 %all-to-all-start.1 = ((bf16[16,4,48,256]{3,2,1,0:T(8,128)(2,1)}), bf16[16,4,48,256]{3,2,1,0:T(8,128)(2,1)S(1)}, u32[]{:S(2)}, u32[]{:S(2)}) async-start(bf16[16,4,48,256]{3,2,1,0:T(8,128)(2,1)} %project.1), calls=%async_computation.1 | async-start | bytes 3145728 | tf_op jit(solution)/shard_map/all_to_all | solution.py:401
  29.5 0.9 unpack.1
  30.3 1.6 %collective-permute-start = (bf16[1056,128]{1,0:T(8,128)(2,1)}, bf16[1056,128]{1,0:T(8,128)(2,1)S(1)}, u32[]{:S(2)}, u32[]{:S(2)}) collective-permute-start(bf16[1056,128]{1,0:T(8,128)(2,1)} %get-tuple-element.37.refs_0_.refs_4_), channel_id=1, source_target_pairs={{0,32},{16,48},{32,64},{48,80},{64,96},{80,112},{96,0},{112,16},{1... | collective-permute-start | bytes 811016 | tf_op jit(solution)/shard_map/ppermute | solution.py:349
  31.9 1.7 %collective-permute-start.1 = (bf16[1056,128]{1,0:T(8,128)(2,1)}, bf16[1056,128]{1,0:T(8,128)(2,1)S(1)}, u32[]{:S(2)}, u32[]{:S(2)}) collective-permute-start(bf16[1056,128]{1,0:T(8,128)(2,1)} %get-tuple-element.38.refs_1_.refs_5_), channel_id=1, source_target_pairs={{0,96},{16,112},{32,0},{48,16},{64,32},{80,48},{96,64},{112,80},{1... | collective-permute-start | bytes 811016 | tf_op jit(solution)/shard_map/ppermute | solution.py:349
  33.6 1.8 %collective-permute-start.3 = (bf16[1056,128]{1,0:T(8,128)(2,1)}, bf16[1056,128]{1,0:T(8,128)(2,1)}, u32[]{:S(2)}, u32[]{:S(2)}) collective-permute-start(bf16[1056,128]{1,0:T(8,128)(2,1)} %get-tuple-element.37.refs_0_.refs_4_), channel_id=1, source_target_pairs={{0,96},{16,112},{32,0},{48,16},{64,32},{80,48},{96,64},{112,80},{1... | collective-permute-start | bytes 811016 | tf_op jit(solution)/shard_map/ppermute | solution.py:349
  35.4 0.2 collective-permute-start.2
  35.6 5.5 %collective-permute-done.refs_2_.refs_6_ = bf16[1056,128]{1,0:T(8,128)(2,1)S(1)} collective-permute-done((bf16[1056,128]{1,0:T(8,128)(2,1)}, bf16[1056,128]{1,0:T(8,128)(2,1)S(1)}, u32[]{:S(2)}, u32[]{:S(2)}) %collective-permute-start) | collective-permute-done | bytes 270368 | tf_op jit(solution)/shard_map/ppermute | solution.py:349
  41.1 0.4 collective-permute-start.4
  41.4 0.0 collective-permute-done.1.refs_3_.refs_7_
  41.5 2.9 %collective-permute-start.5 = (bf16[1056,128]{1,0:T(8,128)(2,1)S(1)}, bf16[1056,128]{1,0:T(8,128)(2,1)}, u32[]{:S(2)}, u32[]{:S(2)}) collective-permute-start(bf16[1056,128]{1,0:T(8,128)(2,1)S(1)} %collective-permute-done.1.refs_3_.refs_7_), channel_id=1, source_target_pairs={{0,96},{16,112},{32,0},{48,16},{64,32},{80,48},{96,64},{112,80},{1... | collective-permute-start | bytes 811016 | tf_op jit(solution)/shard_map/ppermute | solution.py:349
  44.3 0.1 stack.35.order_ref
  44.4 3.7 %early.2 = (f32[1024,128]{1,0:T(8,128)}, f32[1024,128]{1,0:T(8,128)}, f32[1024,128]{1,0:T(8,128)}, f32[1024,128]{1,0:T(8,128)}) custom-call(bf16[1056,128]{1,0:T(8,128)(2,1)} %get-tuple-element.37.refs_0_.refs_4_, bf16[1056,128]{1,0:T(8,128)(2,1)} %get-tuple-element.38.refs_1_.refs_5_, bf16[1056,128]{1,0:T(8,128)(2,1)S(1)} %collective-permute-done.refs_2_.refs_6_, ...), custom_call_target="tpu_custom_call" | custom-call | tf_op jit(solution)/shard_map/early/pallas_call | solution.py:80
  48.2 3.4 %early.3 = (f32[1024,128]{1,0:T(8,128)}, f32[1024,128]{1,0:T(8,128)}) custom-call(bf16[1056,128]{1,0:T(8,128)(2,1)} %collective-permute-done.2.refs_0_.refs_2_, bf16[1056,128]{1,0:T(8,128)(2,1)} %collective-permute-done.3.refs_1_.refs_3_, bf16[1056,128]{1,0:T(8,128)(2,1)} %collective-permute-done.2.refs_0_.refs_2_, ...), custom_call_target="tpu_custom_call" | custom-call | tf_op jit(solution)/shard_map/early/pallas_call | solution.py:80
  51.6 0.1 all-to-all-done.1.r_ref
  51.7 1.6 %prep.1 = (bf16[4,48,1024]{2,1,0:T(8,128)(2,1)S(1)}, bf16[4,48,1024]{2,1,0:T(8,128)(2,1)S(1)}, bf16[4,48,1024]{2,1,0:T(8,128)(2,1)S(1)}, bf16[4,48,1024]{2,1,0:T(8,128)(2,1)S(1)}, bf16[4,1024,48]{2,1,0:T(8,128)(2,1)S(1)}) custom-call(s32[8]{0:T(128)S(1)} %stack.35.order_ref, bf16[16,4,48,256]{3,2,1,0:T(8,128)(2,1)S(1)} %all-to-all-done.1.r_ref), custom_call_target="tpu_custom_call" | custom-call | tf_op jit(solution)/shard_map/prep/pallas_call | solution.py:40
  53.3 17.5 %attend.1 = (bf16[1024,128]{1,0:T(8,128)(2,1)}, bf16[1024,128]{1,0:T(8,128)(2,1)}, bf16[1024,128]{1,0:T(8,128)(2,1)}, bf16[1024,128]{1,0:T(8,128)(2,1)}, bf16[10...) custom-call(s32[8]{0:T(128)S(1)} %stack.35.order_ref, ...), custom_call_target="tpu_custom_call" | custom-call | flops 1000000 | bytes 1024 | tf_op jit(solution)/shard_map/attend/pallas_call | solution.py:181
  70.9 5.7 %all-to-all-start.2 = ((bf16[16,3,48,256]{3,2,1,0:T(8,128)(2,1)}), bf16[16,3,48,256]{3,2,1,0:T(8,128)(2,1)}, u32[]{:S(2)}, u32[]{:S(2)}) async-start(bf16[16,3,48,256]{3,2,1,0:T(8,128)(2,1)} %get-tuple-element.57), calls=%async_computation.2 | async-start | bytes 2359296 | tf_op jit(solution)/shard_map/all_to_all | solution.py:405
  76.7 0.0 copy-start.9
  76.7 0.9 collective-permute-start.6
  77.6 2.5 %collective-permute-start.10 = (bf16[1024,128]{1,0:T(8,128)(2,1)S(1)}, bf16[1024,128]{1,0:T(8,128)(2,1)S(1)}, u32[]{:S(2)}, u32[]{:S(2)}) collective-permute-start(bf16[1024,128]{1,0:T(8,128)(2,1)S(1)} %copy-done.16), channel_id=1, source_target_pairs={{0,96},{16,112},{32,0},{48,16},{64,32},{80,48},{96,64},{112,80},{1... | collective-permute-start | bytes 786440 | tf_op jit(solution)/shard_map/ppermute | solution.py:349
  80.0 0.9 collective-permute-start.8
  80.9 1.2 collective-permute-start.9
  82.1 5.1 %collective-permute-done.6 = bf16[1024,128]{1,0:T(8,128)(2,1)S(1)} collective-permute-done((bf16[1024,128]{1,0:T(8,128)(2,1)S(1)}, bf16[1024,128]{1,0:T(8,128)(2,1)S(1)}, u32[]{:S(2)}, u32[]{:S(2)}) %collective-permute-start.6) | collective-permute-done | bytes 262176 | tf_op jit(solution)/shard_map/ppermute | solution.py:349
  87.1 0.1 add_convert_fusion.1
  87.2 0.1 collective-permute-start.7
  87.3 0.1 add_convert_fusion
  87.4 3.3 %collective-permute-start.11 = (bf16[1024,128]{1,0:T(8,128)(2,1)S(1)}, bf16[1024,128]{1,0:T(8,128)(2,1)S(1)}, u32[]{:S(2)}, u32[]{:S(2)}) collective-permute-start(bf16[1024,128]{1,0:T(8,128)(2,1)S(1)} %add_convert_fusion), channel_id=1, source_target_pairs={{0,96},{16,112},{32,0},{48,16},{64,32},{80,48},{96,64},{112,80},{1... | collective-permute-start | bytes 786440 | tf_op jit(solution)/shard_map/ppermute | solution.py:349
  90.7 1.7 %collective-permute-done.8.c0 = bf16[1024,128]{1,0:T(8,128)(2,1)S(1)} collective-permute-done((bf16[1024,128]{1,0:T(8,128)(2,1)S(1)}, bf16[1024,128]{1,0:T(8,128)(2,1)S(1)}, u32[]{:S(2)}, u32[]{:S(2)}) %collective-permute-start.8) | collective-permute-done | bytes 262176 | tf_op jit(solution)/shard_map/ppermute | solution.py:349
  92.4 0.4 collective-permute-done.9.b1
  92.7 5.1 %collective-permute-done.7.b0 = bf16[1024,128]{1,0:T(8,128)(2,1)S(1)} collective-permute-done((bf16[1024,128]{1,0:T(8,128)(2,1)S(1)}, bf16[1024,128]{1,0:T(8,128)(2,1)S(1)}, u32[]{:S(2)}, u32[]{:S(2)}) %collective-permute-start.7) | collective-permute-done | bytes 262176 | tf_op jit(solution)/shard_map/ppermute | solution.py:349
  97.8 0.0 copy-start.2
  97.8 0.2 own_sum.1
  98.0 0.8 copy-done.5
  98.8 5.7 %all-to-all-start.3 = ((bf16[32,64,128]{2,1,0:T(8,128)(2,1)}), bf16[32,64,128]{2,1,0:T(8,128)(2,1)S(1)}, u32[]{:S(2)}, u32[]{:S(2)}) async-start(bf16[32,64,128]{2,1,0:T(8,128)(2,1)} %bitcast.14), calls=%async_computation.3 | async-start | bytes 1048576 | tf_op jit(solution)/shard_map/all_to_all | solution.py:354
  104.6 0.0 copy-start.4
  104.6 1.3 %copy-done.4 = bf16[768,768]{1,0:T(8,128)(2,1)S(1)} copy-done((bf16[768,768]{1,0:T(8,128)(2,1)S(1)}, bf16[768,768]{1,0:T(8,128)(2,1)}, u32[]{:S(2)}) %copy-start.4) | copy-done | bytes 1179672
  105.9 3.2 %final.1 = bf16[4,64,768]{2,1,0:T(8,128)(2,1)} custom-call(bf16[16,3,48,256]{3,2,1,0:T(8,128)(2,1)} %all-to-all-done.2.g_ref, bf16[768,768]{1,0:T(8,128)(2,1)S(1)} %copy-done, bf16[768,768]{1,0:T(8,128)(2,1)S(1)} %copy-done.2, bf16[768,768]{1,0:T(8,128)(2,1)S(1)} %copy-done.4), custom_call_target="tpu_custom_call" | custom-call | tf_op jit(solution)/shard_map/final/pallas_call | solution.py:341
  109.0 7.4 %all-to-all-done.3 = bf16[32,64,128]{2,1,0:T(8,128)(2,1)S(1)} async-done(((bf16[32,64,128]{2,1,0:T(8,128)(2,1)}), bf16[32,64,128]{2,1,0:T(8,128)(2,1)S(1)}, u32[]{:S(2)}, u32[]{:S(2)}) %all-to-all-start.3) | async-done | bytes 524320 | tf_op jit(solution)/shard_map/all_to_all | solution.py:354
  116.5 2.1 %gpair.1 = bf16[64,128,128]{2,1,0:T(8,128)(2,1)} custom-call(bf16[2,16,64,128]{3,2,1,0:T(8,128)(2,1)S(1)} %bitcast.13, bf16[16,128]{1,0:T(8,128)(2,1)S(1)} %bitcast.16), custom_call_target="tpu_custom_call" | custom-call | tf_op jit(solution)/shard_map/gpair/pallas_call | solution.py:302
  (33 shorter events, 0.1 us)
Async XLA Ops:
  0.6 12.0 %copy-start.1 = (bf16[768,768]{1,0:T(8,128)(2,1)S(1)}, bf16[768,768]{1,0:T(8,128)(2,1)}, u32[]{:S(2)}) copy-start(bf16[768,768]{1,0:T(8,128)(2,1)} %wk_ref.3) | copy-start | bytes 3538948
  0.6 12.0 %copy-start.7 = (bf16[4,64,768]{2,1,0:T(8,128)(2,1)S(1)}, bf16[4,64,768]{2,1,0:T(8,128)(2,1)}, u32[]{:S(2)}) copy-start(bf16[4,64,768]{2,1,0:T(8,128)(2,1)} %x_ref.1) | copy-start | bytes 1179652
  4.3 8.4 %copy-start = (bf16[768,768]{1,0:T(8,128)(2,1)S(1)}, bf16[768,768]{1,0:T(8,128)(2,1)}, u32[]{:S(2)}) copy-start(bf16[768,768]{1,0:T(8,128)(2,1)} %wq_ref.3) | copy-start | bytes 3538948
  4.3 21.5 %all-to-all-start = ((bf16[32,80,128]{2,1,0:T(8,128)(2,1)}), bf16[32,80,128]{2,1,0:T(8,128)(2,1)S(1)}, u32[]{:S(2)}, u32[]{:S(2)}) async-start(bf16[32,80,128]{2,1,0:T(8,128)(2,1)} %bias_part.1), calls=%async_computation | async-start | bytes 1310720 | tf_op jit(solution)/shard_map/all_to_all | solution.py:354
  12.7 1.3 %copy-start.3 = (bf16[768,768]{1,0:T(8,128)(2,1)S(1)}, bf16[768,768]{1,0:T(8,128)(2,1)}, u32[]{:S(2)}) copy-start(bf16[768,768]{1,0:T(8,128)(2,1)} %wv_ref.3) | copy-start | bytes 3538948
  13.9 1.3 %copy-start.6 = (bf16[768,768]{1,0:T(8,128)(2,1)S(1)}, bf16[768,768]{1,0:T(8,128)(2,1)}, u32[]{:S(2)}) copy-start(bf16[768,768]{1,0:T(8,128)(2,1)} %wo_ref.1) | copy-start | bytes 3538948
  15.2 1.0 copy-start.8
  25.7 26.0 %all-to-all-start.1 = ((bf16[16,4,48,256]{3,2,1,0:T(8,128)(2,1)}), bf16[16,4,48,256]{3,2,1,0:T(8,128)(2,1)S(1)}, u32[]{:S(2)}, u32[]{:S(2)}) async-start(bf16[16,4,48,256]{3,2,1,0:T(8,128)(2,1)} %project.1), calls=%async_computation.1 | async-start | bytes 3145728 | tf_op jit(solution)/shard_map/all_to_all | solution.py:401
  30.3 10.7 %collective-permute-start = (bf16[1056,128]{1,0:T(8,128)(2,1)}, bf16[1056,128]{1,0:T(8,128)(2,1)S(1)}, u32[]{:S(2)}, u32[]{:S(2)}) collective-permute-start(bf16[1056,128]{1,0:T(8,128)(2,1)} %get-tuple-element.37.refs_0_.refs_4_), channel_id=1, source_target_pairs={{0,32},{16,48},{32,64},{48,80},{64,96},{80,112},{96,0},{112,16},{1... | collective-permute-start | bytes 811016 | tf_op jit(solution)/shard_map/ppermute | solution.py:349
  31.9 9.6 %collective-permute-start.1 = (bf16[1056,128]{1,0:T(8,128)(2,1)}, bf16[1056,128]{1,0:T(8,128)(2,1)S(1)}, u32[]{:S(2)}, u32[]{:S(2)}) collective-permute-start(bf16[1056,128]{1,0:T(8,128)(2,1)} %get-tuple-element.38.refs_1_.refs_5_), channel_id=1, source_target_pairs={{0,96},{16,112},{32,0},{48,16},{64,32},{80,48},{96,64},{112,80},{1... | collective-permute-start | bytes 811016 | tf_op jit(solution)/shard_map/ppermute | solution.py:349
  33.6 14.6 %collective-permute-start.3 = (bf16[1056,128]{1,0:T(8,128)(2,1)}, bf16[1056,128]{1,0:T(8,128)(2,1)}, u32[]{:S(2)}, u32[]{:S(2)}) collective-permute-start(bf16[1056,128]{1,0:T(8,128)(2,1)} %get-tuple-element.37.refs_0_.refs_4_), channel_id=1, source_target_pairs={{0,96},{16,112},{32,0},{48,16},{64,32},{80,48},{96,64},{112,80},{1... | collective-permute-start | bytes 811016 | tf_op jit(solution)/shard_map/ppermute | solution.py:349
  35.4 12.8 %collective-permute-start.2 = (bf16[1056,128]{1,0:T(8,128)(2,1)}, bf16[1056,128]{1,0:T(8,128)(2,1)}, u32[]{:S(2)}, u32[]{:S(2)}) collective-permute-start(bf16[1056,128]{1,0:T(8,128)(2,1)} %get-tuple-element.38.refs_1_.refs_5_), channel_id=1, source_target_pairs={{0,32},{16,48},{32,64},{48,80},{64,96},{80,112},{96,0},{112,16},{1... | collective-permute-start | bytes 811016 | tf_op jit(solution)/shard_map/ppermute | solution.py:349
  41.1 12.3 %collective-permute-start.4 = (bf16[1056,128]{1,0:T(8,128)(2,1)S(1)}, bf16[1056,128]{1,0:T(8,128)(2,1)}, u32[]{:S(2)}, u32[]{:S(2)}) collective-permute-start(bf16[1056,128]{1,0:T(8,128)(2,1)S(1)} %collective-permute-done.refs_2_.refs_6_), channel_id=1, source_target_pairs={{0,32},{16,48},{32,64},{48,80},{64,96},{80,112},{96,0},{112,16},{1... | collective-permute-start | bytes 811016 | tf_op jit(solution)/shard_map/ppermute | solution.py:349
  41.5 11.8 %collective-permute-start.5 = (bf16[1056,128]{1,0:T(8,128)(2,1)S(1)}, bf16[1056,128]{1,0:T(8,128)(2,1)}, u32[]{:S(2)}, u32[]{:S(2)}) collective-permute-start(bf16[1056,128]{1,0:T(8,128)(2,1)S(1)} %collective-permute-done.1.refs_3_.refs_7_), channel_id=1, source_target_pairs={{0,96},{16,112},{32,0},{48,16},{64,32},{80,48},{96,64},{112,80},{1... | collective-permute-start | bytes 811016 | tf_op jit(solution)/shard_map/ppermute | solution.py:349
  70.9 5.8 %copy-start.17 = (bf16[1024,128]{1,0:T(8,128)(2,1)S(1)}, bf16[1024,128]{1,0:T(8,128)(2,1)}, u32[]{:S(2)}) copy-start(bf16[1024,128]{1,0:T(8,128)(2,1)} %get-tuple-element.60) | copy-start | bytes 786436
  70.9 6.7 %copy-start.16 = (bf16[1024,128]{1,0:T(8,128)(2,1)S(1)}, bf16[1024,128]{1,0:T(8,128)(2,1)}, u32[]{:S(2)}) copy-start(bf16[1024,128]{1,0:T(8,128)(2,1)} %get-tuple-element.65) | copy-start | bytes 786436
  70.9 9.2 %copy-start.15 = (bf16[1024,128]{1,0:T(8,128)(2,1)S(1)}, bf16[1024,128]{1,0:T(8,128)(2,1)}, u32[]{:S(2)}) copy-start(bf16[1024,128]{1,0:T(8,128)(2,1)} %get-tuple-element.61) | copy-start | bytes 786436
  70.9 10.0 %copy-start.14 = (bf16[1024,128]{1,0:T(8,128)(2,1)S(1)}, bf16[1024,128]{1,0:T(8,128)(2,1)}, u32[]{:S(2)}) copy-start(bf16[1024,128]{1,0:T(8,128)(2,1)} %get-tuple-element.63) | copy-start | bytes 786436
  70.9 16.2 %copy-start.13 = (bf16[1024,128]{1,0:T(8,128)(2,1)S(1)}, bf16[1024,128]{1,0:T(8,128)(2,1)}, u32[]{:S(2)}) copy-start(bf16[1024,128]{1,0:T(8,128)(2,1)} %get-tuple-element.59) | copy-start | bytes 786436
  70.9 16.4 %copy-start.12 = (bf16[1024,128]{1,0:T(8,128)(2,1)S(1)}, bf16[1024,128]{1,0:T(8,128)(2,1)}, u32[]{:S(2)}) copy-start(bf16[1024,128]{1,0:T(8,128)(2,1)} %get-tuple-element.64) | copy-start | bytes 786436
  70.9 27.9 %all-to-all-start.2 = ((bf16[16,3,48,256]{3,2,1,0:T(8,128)(2,1)}), bf16[16,3,48,256]{3,2,1,0:T(8,128)(2,1)}, u32[]{:S(2)}, u32[]{:S(2)}) async-start(bf16[16,3,48,256]{3,2,1,0:T(8,128)(2,1)} %get-tuple-element.57), calls=%async_computation.2 | async-start | bytes 2359296 | tf_op jit(solution)/shard_map/all_to_all | solution.py:405
  76.7 21.1 %copy-start.9 = (bf16[1024,128]{1,0:T(8,128)(2,1)S(1)}, bf16[1024,128]{1,0:T(8,128)(2,1)}, u32[]{:S(2)}) copy-start(bf16[1024,128]{1,0:T(8,128)(2,1)} %get-tuple-element.58.a0) | copy-start | bytes 786436
  76.7 21.1 %copy-start.10 = (bf16[1024,128]{1,0:T(8,128)(2,1)S(1)}, bf16[1024,128]{1,0:T(8,128)(2,1)}, u32[]{:S(2)}) copy-start(bf16[1024,128]{1,0:T(8,128)(2,1)} %get-tuple-element.62.a1) | copy-start | bytes 786436
  76.7 10.4 %collective-permute-start.6 = (bf16[1024,128]{1,0:T(8,128)(2,1)S(1)}, bf16[1024,128]{1,0:T(8,128)(2,1)S(1)}, u32[]{:S(2)}, u32[]{:S(2)}) collective-permute-start(bf16[1024,128]{1,0:T(8,128)(2,1)S(1)} %copy-done.17), channel_id=1, source_target_pairs={{0,32},{16,48},{32,64},{48,80},{64,96},{80,112},{96,0},{112,16},{1... | collective-permute-start | bytes 786440 | tf_op jit(solution)/shard_map/ppermute | solution.py:349
  77.6 9.7 %collective-permute-start.10 = (bf16[1024,128]{1,0:T(8,128)(2,1)S(1)}, bf16[1024,128]{1,0:T(8,128)(2,1)S(1)}, u32[]{:S(2)}, u32[]{:S(2)}) collective-permute-start(bf16[1024,128]{1,0:T(8,128)(2,1)S(1)} %copy-done.16), channel_id=1, source_target_pairs={{0,96},{16,112},{32,0},{48,16},{64,32},{80,48},{96,64},{112,80},{1... | collective-permute-start | bytes 786440 | tf_op jit(solution)/shard_map/ppermute | solution.py:349
  80.0 12.3 %collective-permute-start.8 = (bf16[1024,128]{1,0:T(8,128)(2,1)S(1)}, bf16[1024,128]{1,0:T(8,128)(2,1)S(1)}, u32[]{:S(2)}, u32[]{:S(2)}) collective-permute-start(bf16[1024,128]{1,0:T(8,128)(2,1)S(1)} %copy-done.15), channel_id=1, source_target_pairs={{0,96},{16,112},{32,0},{48,16},{64,32},{80,48},{96,64},{112,80},{1... | collective-permute-start | bytes 786440 | tf_op jit(solution)/shard_map/ppermute | solution.py:349
  80.9 11.8 %collective-permute-start.9 = (bf16[1024,128]{1,0:T(8,128)(2,1)S(1)}, bf16[1024,128]{1,0:T(8,128)(2,1)S(1)}, u32[]{:S(2)}, u32[]{:S(2)}) collective-permute-start(bf16[1024,128]{1,0:T(8,128)(2,1)S(1)} %copy-done.14), channel_id=1, source_target_pairs={{0,32},{16,48},{32,64},{48,80},{64,96},{80,112},{96,0},{112,16},{1... | collective-permute-start | bytes 786440 | tf_op jit(solution)/shard_map/ppermute | solution.py:349
  87.2 10.6 %collective-permute-start.7 = (bf16[1024,128]{1,0:T(8,128)(2,1)S(1)}, bf16[1024,128]{1,0:T(8,128)(2,1)S(1)}, u32[]{:S(2)}, u32[]{:S(2)}) collective-permute-start(bf16[1024,128]{1,0:T(8,128)(2,1)S(1)} %add_convert_fusion.1), channel_id=1, source_target_pairs={{0,32},{16,48},{32,64},{48,80},{64,96},{80,112},{96,0},{112,16},{1... | collective-permute-start | bytes 786440 | tf_op jit(solution)/shard_map/ppermute | solution.py:349
  87.4 10.4 %collective-permute-start.11 = (bf16[1024,128]{1,0:T(8,128)(2,1)S(1)}, bf16[1024,128]{1,0:T(8,128)(2,1)S(1)}, u32[]{:S(2)}, u32[]{:S(2)}) collective-permute-start(bf16[1024,128]{1,0:T(8,128)(2,1)S(1)} %add_convert_fusion), channel_id=1, source_target_pairs={{0,96},{16,112},{32,0},{48,16},{64,32},{80,48},{96,64},{112,80},{1... | collective-permute-start | bytes 786440 | tf_op jit(solution)/shard_map/ppermute | solution.py:349
  97.8 6.8 %copy-start.2 = (bf16[768,768]{1,0:T(8,128)(2,1)S(1)}, bf16[768,768]{1,0:T(8,128)(2,1)}, u32[]{:S(2)}) copy-start(bf16[768,768]{1,0:T(8,128)(2,1)} %wk_ref.3) | copy-start | bytes 3538948
  98.0 0.8 copy-start.5
  98.8 17.6 %all-to-all-start.3 = ((bf16[32,64,128]{2,1,0:T(8,128)(2,1)}), bf16[32,64,128]{2,1,0:T(8,128)(2,1)S(1)}, u32[]{:S(2)}, u32[]{:S(2)}) async-start(bf16[32,64,128]{2,1,0:T(8,128)(2,1)} %bitcast.14), calls=%async_computation.3 | async-start | bytes 1048576 | tf_op jit(solution)/shard_map/all_to_all | solution.py:354
  104.6 1.3 %copy-start.4 = (bf16[768,768]{1,0:T(8,128)(2,1)S(1)}, bf16[768,768]{1,0:T(8,128)(2,1)}, u32[]{:S(2)}) copy-start(bf16[768,768]{1,0:T(8,128)(2,1)} %wv_ref.3) | copy-start | bytes 3538948
  105.9 10.6 %copy-start.11 = (bf16[128,16]{0,1:T(8,128)(2,1)S(1)}, bf16[128,16]{0,1:T(8,128)(2,1)}, u32[]{:S(2)}) copy-start(bf16[128,16]{0,1:T(8,128)(2,1)} %param.14) | copy-start | bytes 12292
